TPU v7x, 32 devices: a whole 2x2x4 slice. The times are simulated.
32 devices in a mesh: fsdp: 4 (over z), ctx: 4 (over y, x), tp: 2 (over core).
Axes of the slice: x: 2, y: 2, z: 4, core: 2. Of those that a mesh axis runs over, the one named last changes fastest.
Arguments:
- inputs: bfloat16 [2, 4, 1024, 2048], P(None, 'fsdp', 'ctx'), may hold values from -6 to 6
- segment_ids: int32 [2, 4, 1024], P(None, 'fsdp'), may hold values from 0 to 2, never falling along the last dimension, each value on 1 to 512 neighbouring positions
- cotangent: bfloat16 [2, 4, 1024, 2048], P(None, 'fsdp', 'ctx'), may hold values from -6 to 6
- w_qkv: float32 [3, 2048, 2048], P(None, ('fsdp', 'ctx'), 'tp'), may hold values from -0.125 to 0.125
- w_out: float32 [2048, 2048], P('tp', ('fsdp', 'ctx')), may hold values from -1 to 1
- w_up: float32 [2048, 8192], P(('fsdp', 'ctx'), 'tp'), may hold values from -0.125 to 0.125
- w_down: float32 [8192, 2048], P('tp', ('fsdp', 'ctx')), may hold values from -0.0625 to 0.0625
- bias_qv: float32 [2, 2048], P(None, 'tp'), may hold values from -3 to 3
- bias_up: float32 [8192], P('tp'), may hold values from -3 to 3
- bias_res: float32 [2, 2048], replicated, may hold values from -3 to 3
- norm_gain: float32 [2, 2048], replicated, may hold values from 0.5 to 1.5
- norm_shift: float32 [2, 2048], replicated, may hold values from -3 to 3
- moment_qkv: float32 [3, 2048, 2048], P(None, ('fsdp', 'ctx'), 'tp'), may hold values from -28 to 28
- moment_out: float32 [2048, 2048], P('tp', ('fsdp', 'ctx')), may hold values from -28 to 28
- moment_up: float32 [2048, 8192], P(('fsdp', 'ctx'), 'tp'), may hold values from -28 to 28
- moment_down: float32 [8192, 2048], P('tp', ('fsdp', 'ctx')), may hold values from -28 to 28
- moment_bqv: float32 [2, 2048], P(None, 'tp'), may hold values from -256 to 256
- moment_bup: float32 [8192], P('tp'), may hold values from -256 to 256
- moment_bres: float32 [2, 2048], replicated, may hold values from -256 to 256
- moment_gain: float32 [2, 2048], replicated, may hold values from -256 to 256
- moment_shift: float32 [2, 2048], replicated, may hold values from -256 to 256
Outputs:
- layer_out: bfloat16 [2, 4, 1024, 2048], P(None, 'fsdp', 'ctx')
- input_grad: float32 [2, 4, 1024, 2048], P(None, 'fsdp', 'ctx')
- grad_qkv: float32 [3, 2048, 2048], P(None, ('fsdp', 'ctx'), 'tp')
- grad_out: float32 [2048, 2048], P('tp', ('fsdp', 'ctx'))
- grad_up: float32 [2048, 8192], P(('fsdp', 'ctx'), 'tp')
- grad_down: float32 [8192, 2048], P('tp', ('fsdp', 'ctx'))
- grad_bqv: float32 [2, 2048], P(None, 'tp')
- grad_bup: float32 [8192], P('tp')
- grad_bres: float32 [2, 2048], replicated
- grad_gain: float32 [2, 2048], replicated
- grad_shift: float32 [2, 2048], replicated
- state_qkv: float32 [3, 2048, 2048], P(None, ('fsdp', 'ctx'), 'tp')
- state_out: float32 [2048, 2048], P('tp', ('fsdp', 'ctx'))
- state_up: float32 [2048, 8192], P(('fsdp', 'ctx'), 'tp')
- state_down: float32 [8192, 2048], P('tp', ('fsdp', 'ctx'))
- state_bqv: float32 [2, 2048], P(None, 'tp')
- state_bup: float32 [8192], P('tp')
- state_bres: float32 [2, 2048], replicated
- state_gain: float32 [2, 2048], replicated
- state_shift: float32 [2, 2048], replicated
- master_qkv: float32 [3, 2048, 2048], P(None, ('fsdp', 'ctx'), 'tp')
- master_out: float32 [2048, 2048], P('tp', ('fsdp', 'ctx'))
- master_up: float32 [2048, 8192], P(('fsdp', 'ctx'), 'tp')
- master_down: float32 [8192, 2048], P('tp', ('fsdp', 'ctx'))
- master_bqv: float32 [2, 2048], P(None, 'tp')
- master_bup: float32 [8192], P('tp')
- master_bres: float32 [2, 2048], replicated
- master_gain: float32 [2, 2048], replicated
- master_shift: float32 [2, 2048], replicated
Inputs may be any that keep to these rules, and one draw needn't show every extreme that they name: `segment_ids`: segment numbers never fall along a sequence.
All inputs are finite; a program needn't handle non-finite values.
Results may differ from a plain program's by a relative error of at most 0.025.
Values may be sent and summed in bfloat16 or wider, within the bound.
A program may use at most 320 MiB of HBM per device.

v0:
```python
import math

import jax
import jax.numpy as jnp
from jax import lax
from jax.sharding import PartitionSpec as P

HDIM = 128
NS_STEPS = 5
HALF = 512


highest = lax.Precision.HIGHEST
norm_epsilon = 1e-05
ortho_epsilon = 1e-07
coef_first = 3.4445
coef_second = -4.775
coef_third = 2.0315
decay_rate = 0.5
matrix_rate = 0.25
masked_value = -1000000000.0


def from_behind(block, axis, distance):
    devices = range(lax.axis_size(axis))
    route = [(i - distance, i) for i in devices if i - distance in devices]
    return lax.ppermute(block, axis, route)


def for_sending(shard):

    def short(part):
        return part.astype(jnp.bfloat16) if part.dtype == jnp.float32 else part

    return jax.tree.map(short, shard)


def gelu_tanh(values):
    return jax.nn.gelu(values, approximate=True)


def layer_norm(values, gain_row, shift_row):
    center = values - jnp.mean(values, axis=-1, keepdims=True)
    inverse = lax.rsqrt(jnp.mean(center * center, axis=-1, keepdims=True) + norm_epsilon)
    normed = center * inverse
    return (normed * gain_row + shift_row, normed, inverse)


def layer_norm_back(grad_upper, normed, inverse, gain_row):
    grad_normed = grad_upper * gain_row
    mean_grad = jnp.mean(grad_normed, axis=-1, keepdims=True)
    mean_dot = jnp.mean(grad_normed * normed, axis=-1, keepdims=True)
    grad_in = inverse * (grad_normed - mean_grad - normed * mean_dot)
    return (grad_in, jnp.sum(grad_upper * normed, axis=0), jnp.sum(grad_upper, axis=0))


def fetch_edge(rows, distance_by):
    return from_behind(rows, "ctx", distance_by)


def return_edge(rows, distance_by):
    return from_behind(rows.astype(jnp.bfloat16), "ctx", distance_by).astype(rows.dtype)


def block_scores(query_heads, kv_ext, segment_row, seg_pad, offset, first_row, block_rows):
    query_seg = lax.dynamic_slice_in_dim(segment_row, offset + first_row, block_rows, 0)
    key_seg = lax.dynamic_slice_in_dim(seg_pad, offset + first_row, block_rows + 2 * HALF, 0)
    distance = jnp.arange(block_rows, dtype=jnp.int32)[:, None] - (
        jnp.arange(block_rows + 2 * HALF, dtype=jnp.int32)[None, :] - HALF
    )
    allowed = (query_seg[:, None] == key_seg[None, :]) & (jnp.abs(distance) <= HALF)
    raw_scores = jnp.einsum(
        "qhd,khd->hqk", query_heads, kv_ext[:, 0], preferred_element_type=jnp.float32
    ) * HDIM ** (-0.5)
    return (jnp.where(allowed[None], raw_scores, masked_value), query_heads, kv_ext)


def attend_forward(query_heads, kv_ext, segment_row, seg_pad, offset):
    seq_rows = query_heads.shape[0]
    block_rows = min(512, seq_rows)

    def one_block(block_index):
        first_row = block_index * block_rows
        scores, query_part, kv_part = block_scores(
            query_heads, kv_ext, segment_row, seg_pad, offset, first_row, block_rows
        )
        top_score = jnp.max(scores, axis=-1, keepdims=True)
        log_total = top_score + jnp.log(
            jnp.sum(jnp.exp(scores - top_score), axis=-1, keepdims=True)
        )
        probabilities = jnp.exp(scores - log_total).astype(jnp.bfloat16)
        context = jnp.einsum(
            "hqk,khd->qhd", probabilities, kv_part[:, 1], preferred_element_type=jnp.float32
        )
        return (context, log_total[..., 0])

    contexts, log_totals = lax.map(one_block, jnp.arange(seq_rows // block_rows, dtype=jnp.int32))
    return (contexts.reshape(seq_rows, -1), log_totals)


def attend_backward(query_heads, kv_ext, segment_row, seg_pad, offset, log_totals, grad_context):
    seq_rows = query_heads.shape[0]
    block_rows = min(512, seq_rows)

    def one_back(grad_ext, block_index):
        first_row = block_index * block_rows
        scores, query_part, kv_part = block_scores(
            query_heads, kv_ext, segment_row, seg_pad, offset, first_row, block_rows
        )
        probabilities = jnp.exp(scores - log_totals[block_index][..., None])
        grad_values = jnp.einsum(
            "hqk,qhd->khd",
            probabilities.astype(jnp.bfloat16),
            grad_context,
            preferred_element_type=jnp.float32,
        )
        grad_probs = jnp.einsum(
            "qhd,khd->hqk", grad_context, kv_part[:, 1], preferred_element_type=jnp.float32
        )
        inner_sum = jnp.sum(probabilities * grad_probs, axis=-1, keepdims=True)
        grad_scores = (probabilities * (grad_probs - inner_sum)).astype(jnp.bfloat16)
        grad_queries = jnp.einsum(
            "hqk,khd->qhd", grad_scores, kv_part[:, 0], preferred_element_type=jnp.float32
        ) * HDIM ** (-0.5)
        grad_keys = jnp.einsum(
            "hqk,qhd->khd", grad_scores, query_part, preferred_element_type=jnp.float32
        ) * HDIM ** (-0.5)
        update = jnp.stack([grad_keys, grad_values], axis=1)
        current = grad_ext
        grad_ext = current + update
        return (grad_ext, grad_queries)

    start_ext = jnp.zeros(kv_ext.shape, jnp.float32)
    grad_ext, grad_queries = lax.scan(
        one_back, start_ext, jnp.arange(seq_rows // block_rows, dtype=jnp.int32)
    )
    return (grad_ext, grad_queries.reshape(seq_rows, -1))


def micro_step(
    full_weights, row_low, segment_row, cot_row, bias_qv, bias_up, bias_res, norm_gain, norm_shift
):
    qkv_full, out_full, up_full, down_full = full_weights
    seq_rows = row_low.shape[0]
    local_width = qkv_full.shape[2]
    local_heads = local_width // HDIM
    row_values = row_low.astype(jnp.float32)
    offset = lax.axis_index("ctx") * seq_rows
    seg_pad = jnp.pad(segment_row, (HALF, HALF), constant_values=-1)
    reach_count = -(-HALF // seq_rows)
    projected = jnp.einsum("sd,cde->sce", row_low, qkv_full, preferred_element_type=jnp.float32)
    bias_three = jnp.stack([bias_qv[0], jnp.zeros_like(bias_qv[0]), bias_qv[1]])
    qkv_low = (projected + bias_three[None]).astype(jnp.bfloat16)
    query_heads = qkv_low[:, 0].reshape(seq_rows, local_heads, HDIM)
    kv_flat = qkv_low[:, 1:].reshape(seq_rows, 2 * local_width)
    left_list = []
    right_list = []
    for distance_index in range(1, reach_count + 1):
        edge_width = min(seq_rows, HALF - (distance_index - 1) * seq_rows)
        left_list.insert(0, fetch_edge(kv_flat, distance_index))
        right_list.append(fetch_edge(kv_flat, -distance_index))
    kv_ext = jnp.concatenate(left_list + [kv_flat] + right_list, axis=0)
    kv_ext = kv_ext.reshape(seq_rows + 2 * HALF, 2, local_heads, HDIM)
    context, log_totals = attend_forward(query_heads, kv_ext, segment_row, seg_pad, offset)
    context_low = context.astype(jnp.bfloat16)
    attn_part = jnp.dot(context_low, out_full, preferred_element_type=jnp.float32)
    attended = lax.psum(attn_part, "tp") + bias_res[0]
    first, first_unit, first_inverse = layer_norm(
        row_values + attended, norm_gain[0], norm_shift[0]
    )
    first_low = first.astype(jnp.bfloat16)
    pre_act = jnp.dot(first_low, up_full, preferred_element_type=jnp.float32) + bias_up
    activated, gelu_back = jax.vjp(gelu_tanh, pre_act)
    activated_low = activated.astype(jnp.bfloat16)
    ffn_part = jnp.dot(activated_low, down_full, preferred_element_type=jnp.float32)
    branch = lax.psum(ffn_part, "tp") + bias_res[1]
    out_rows, second_unit, second_inverse = layer_norm(first + branch, norm_gain[1], norm_shift[1])
    grad_upper = cot_row.astype(jnp.float32)
    grad_second, gain_second, shift_second = layer_norm_back(
        grad_upper, second_unit, second_inverse, norm_gain[1]
    )
    grad_branch = grad_second.astype(jnp.bfloat16)
    term_down = jnp.einsum(
        "sf,sd->fd", activated_low, grad_branch, preferred_element_type=jnp.float32
    )
    grad_act = jnp.einsum("sd,fd->sf", grad_branch, down_full, preferred_element_type=jnp.float32)
    grad_pre = gelu_back(grad_act)[0].astype(jnp.bfloat16)
    term_up = jnp.einsum("sd,sf->df", first_low, grad_pre, preferred_element_type=jnp.float32)
    grad_first_part = jnp.einsum("sf,df->sd", grad_pre, up_full, preferred_element_type=jnp.float32)
    grad_first_out = grad_second + lax.psum(grad_first_part, "tp")
    grad_first, gain_first, shift_first = layer_norm_back(
        grad_first_out, first_unit, first_inverse, norm_gain[0]
    )
    grad_attended = grad_first.astype(jnp.bfloat16)
    term_out = jnp.einsum(
        "se,sd->ed", context_low, grad_attended, preferred_element_type=jnp.float32
    )
    grad_context = jnp.einsum(
        "sd,ed->se", grad_attended, out_full, preferred_element_type=jnp.float32
    )
    grad_context = grad_context.astype(jnp.bfloat16).reshape(seq_rows, local_heads, HDIM)
    grad_ext, grad_queries = attend_backward(
        query_heads, kv_ext, segment_row, seg_pad, offset, log_totals, grad_context
    )
    grad_flat = grad_ext.reshape(seq_rows + 2 * HALF, 2 * local_width)
    own_rows = grad_flat[HALF : HALF + seq_rows]
    for distance_index in range(1, reach_count + 1):
        edge_width = min(seq_rows, HALF - (distance_index - 1) * seq_rows)
        left_start = HALF - (distance_index - 1) * seq_rows - edge_width
        right_start = HALF + seq_rows + (distance_index - 1) * seq_rows
        own_rows = own_rows.at[seq_rows - edge_width :].add(
            return_edge(grad_flat[left_start : left_start + edge_width], -distance_index)
        )
        own_rows = own_rows.at[:edge_width].add(
            return_edge(grad_flat[right_start : right_start + edge_width], distance_index)
        )
    grad_qkv_low = jnp.concatenate(
        [
            grad_queries.reshape(seq_rows, 1, local_width),
            own_rows.reshape(seq_rows, 2, local_width),
        ],
        axis=1,
    ).astype(jnp.bfloat16)
    term_qkv = jnp.einsum("sd,sce->cde", row_low, grad_qkv_low, preferred_element_type=jnp.float32)
    grad_in_part = jnp.einsum(
        "sce,cde->sd", grad_qkv_low, qkv_full, preferred_element_type=jnp.float32
    )
    input_rows = grad_first + lax.psum(grad_in_part.astype(jnp.bfloat16), "tp").astype(jnp.float32)
    qkv_sums = jnp.sum(grad_qkv_low.astype(jnp.float32), axis=0)
    vector_terms = (
        jnp.stack([qkv_sums[0], qkv_sums[2]]),
        jnp.sum(grad_pre.astype(jnp.float32), axis=0),
        jnp.stack(
            [
                jnp.sum(grad_attended.astype(jnp.float32), axis=0),
                jnp.sum(grad_branch.astype(jnp.float32), axis=0),
            ]
        ),
        jnp.stack([gain_first, gain_second]),
        jnp.stack([shift_first, shift_second]),
    )
    return (
        out_rows.astype(jnp.bfloat16),
        input_rows,
        (term_qkv, term_out, term_up, term_down),
        vector_terms,
    )


def orthogonalize(slabs):
    slab_norm = jnp.sqrt(jnp.sum(slabs * slabs, axis=(1, 2), keepdims=True))
    current = slabs / (slab_norm + ortho_epsilon)
    for sweep_index in range(NS_STEPS):
        gram_matrix = jnp.einsum("ndk,ndl->nkl", current, current, precision=highest)
        polynomial = coef_second * gram_matrix + coef_third * jnp.einsum(
            "nkl,nlm->nkm", gram_matrix, gram_matrix, precision=highest
        )
        current = coef_first * current + jnp.einsum(
            "ndk,nkl->ndl", current, polynomial, precision=highest
        )
    return current


def orthogonal_slabs(received):
    result = orthogonalize(received[0])[None]
    return lax.all_to_all(
        for_sending(result), ("fsdp", "ctx"), split_axis=2, concat_axis=0, tiled=True
    ).astype(result.dtype)


def body(
    inputs,
    segment_ids,
    cotangent,
    w_qkv,
    w_out,
    w_up,
    w_down,
    bias_qv,
    bias_up,
    bias_res,
    norm_gain,
    norm_shift,
    moment_qkv,
    moment_out,
    moment_up,
    moment_down,
    moment_bqv,
    moment_bup,
    moment_bres,
    moment_gain,
    moment_shift,
):
    micro_count = inputs.shape[0]
    model_width = inputs.shape[3]
    token_total = (
        micro_count
        * inputs.shape[1]
        * lax.axis_size("fsdp")
        * inputs.shape[2]
        * lax.axis_size("ctx")
    )
    qkv_low = w_qkv.astype(jnp.bfloat16)
    out_low = w_out.astype(jnp.bfloat16)
    up_low = w_up.astype(jnp.bfloat16)
    down_low = w_down.astype(jnp.bfloat16)
    out_list = []
    grad_list = []
    shard_sums = (
        jnp.zeros(w_qkv.shape, jnp.float32),
        jnp.zeros(w_out.shape, jnp.float32),
        jnp.zeros(w_up.shape, jnp.float32),
        jnp.zeros(w_down.shape, jnp.float32),
    )
    vector_sums = None
    for micro_index in range(micro_count):
        full_weights = (
            lax.all_gather(qkv_low, ("fsdp", "ctx"), axis=1, tiled=True),
            lax.all_gather(out_low, ("fsdp", "ctx"), axis=1, tiled=True),
            lax.all_gather(up_low, ("fsdp", "ctx"), axis=0, tiled=True),
            lax.all_gather(down_low, ("fsdp", "ctx"), axis=1, tiled=True),
        )
        out_rows, input_rows, grad_terms, vector_terms = micro_step(
            full_weights,
            inputs[micro_index, 0],
            segment_ids[micro_index, 0],
            cotangent[micro_index, 0],
            bias_qv,
            bias_up,
            bias_res,
            norm_gain,
            norm_shift,
        )
        out_list.append(out_rows)
        grad_list.append(input_rows)
        vector_sums = (
            vector_terms
            if vector_sums is None
            else jax.tree.map(jnp.add, vector_sums, vector_terms)
        )
        shards = (
            lax.psum_scatter(grad_terms[0], ("fsdp", "ctx"), scatter_dimension=1, tiled=True),
            lax.psum_scatter(grad_terms[1], ("fsdp", "ctx"), scatter_dimension=1, tiled=True),
            lax.psum_scatter(grad_terms[2], ("fsdp", "ctx"), scatter_dimension=0, tiled=True),
            lax.psum_scatter(grad_terms[3], ("fsdp", "ctx"), scatter_dimension=1, tiled=True),
        )
        shard_sums = jax.tree.map(jnp.add, shard_sums, shards)
    grad_qkv, grad_out, grad_up, grad_down = shard_sums
    grad_bqv, grad_bup, grad_bres, grad_gain, grad_shift = lax.psum(
        (vector_sums[0], vector_sums[1], vector_sums[2], vector_sums[3], vector_sums[4]),
        ("fsdp", "ctx"),
    )
    layer_out = jnp.stack(out_list)[:, None]
    input_grad = jnp.stack(grad_list)[:, None]
    state_qkv = decay_rate * moment_qkv + grad_qkv
    state_out = decay_rate * moment_out + grad_out
    state_up = decay_rate * moment_up + grad_up
    state_down = decay_rate * moment_down + grad_down
    shard_rows = state_qkv.shape[1]
    local_width = state_qkv.shape[2]
    local_heads = local_width // HDIM
    local_units = state_up.shape[1] // HDIM
    pieces = jnp.concatenate(
        [
            state_qkv.reshape(3, shard_rows, local_heads, HDIM)
            .transpose(0, 2, 1, 3)
            .reshape(3 * local_heads, shard_rows, HDIM),
            state_out.reshape(local_heads, HDIM, shard_rows).transpose(0, 2, 1),
            state_up.reshape(shard_rows, local_units, HDIM).transpose(1, 0, 2),
            state_down.reshape(local_units, HDIM, shard_rows).transpose(0, 2, 1),
        ],
        axis=0,
    )
    slab_count = pieces.shape[0]
    group_size = lax.axis_size(("fsdp", "ctx"))
    slot_count = -(-slab_count // group_size)
    padded = jnp.concatenate(
        [pieces, jnp.zeros((slot_count * group_size - slab_count, shard_rows, HDIM), jnp.float32)],
        axis=0,
    )
    outgoing = padded.reshape(slot_count, group_size, shard_rows, HDIM).transpose(1, 0, 2, 3)
    returned = orthogonal_slabs(
        lax.all_to_all(
            outgoing.astype(jnp.bfloat16), ("fsdp", "ctx"), split_axis=0, concat_axis=2, tiled=True
        ).astype(outgoing.dtype)
    )
    ortho = returned.transpose(1, 0, 2, 3).reshape(slot_count * group_size, shard_rows, HDIM)[
        :slab_count
    ]
    cut_out = 3 * local_heads
    cut_up = cut_out + local_heads
    cut_down = cut_up + local_units
    ortho_qkv = (
        ortho[:cut_out]
        .reshape(3, local_heads, shard_rows, HDIM)
        .transpose(0, 2, 1, 3)
        .reshape(3, shard_rows, local_width)
    )
    ortho_out = ortho[cut_out:cut_up].transpose(0, 2, 1).reshape(local_width, shard_rows)
    ortho_up = ortho[cut_up:cut_down].transpose(1, 0, 2).reshape(shard_rows, local_units * HDIM)
    ortho_down = ortho[cut_down:].transpose(0, 2, 1).reshape(local_units * HDIM, shard_rows)
    step_scale = matrix_rate * math.sqrt(model_width / HDIM)
    master_qkv = w_qkv - step_scale * ortho_qkv
    master_out = w_out - step_scale * ortho_out
    master_up = w_up - step_scale * ortho_up
    master_down = w_down - step_scale * ortho_down
    vector_step = 1.0 / math.sqrt(token_total)
    state_bqv = decay_rate * moment_bqv + grad_bqv
    state_bup = decay_rate * moment_bup + grad_bup
    state_bres = decay_rate * moment_bres + grad_bres
    state_gain = decay_rate * moment_gain + grad_gain
    state_shift = decay_rate * moment_shift + grad_shift
    master_bqv = bias_qv - vector_step * state_bqv
    master_bup = bias_up - vector_step * state_bup
    master_bres = bias_res - vector_step * state_bres
    master_gain = norm_gain - vector_step * state_gain
    master_shift = norm_shift - vector_step * state_shift
    return (
        layer_out,
        input_grad,
        grad_qkv,
        grad_out,
        grad_up,
        grad_down,
        grad_bqv,
        grad_bup,
        grad_bres,
        grad_gain,
        grad_shift,
        state_qkv,
        state_out,
        state_up,
        state_down,
        state_bqv,
        state_bup,
        state_bres,
        state_gain,
        state_shift,
        master_qkv,
        master_out,
        master_up,
        master_down,
        master_bqv,
        master_bup,
        master_bres,
        master_gain,
        master_shift,
    )


def solution(mesh):
    placed = (
        P(None, "fsdp", "ctx", None),
        P(None, "fsdp", None),
        P(None, "fsdp", "ctx", None),
        P(None, ("fsdp", "ctx"), "tp"),
        P("tp", ("fsdp", "ctx")),
        P(("fsdp", "ctx"), "tp"),
        P("tp", ("fsdp", "ctx")),
        P(None, "tp"),
        P("tp"),
        P(),
        P(),
        P(),
        P(None, ("fsdp", "ctx"), "tp"),
        P("tp", ("fsdp", "ctx")),
        P(("fsdp", "ctx"), "tp"),
        P("tp", ("fsdp", "ctx")),
        P(None, "tp"),
        P("tp"),
        P(),
        P(),
        P(),
    )
    return jax.shard_map(
        body,
        mesh=mesh,
        in_specs=placed,
        out_specs=(
            P(None, "fsdp", "ctx", None),
            P(None, "fsdp", "ctx", None),
            P(None, ("fsdp", "ctx"), "tp"),
            P("tp", ("fsdp", "ctx")),
            P(("fsdp", "ctx"), "tp"),
            P("tp", ("fsdp", "ctx")),
            P(None, "tp"),
            P("tp"),
            P(),
            P(),
            P(),
            P(None, ("fsdp", "ctx"), "tp"),
            P("tp", ("fsdp", "ctx")),
            P(("fsdp", "ctx"), "tp"),
            P("tp", ("fsdp", "ctx")),
            P(None, "tp"),
            P("tp"),
            P(),
            P(),
            P(),
            P(None, ("fsdp", "ctx"), "tp"),
            P("tp", ("fsdp", "ctx")),
            P(("fsdp", "ctx"), "tp"),
            P("tp", ("fsdp", "ctx")),
            P(None, "tp"),
            P("tp"),
            P(),
            P(),
            P(),
        ),
        check_vma=False,
    )
```

profile of v0, /device:TPU:0, one launch (start us, length us, event | category | flops | bytes accessed | tf_op | source)
XLA Modules:
  0.0 3421.8 jit_solution(14526225026345066333)
XLA Ops:
  11.9 154.1 %all-gather.5.cloned.1.call-done = bf16[3,2048,1024]{2,1,0:T(8,128)(2,1)} async-done(((bf16[3,128,1024]{2,1,0:T(8,128)(2,1)}), bf16[3,2048,1024]{2,1,0:T(8,128)(2,1)}) %all-gather.5.cloned.1.call-update) | async-done | bytes 12582928 | tf_op jit(solution)/shard_map/all_gather | solution.py:318
  166.0 8.0 add_convert_fusion.1
  189.2 8.2 add_convert_fusion.2
  208.6 25.6 collective-permute-done.4
  257.6 17.3 collective-permute-done
  279.4 25.8 collective-permute-done.2
  355.7 23.1 all-reduce.19.cloned.1.call-done
  384.4 190.8 %all-gather.9.cloned.1.call-done = bf16[2048,4096]{1,0:T(8,128)(2,1)} async-done(((bf16[128,4096]{1,0:T(8,128)(2,1)}), bf16[2048,4096]{1,0:T(8,128)(2,1)}) %all-gather.9.cloned.1.call-update) | async-done | bytes 16777232 | tf_op jit(solution)/shard_map/all_gather | solution.py:320
  575.2 13.2 convolution_add_fusion.2
  594.7 231.8 %all-gather.11.cloned.1.call-done = bf16[4096,2048]{1,0:T(8,128)(2,1)} async-done(((bf16[4096,128]{1,0:T(8,128)(2,1)}), bf16[4096,2048]{1,0:T(8,128)(2,1)}) %all-gather.11.cloned.1.call-update) | async-done | bytes 16777232 | tf_op jit(solution)/shard_map/all_gather | solution.py:321
  826.5 13.4 fusion.107
  846.2 26.9 all-reduce.17.cloned.1.call-done
  885.6 12.9 convert_reduce_fusion
  898.5 12.2 fusion.130
  910.8 13.4 convert_reduce_fusion.1
  924.2 12.2 fusion.129
  936.5 29.8 all-reduce.15.cloned.1.call-done
  983.9 8.1 multiply_reduce_fusion
  1030.1 7.3 convolution_bitcast_fusion.1
  1037.5 11.5 multiply_reduce_fusion.1
  1066.6 7.6 collective-permute-start.11
  1104.6 8.4 collective-permute-done.12
  1127.5 75.0 %collective-permute-done.8 = bf16[256,2048]{0,1:T(8,128)(2,1)} collective-permute-done((bf16[256,2048]{0,1:T(8,128)(2,1)}, bf16[256,2048]{0,1:T(8,128)(2,1)}, u32[]{:S(2)}, u32[]{:S(2)}) %collective-permute-start.8) | collective-permute-done | bytes 1048608 | tf_op jit(solution)/shard_map/ppermute | solution.py:27
  1214.0 10.3 fusion.70
  1224.3 17.0 add_bitcast_fusion
  1242.9 16.0 fusion.91
  1258.8 26.6 convolution_add_fusion
  1287.1 15.8 fusion.103
  1302.9 26.8 convolution_add_fusion.1
  1334.1 285.9 %reduce-scatter.5.cloned.1.call-done = f32[3,128,1024]{1,2,0:T(8,128)} async-done(((f32[3,2048,1024]{1,2,0:T(8,128)}), f32[3,128,1024]{1,2,0:T(8,128)}) %reduce-scatter.5.cloned.1.call-update) | async-done | bytes 1572880 | tf_op jit(solution)/shard_map/reduce_scatter | solution.py:342
  1624.6 680.8 %reduce-scatter.11.cloned.1.call-done = f32[4096,128]{1,0:T(8,128)} async-done(((f32[4096,2048]{1,0:T(8,128)}), f32[4096,128]{1,0:T(8,128)}) %reduce-scatter.11.cloned.1.call-update) | async-done | bytes 2097168 | tf_op jit(solution)/shard_map/reduce_scatter | solution.py:345
  2309.9 687.7 %reduce-scatter.9.cloned.1.call-done = f32[128,4096]{1,0:T(8,128)} async-done(((f32[2048,4096]{1,0:T(8,128)}), f32[128,4096]{1,0:T(8,128)}) %reduce-scatter.9.cloned.1.call-update) | async-done | bytes 2097168 | tf_op jit(solution)/shard_map/reduce_scatter | solution.py:344
  3004.4 11.9 all-to-all-start
  3022.9 53.7 %all-to-all-done = bf16[16,6,128,128]{3,2,1,0:T(8,128)(2,1)S(1)} async-done(((bf16[16,6,128,128]{3,2,1,0:T(8,128)(2,1)}), bf16[16,6,128,128]{3,2,1,0:T(8,128)(2,1)S(1)}, u32[]{:S(2)}, u32[]{:S(2)}) %all-to-all-start) | async-done | bytes 3145760 | tf_op jit(solution)/shard_map/all_to_all | solution.py:383
  3079.0 10.8 fusion.65
  3090.4 7.2 multiply_add_fusion.3
  3097.6 10.6 fusion.131
  3108.8 7.1 multiply_add_fusion.2
  3115.9 10.6 fusion.132
  3127.0 6.7 multiply_add_fusion.1
  3133.7 10.6 fusion.133
  3151.6 10.8 fusion.134
  3169.3 13.3 copy.309
  3182.5 14.8 all-to-all-start.1
  3198.3 9.1 fusion.33
  3207.5 9.0 fusion.32
  3222.6 125.5 %all-reduce.13.cloned.1.call-done = (f32[2,1024]{1,0:T(2,128)}, f32[4096]{0:T(1024)}, f32[2,2048]{1,0:T(2,128)}, f32[2,2048]{1,0:T(2,128)}, f32[2,2048]{1,0:T(2,128)}) async-done(((f32[2,1024]{1,0:T(2,128)}, f32[4096]{0:T(1024)}, f32[2,2048]{1,0:T(2,128)}, f32[2,2048]{1,0:T(2,128)}, f32[2,2048]{1,0:T(2,128)}), (f32[2,1024]{1,0:T(2,128)}, f32[4096]{0:T(1024)}, f32[2,2048]{1,0:T(2,128)}, f32[2,2048]{1,0:T(2,128)}, ...) | async-done | bytes 73744 | tf_op jit(solution)/shard_map/psum | solution.py:349
  3354.8 17.6 all-reduce.21.cloned.1.call-done
  (477 shorter events, 373.0 us)
Async XLA Ops:
  7.2 158.8 %copy-start.35 = (bf16[2,1,256,2048]{3,2,1,0:T(8,128)(2,1)S(1)}, bf16[2,1,256,2048]{3,2,1,0:T(8,128)(2,1)}, u32[]{:S(2)}) copy-start(bf16[2,1,256,2048]{3,2,1,0:T(8,128)(2,1)} %param.53) | copy-start | bytes 6291460
  7.2 158.8 %all-gather.5.cloned.1.call-start = ((), (), s32[]{:S(2)}) async-start(), calls=%async_computation.6 | async-start | bytes 13369344 | tf_op jit(solution)/shard_map/all_gather | solution.py:318
  9.8 334.0 %all-gather.7.cloned.1.call-start = ((), (), s32[]{:S(2)}) async-start(), calls=%async_computation.7 | async-start | bytes 4456448 | tf_op jit(solution)/shard_map/all_gather | solution.py:319
  11.7 367.1 %all-reduce.19.cloned.1.call-start = ((), (), s32[]{:S(2)}) async-start(), calls=%async_computation.17 | async-start | bytes 8388608 | tf_op jit(solution)/shard_map/psum | solution.py:167
  178.8 55.4 %collective-permute-start.4 = (bf16[256,2048]{0,1:T(8,128)(2,1)}, bf16[256,2048]{0,1:T(8,128)(2,1)}, u32[]{:S(2)}, u32[]{:S(2)}) collective-permute-start(bf16[256,2048]{0,1:T(8,128)(2,1)} %bitcast.372), channel_id=1, source_target_pairs={{0,4},{2,6},{1,5},{3,7},{8,12},{10,14},{9,13},{11,15},{16,20},{18,... | collective-permute-start | bytes 3145736 | tf_op jit(solution)/shard_map/ppermute | solution.py:27
  183.2 53.3 %collective-permute-start.5 = (bf16[256,2048]{0,1:T(8,128)(2,1)}, bf16[256,2048]{0,1:T(8,128)(2,1)}, u32[]{:S(2)}, u32[]{:S(2)}) collective-permute-start(bf16[256,2048]{0,1:T(8,128)(2,1)} %bitcast.373), channel_id=1, source_target_pairs={{0,2},{2,4},{4,6},{1,3},{3,5},{5,7},{8,10},{10,12},{12,14},{9,11},... | collective-permute-start | bytes 3145736 | tf_op jit(solution)/shard_map/ppermute | solution.py:27
  186.6 51.2 %collective-permute-start.6 = (bf16[256,2048]{0,1:T(8,128)(2,1)}, bf16[256,2048]{0,1:T(8,128)(2,1)}, u32[]{:S(2)}, u32[]{:S(2)}) collective-permute-start(bf16[256,2048]{0,1:T(8,128)(2,1)} %bitcast.374), channel_id=1, source_target_pairs={{2,0},{4,2},{6,4},{3,1},{5,3},{7,5},{10,8},{12,10},{14,12},{11,9},... | collective-permute-start | bytes 3145736 | tf_op jit(solution)/shard_map/ppermute | solution.py:27
  187.9 67.4 %collective-permute-start.7 = (bf16[256,2048]{0,1:T(8,128)(2,1)}, bf16[256,2048]{0,1:T(8,128)(2,1)}, u32[]{:S(2)}, u32[]{:S(2)}) collective-permute-start(bf16[256,2048]{0,1:T(8,128)(2,1)} %bitcast.375), channel_id=1, source_target_pairs={{4,0},{6,2},{5,1},{7,3},{12,8},{14,10},{13,9},{15,11},{20,16},{22,... | collective-permute-start | bytes 3145736 | tf_op jit(solution)/shard_map/ppermute | solution.py:27
  202.2 72.7 %collective-permute-start = (bf16[256,2048]{0,1:T(8,128)(2,1)}, bf16[256,2048]{0,1:T(8,128)(2,1)}, u32[]{:S(2)}, u32[]{:S(2)}) collective-permute-start(bf16[256,2048]{0,1:T(8,128)(2,1)} %bitcast.376), channel_id=1, source_target_pairs={{0,4},{2,6},{1,5},{3,7},{8,12},{10,14},{9,13},{11,15},{16,20},{18,... | collective-permute-start | bytes 3145736 | tf_op jit(solution)/shard_map/ppermute | solution.py:27
  234.2 43.0 %collective-permute-start.1 = (bf16[256,2048]{0,1:T(8,128)(2,1)}, bf16[256,2048]{0,1:T(8,128)(2,1)}, u32[]{:S(2)}, u32[]{:S(2)}) collective-permute-start(bf16[256,2048]{0,1:T(8,128)(2,1)} %bitcast.377), channel_id=1, source_target_pairs={{0,2},{2,4},{4,6},{1,3},{3,5},{5,7},{8,10},{10,12},{12,14},{9,11},... | collective-permute-start | bytes 3145736 | tf_op jit(solution)/shard_map/ppermute | solution.py:27
  236.5 68.7 %collective-permute-start.2 = (bf16[256,2048]{0,1:T(8,128)(2,1)}, bf16[256,2048]{0,1:T(8,128)(2,1)}, u32[]{:S(2)}, u32[]{:S(2)}) collective-permute-start(bf16[256,2048]{0,1:T(8,128)(2,1)} %bitcast.378), channel_id=1, source_target_pairs={{2,0},{4,2},{6,4},{3,1},{5,3},{7,5},{10,8},{12,10},{14,12},{11,9},... | collective-permute-start | bytes 3145736 | tf_op jit(solution)/shard_map/ppermute | solution.py:27
  237.8 69.7 %collective-permute-start.3 = (bf16[256,2048]{0,1:T(8,128)(2,1)}, bf16[256,2048]{0,1:T(8,128)(2,1)}, u32[]{:S(2)}, u32[]{:S(2)}) collective-permute-start(bf16[256,2048]{0,1:T(8,128)(2,1)} %bitcast.379), channel_id=1, source_target_pairs={{4,0},{6,2},{5,1},{7,3},{12,8},{14,10},{13,9},{15,11},{20,16},{22,... | collective-permute-start | bytes 3145736 | tf_op jit(solution)/shard_map/ppermute | solution.py:27
  351.6 223.6 %all-gather.9.cloned.1.call-start = ((), (), s32[]{:S(2)}) async-start(), calls=%async_computation.8 | async-start | bytes 17825792 | tf_op jit(solution)/shard_map/all_gather | solution.py:320
  352.8 473.7 %all-gather.11.cloned.1.call-start = ((), (), s32[]{:S(2)}) async-start(), calls=%async_computation.9 | async-start | bytes 17825792 | tf_op jit(solution)/shard_map/all_gather | solution.py:321
  355.5 517.5 %all-reduce.17.cloned.1.call-start = ((), (), s32[]{:S(2)}) async-start(), calls=%async_computation.16 | async-start | bytes 8388608 | tf_op jit(solution)/shard_map/psum | solution.py:176
  355.6 517.4 %copy-start.68 = (f32[1,2048]{1,0:T(1,128)}, f32[1,2048]{1,0:T(1,128)S(1)}, u32[]{:S(2)}) copy-start(f32[1,2048]{1,0:T(1,128)S(1)} %get-tuple-element.539) | copy-start | bytes 24580
  355.7 618.5 %copy-start.65 = (f32[1,2048]{1,0:T(1,128)}, f32[1,2048]{1,0:T(1,128)S(1)}, u32[]{:S(2)}) copy-start(f32[1,2048]{1,0:T(1,128)S(1)} %get-tuple-element.537) | copy-start | bytes 24580
  382.3 588.0 %copy-start.2 = (f32[256,2048]{1,0:T(8,128)}, f32[256,2048]{1,0:T(8,128)S(1)}, u32[]{:S(2)}) copy-start(f32[256,2048]{1,0:T(8,128)S(1)} %get-tuple-element.506) | copy-start | bytes 6291460
  382.3 192.9 %copy-start.103 = (f32[4096]{0:T(1024)S(1)}, f32[4096]{0:T(1024)}, u32[]{:S(2)}) copy-start(f32[4096]{0:T(1024)} %param.61) | copy-start | bytes 49156
  382.3 591.8 %copy-start.84 = (f32[256]{0:T(256)}, f32[256]{0:T(256)S(1)}, u32[]{:S(2)}) copy-start(f32[256]{0:T(256)S(1)} %broadcast_multiply_fusion.9) | copy-start | bytes 3076
  383.9 586.3 %copy-start.72 = (f32[256]{0:T(256)}, f32[256]{0:T(256)S(1)}, u32[]{:S(2)}) copy-start(f32[256]{0:T(256)S(1)} %broadcast_multiply_fusion.11) | copy-start | bytes 3076
  384.3 589.8 %copy-start.88 = (f32[256]{0:T(256)}, f32[256]{0:T(256)S(1)}, u32[]{:S(2)}) copy-start(f32[256]{0:T(256)S(1)} %add_rsqrt_fusion.1) | copy-start | bytes 3076
  384.3 585.9 %copy-start.86 = (f32[256]{0:T(256)}, f32[256]{0:T(256)S(1)}, u32[]{:S(2)}) copy-start(f32[256]{0:T(256)S(1)} %add_rsqrt_fusion.3) | copy-start | bytes 3076
  846.1 120.2 %all-reduce.15.cloned.1.call-start = ((), (), s32[]{:S(2)}) async-start(), calls=%async_computation.15 | async-start | bytes 8388608 | tf_op jit(solution)/shard_map/psum | solution.py:190
  936.5 395.4 %reduce-scatter.7.cloned.1.call-start = ((), (), s32[]{:S(2)}) async-start(), calls=%async_computation.11 | async-start | bytes 8912896 | tf_op jit(solution)/shard_map/reduce_scatter | solution.py:343
  980.1 640.0 %reduce-scatter.5.cloned.1.call-start = ((), (), s32[]{:S(2)}) async-start(), calls=%async_computation.10 | async-start | bytes 26738688 | tf_op jit(solution)/shard_map/reduce_scatter | solution.py:342
  1009.2 67.5 %collective-permute-start.15 = (bf16[256,2048]{0,1:T(8,128)(2,1)}, bf16[256,2048]{0,1:T(8,128)(2,1)S(1)}, u32[]{:S(2)}, u32[]{:S(2)}) collective-permute-start(bf16[256,2048]{0,1:T(8,128)(2,1)} %bitcast.68), channel_id=1, source_target_pairs={{0,4},{2,6},{1,5},{3,7},{8,12},{10,14},{9,13},{11,15},{16,20},{18,... | collective-permute-start | bytes 3145736 | tf_op jit(solution)/shard_map/ppermute | solution.py:27
  1012.9 65.1 %collective-permute-start.14 = (bf16[256,2048]{0,1:T(8,128)(2,1)}, bf16[256,2048]{0,1:T(8,128)(2,1)}, u32[]{:S(2)}, u32[]{:S(2)}) collective-permute-start(bf16[256,2048]{0,1:T(8,128)(2,1)} %bitcast.66), channel_id=1, source_target_pairs={{4,0},{6,2},{5,1},{7,3},{12,8},{14,10},{13,9},{15,11},{20,16},{22,... | collective-permute-start | bytes 3145736 | tf_op jit(solution)/shard_map/ppermute | solution.py:27
  1014.2 66.1 %collective-permute-start.13 = (bf16[256,2048]{0,1:T(8,128)(2,1)}, bf16[256,2048]{0,1:T(8,128)(2,1)}, u32[]{:S(2)}, u32[]{:S(2)}) collective-permute-start(bf16[256,2048]{0,1:T(8,128)(2,1)} %bitcast.64), channel_id=1, source_target_pairs={{0,2},{2,4},{4,6},{1,3},{3,5},{5,7},{8,10},{10,12},{12,14},{9,11},... | collective-permute-start | bytes 3145736 | tf_op jit(solution)/shard_map/ppermute | solution.py:27
  1023.1 89.8 %collective-permute-start.12 = (bf16[256,2048]{0,1:T(8,128)(2,1)}, bf16[256,2048]{0,1:T(8,128)(2,1)}, u32[]{:S(2)}, u32[]{:S(2)}) collective-permute-start(bf16[256,2048]{0,1:T(8,128)(2,1)} %bitcast.380), channel_id=1, source_target_pairs={{2,0},{4,2},{6,4},{3,1},{5,3},{7,5},{10,8},{12,10},{14,12},{11,9},... | collective-permute-start | bytes 3145736 | tf_op jit(solution)/shard_map/ppermute | solution.py:27
  1066.6 49.0 %collective-permute-start.11 = (bf16[256,2048]{0,1:T(8,128)(2,1)}, bf16[256,2048]{0,1:T(8,128)(2,1)}, u32[]{:S(2)}, u32[]{:S(2)}) collective-permute-start(bf16[256,2048]{0,1:T(8,128)(2,1)} %bitcast.50), channel_id=1, source_target_pairs={{0,4},{2,6},{1,5},{3,7},{8,12},{10,14},{9,13},{11,15},{16,20},{18,... | collective-permute-start | bytes 3145736 | tf_op jit(solution)/shard_map/ppermute | solution.py:27
  1076.7 41.4 %collective-permute-start.10 = (bf16[256,2048]{0,1:T(8,128)(2,1)}, bf16[256,2048]{0,1:T(8,128)(2,1)}, u32[]{:S(2)}, u32[]{:S(2)}) collective-permute-start(bf16[256,2048]{0,1:T(8,128)(2,1)} %bitcast.48), channel_id=1, source_target_pairs={{4,0},{6,2},{5,1},{7,3},{12,8},{14,10},{13,9},{15,11},{20,16},{22,... | collective-permute-start | bytes 3145736 | tf_op jit(solution)/shard_map/ppermute | solution.py:27
  1078.0 46.9 %collective-permute-start.9 = (bf16[256,2048]{0,1:T(8,128)(2,1)}, bf16[256,2048]{0,1:T(8,128)(2,1)}, u32[]{:S(2)}, u32[]{:S(2)}) collective-permute-start(bf16[256,2048]{0,1:T(8,128)(2,1)} %bitcast.46), channel_id=1, source_target_pairs={{0,2},{2,4},{4,6},{1,3},{3,5},{5,7},{8,10},{10,12},{12,14},{9,11},... | collective-permute-start | bytes 3145736 | tf_op jit(solution)/shard_map/ppermute | solution.py:27
  1080.3 122.1 %collective-permute-start.8 = (bf16[256,2048]{0,1:T(8,128)(2,1)}, bf16[256,2048]{0,1:T(8,128)(2,1)}, u32[]{:S(2)}, u32[]{:S(2)}) collective-permute-start(bf16[256,2048]{0,1:T(8,128)(2,1)} %bitcast.44), channel_id=1, source_target_pairs={{2,0},{4,2},{6,4},{3,1},{5,3},{7,5},{10,8},{12,10},{14,12},{11,9},... | collective-permute-start | bytes 3145736 | tf_op jit(solution)/shard_map/ppermute | solution.py:27
  1241.3 1064.1 %reduce-scatter.11.cloned.1.call-start = ((), (), s32[]{:S(2)}) async-start(), calls=%async_computation.13 | async-start | bytes 35651584 | tf_op jit(solution)/shard_map/reduce_scatter | solution.py:345
  1285.6 1712.0 %reduce-scatter.9.cloned.1.call-start = ((), (), s32[]{:S(2)}) async-start(), calls=%async_computation.12 | async-start | bytes 35651584 | tf_op jit(solution)/shard_map/reduce_scatter | solution.py:344
  3004.4 72.2 %all-to-all-start = ((bf16[16,6,128,128]{3,2,1,0:T(8,128)(2,1)}), bf16[16,6,128,128]{3,2,1,0:T(8,128)(2,1)S(1)}, u32[]{:S(2)}, u32[]{:S(2)}) async-start(bf16[16,6,128,128]{3,2,1,0:T(8,128)(2,1)} %copy.302), calls=%async_computation | async-start | bytes 6291456 | tf_op jit(solution)/shard_map/all_to_all | solution.py:383
  3182.5 198.1 %all-to-all-start.1 = ((bf16[1,6,2048,128]{3,1,0,2:T(8,128)(2,1)}), bf16[1,6,2048,128]{3,1,0,2:T(8,128)(2,1)}, u32[]{:S(2)}, u32[]{:S(2)}) async-start(bf16[1,6,2048,128]{3,1,0,2:T(8,128)(2,1)} %copy.309), calls=%async_computation.1 | async-start | bytes 8388608 | tf_op jit(solution)/shard_map/all_to_all | solution.py:266
  3197.3 150.7 %all-reduce.13.cloned.1.call-start = ((), (), s32[]{:S(2)}) async-start(), calls=%async_computation.14 | async-start | bytes 147456 | tf_op jit(solution)/shard_map/psum | solution.py:349
  3198.1 174.4 %all-reduce.21.cloned.1.call-start = ((), (), s32[]{:S(2)}) async-start(), calls=%async_computation.18 | async-start | bytes 4194304 | tf_op jit(solution)/shard_map/psum | solution.py:228
  3216.5 132.9 %copy-start.104 = (f32[4096]{0:T(1024)S(1)}, f32[4096]{0:T(1024)}, u32[]{:S(2)}) copy-start(f32[4096]{0:T(1024)} %param.61) | copy-start | bytes 49156
  3216.5 134.2 %copy-start.75 = (f32[2,2048]{1,0:T(2,128)S(1)}, f32[2,2048]{1,0:T(2,128)}, u32[]{:S(2)}) copy-start(f32[2,2048]{1,0:T(2,128)} %param.62) | copy-start | bytes 49156
  3216.5 134.2 %copy-start.106 = (f32[2,2048]{1,0:T(2,128)S(1)}, f32[2,2048]{1,0:T(2,128)}, u32[]{:S(2)}) copy-start(f32[2,2048]{1,0:T(2,128)} %param.71) | copy-start | bytes 49156
  3216.6 135.5 %copy-start.77 = (f32[2,2048]{1,0:T(2,128)S(1)}, f32[2,2048]{1,0:T(2,128)}, u32[]{:S(2)}) copy-start(f32[2,2048]{1,0:T(2,128)} %param.63) | copy-start | bytes 49156
  3216.6 135.5 %copy-start.107 = (f32[2,2048]{1,0:T(2,128)S(1)}, f32[2,2048]{1,0:T(2,128)}, u32[]{:S(2)}) copy-start(f32[2,2048]{1,0:T(2,128)} %param.72) | copy-start | bytes 49156
  3216.6 136.8 %copy-start.79 = (f32[2,2048]{1,0:T(2,128)S(1)}, f32[2,2048]{1,0:T(2,128)}, u32[]{:S(2)}) copy-start(f32[2,2048]{1,0:T(2,128)} %param.64) | copy-start | bytes 49156
  3216.6 136.8 %copy-start.108 = (f32[2,2048]{1,0:T(2,128)S(1)}, f32[2,2048]{1,0:T(2,128)}, u32[]{:S(2)}) copy-start(f32[2,2048]{1,0:T(2,128)} %param.73) | copy-start | bytes 49156
  3219.7 154.9 %copy-start.12 = (f32[256,2048]{1,0:T(8,128)S(1)}, f32[256,2048]{1,0:T(8,128)}, u32[]{:S(2)}) copy-start(f32[256,2048]{1,0:T(8,128)} %copy-done.10) | copy-start | bytes 6291460
  (105 other events, 1351.6 us)
Sparse Core Ops, SparseCore 0:
  11.4 154.5 all-gather.4
  169.3 131.6 all-gather.6
  351.7 27.0 all-reduce.18
  382.3 192.7 all-gather.8
  578.6 247.8 all-gather.10
  846.3 26.7 all-reduce.16
  936.6 29.6 all-reduce.14
  980.2 268.7 reduce-scatter.6
  1255.6 364.3 reduce-scatter.4
  1622.9 682.4 reduce-scatter.10
  2308.5 689.0 reduce-scatter.8
  3207.0 140.9 all-reduce.12
  3351.1 21.2 all-reduce.20
where the time goes:
time: 3430 us; the launch traced here: 3420 us
  waiting for transfers between devices  2670 us (78%)
  matrix products  410 us (12%)
  local copies, waits for them, and re-layouts  146 us (4%)
  other arithmetic  111 us (3%)
  starting transfers between devices  72.9 us (2%)
    reduce_scatter x1, waiting for transfers between devices, body(): lax.psum_scatter(grad_terms[2], ('fsdp', 'ctx'), scatter_dimension=0, til...  688 us
    reduce_scatter x1, waiting for transfers between devices, body(): lax.psum_scatter(grad_terms[3], ('fsdp', 'ctx'), scatter_dimension=1, til...  681 us
    reduce_scatter x1, waiting for transfers between devices, body(): lax.psum_scatter(grad_terms[0], ('fsdp', 'ctx'), scatter_dimension=1, til...  286 us
    all_gather x1, waiting for transfers between devices, body(): lax.all_gather(down_low, ('fsdp', 'ctx'), axis=1, tiled=True)  232 us
    all_gather x1, waiting for transfers between devices, body(): lax.all_gather(up_low, ('fsdp', 'ctx'), axis=0, tiled=True)  191 us
    ppermute x16, waiting for transfers between devices, from_behind(): return lax.ppermute(block, axis, route)  159 us
    all_gather x1, waiting for transfers between devices, body(): lax.all_gather(qkv_low, ('fsdp', 'ctx'), axis=1, tiled=True)  154 us
    psum x1, waiting for transfers between devices, body(): lax.psum((vector_sums[0], vector_sums[1], vector_sums[2], vector_sums[3],...  125 us
  transfers between devices with their start and end apart: 31, of which 19 were waited for; matrix products, arithmetic and copies ran while one was open for 11% of the time, Pallas kernels for 0%

commit v1 on v0

v1 whole, which is shorter than its diff:
```python
import math

import jax
import jax.numpy as jnp
from jax import lax
from jax.experimental import pallas as pl
from jax.experimental.pallas import tpu as pltpu
from jax.sharding import PartitionSpec as P

HDIM = 128
NS_STEPS = 5
HALF = 512

bf16 = jnp.bfloat16
f32 = jnp.float32
highest = lax.Precision.HIGHEST
norm_epsilon = 1e-05
ortho_epsilon = 1e-07
coef_first = 3.4445
coef_second = -4.775
coef_third = 2.0315
decay_rate = 0.5
matrix_rate = 0.25
masked_value = -1e30

CORE = [(0, 1), (1, 0)]


def xor_pairs(size, mask):
    return [(i, i ^ mask) for i in range(size)]


def swap_core(value):
    return lax.ppermute(value, "tp", CORE)


def swap_ctx(value, mask):
    return lax.ppermute(value, "ctx", xor_pairs(4, mask))


def swap_fsdp(value, mask):
    return lax.ppermute(value, "fsdp", xor_pairs(4, mask))


def mm(left, right, dims):
    return lax.dot_general(left, right, ((dims[:1], dims[1:]), ((), ())), preferred_element_type=f32)


def spread(own):
    if lax.axis_size("ctx") != 4:
        whole = lax.all_gather(own, "ctx", axis=0, tiled=False)
        return [whole[i] for i in range(whole.shape[0])]
    half = own.shape[0] // 2
    from_x = swap_ctx(own, 1)
    from_y = swap_ctx(own, 2)
    top = swap_ctx(from_x[:half], 2)
    low = swap_ctx(from_y[half:], 1)
    return [own, from_x, from_y, jnp.concatenate([top, low], axis=0)]


def collect(partial):
    count = lax.axis_size("ctx")
    rows = partial.shape[0] // count
    if count != 4:
        return lax.psum_scatter(partial, "ctx", scatter_dimension=0, tiled=True).astype(f32)
    half = rows // 2
    part = [partial[k * rows : (k + 1) * rows] for k in range(4)]
    over_x = swap_ctx(jnp.concatenate([part[1][:half], part[3][:half]], axis=0), 1).astype(f32)
    over_y = swap_ctx(jnp.concatenate([part[2][half:], part[3][half:]], axis=0), 2).astype(f32)
    then_y = swap_ctx((part[2][:half].astype(f32) + over_x[half:]).astype(bf16), 2)
    then_x = swap_ctx((part[1][half:].astype(f32) + over_y[half:]).astype(bf16), 1)
    own = part[0].astype(f32)
    return jnp.concatenate(
        [
            own[:half] + over_x[:half] + then_y.astype(f32),
            own[half:] + over_y[:half] + then_x.astype(f32),
        ],
        axis=0,
    )


def layer_norm(values, gain_row, shift_row):
    center = values - jnp.mean(values, axis=-1, keepdims=True)
    inverse = lax.rsqrt(jnp.mean(center * center, axis=-1, keepdims=True) + norm_epsilon)
    normed = center * inverse
    return (normed * gain_row + shift_row, normed, inverse)


def layer_norm_back(grad_upper, normed, inverse, gain_row):
    grad_normed = grad_upper * gain_row
    mean_grad = jnp.mean(grad_normed, axis=-1, keepdims=True)
    mean_dot = jnp.mean(grad_normed * normed, axis=-1, keepdims=True)
    grad_in = inverse * (grad_normed - mean_grad - normed * mean_dot)
    return (grad_in, jnp.sum(grad_upper * normed, axis=0), jnp.sum(grad_upper, axis=0))


def gelu_tanh(values):
    return jax.nn.gelu(values, approximate=True)


def block_weights(query, keys, place_rows, place_cols):
    scores = mm(query, keys, (1, 1))
    scores = jnp.where(jnp.abs(place_rows - place_cols) <= HALF, scores, masked_value)
    top = jnp.max(scores, axis=-1, keepdims=True)
    weights = jnp.exp((scores - top) * HDIM**-0.5)
    return weights, 1.0 / jnp.sum(weights, axis=-1, keepdims=True)


def attend_kernel(block, q_ref, k_ref, v_ref, rows_ref, cols_ref, out_ref):
    for start in range(0, q_ref.shape[0], block):
        span = pl.ds(start, block)
        weights, inverse = block_weights(q_ref[span, :], k_ref[...], rows_ref[span, :], cols_ref[...])
        out_ref[span, :] = (mm(weights.astype(bf16), v_ref[...], (1, 0)) * inverse).astype(bf16)


def attend_forward(qkv, place):
    length = qkv.shape[0]
    heads = qkv.shape[1] // (3 * HDIM)
    piece = lambda which: pl.BlockSpec((length, HDIM), lambda h, w=which: (0, w * heads + h))
    return pl.pallas_call(
        lambda *refs: attend_kernel(256, *refs),
        out_shape=jax.ShapeDtypeStruct((length, heads * HDIM), bf16),
        grid=(heads,),
        in_specs=[
            piece(0),
            piece(1),
            piece(2),
            pl.BlockSpec((length, 1), lambda h: (0, 0)),
            pl.BlockSpec((1, length), lambda h: (0, 0)),
        ],
        out_specs=pl.BlockSpec((length, HDIM), lambda h: (0, h)),
        compiler_params=pltpu.CompilerParams(vmem_limit_bytes=40 << 20),
        cost_estimate=pl.CostEstimate(
            flops=4 * heads * length * length * HDIM,
            bytes_accessed=8 * heads * length * HDIM,
            transcendentals=heads * length * length,
        ),
        name="attend_forward",
    )(qkv, qkv, qkv, place[:, None], place[None, :])


def attend_back_kernel(
    block, q_ref, k_ref, v_ref, up_ref, rows_ref, cols_ref, gq_ref, gk_ref, gv_ref, sum_k, sum_v
):
    scale = HDIM**-0.5
    for start in range(0, q_ref.shape[0], block):
        span = pl.ds(start, block)
        query = q_ref[span, :]
        upper = up_ref[span, :]
        weights, inverse = block_weights(query, k_ref[...], rows_ref[span, :], cols_ref[...])
        probs = weights * inverse
        grad_probs = mm(upper, v_ref[...], (1, 1))
        inner = jnp.sum(probs * grad_probs, axis=-1, keepdims=True)
        grad_scores = (probs * (grad_probs - inner)).astype(bf16)
        gq_ref[span, :] = (mm(grad_scores, k_ref[...], (1, 0)) * scale).astype(bf16)
        add_k = mm(grad_scores, query, (0, 0))
        add_v = mm(probs.astype(bf16), upper, (0, 0))
        if start == 0:
            sum_k[...] = add_k
            sum_v[...] = add_v
        else:
            sum_k[...] += add_k
            sum_v[...] += add_v
    gk_ref[...] = (sum_k[...] * scale).astype(bf16)
    gv_ref[...] = sum_v[...].astype(bf16)


def attend_backward(qkv, upper, place):
    length = qkv.shape[0]
    heads = qkv.shape[1] // (3 * HDIM)
    piece = lambda which: pl.BlockSpec((length, HDIM), lambda h, w=which: (0, w * heads + h))
    one = jax.ShapeDtypeStruct((length, heads * HDIM), bf16)
    outs = pl.pallas_call(
        lambda *refs: attend_back_kernel(256, *refs),
        out_shape=(one, one, one),
        grid=(heads,),
        in_specs=[
            piece(0),
            piece(1),
            piece(2),
            piece(0),
            pl.BlockSpec((length, 1), lambda h: (0, 0)),
            pl.BlockSpec((1, length), lambda h: (0, 0)),
        ],
        out_specs=(piece(0), piece(0), piece(0)),
        scratch_shapes=[pltpu.VMEM((length, HDIM), f32), pltpu.VMEM((length, HDIM), f32)],
        compiler_params=pltpu.CompilerParams(vmem_limit_bytes=48 << 20),
        cost_estimate=pl.CostEstimate(
            flops=10 * heads * length * length * HDIM,
            bytes_accessed=14 * heads * length * HDIM,
            transcendentals=heads * length * length,
        ),
        name="attend_backward",
    )(qkv, qkv, qkv, upper, place[:, None], place[None, :])
    return jnp.concatenate(outs, axis=1)


def polynomial_kernel(gram_ref, out_ref):
    count, width, _ = gram_ref.shape
    same = lax.broadcasted_iota(jnp.int32, (width, width), 0) == lax.broadcasted_iota(
        jnp.int32, (width, width), 1
    )
    unit = same.astype(f32)
    dot = lambda a, b: jnp.dot(a, b, precision=highest, preferred_element_type=f32)
    grams, totals = [], []
    for n in range(count):
        gram = gram_ref[n]
        square = jnp.sum(jnp.sum(gram * unit, axis=1, keepdims=True), axis=0, keepdims=True)
        inverse = 1.0 / (jnp.sqrt(square) + ortho_epsilon)
        grams.append(gram * (inverse * inverse))
        totals.append(unit * inverse)
    for step in range(NS_STEPS):
        squares = [dot(g, g) for g in grams]
        polys = [
            coef_first * unit + coef_second * g + coef_third * s for g, s in zip(grams, squares)
        ]
        totals = [dot(q, p) for q, p in zip(totals, polys)]
        if step + 1 < NS_STEPS:
            halves = [dot(g, p) for g, p in zip(grams, polys)]
            grams = [dot(p, h) for p, h in zip(polys, halves)]
    for n in range(count):
        out_ref[n] = totals[n]


def polynomials(grams):
    count, width, _ = grams.shape
    return pl.pallas_call(
        polynomial_kernel,
        out_shape=jax.ShapeDtypeStruct(grams.shape, f32),
        in_specs=[pl.BlockSpec(memory_space=pltpu.VMEM)],
        out_specs=pl.BlockSpec(memory_space=pltpu.VMEM),
        compiler_params=pltpu.CompilerParams(vmem_limit_bytes=32 << 20),
        cost_estimate=pl.CostEstimate(
            flops=2 * 6 * 20 * count * width**3,
            bytes_accessed=8 * count * width**2,
            transcendentals=0,
        ),
        name="polynomials",
    )(grams)


def orthogonal(state):
    slabs = state.reshape(state.shape[0], -1, HDIM)
    count = slabs.shape[1]
    grams = jnp.einsum("dnk,dnl->nkl", slabs, slabs, precision=highest)
    size = lax.axis_size("fsdp")
    if size == 4 and count % 4 == 0:
        mine = lax.axis_index("fsdp")
        cut = grams.reshape(4, count // 4, HDIM, HDIM)
        take = lambda k: lax.dynamic_index_in_dim(cut, mine ^ k, 0, keepdims=False)
        total = take(0) + swap_fsdp(take(1), 1) + swap_fsdp(take(2), 2) + swap_fsdp(take(3), 3)
        own = polynomials(total)
        full = jnp.zeros(cut.shape, f32)
        for k in range(4):
            got = own if k == 0 else swap_fsdp(own, k)
            full = lax.dynamic_update_index_in_dim(full, got, mine ^ k, 0)
        full = full.reshape(count, HDIM, HDIM)
    else:
        full = polynomials(lax.psum(grams, "fsdp"))
    return jnp.einsum("dnk,nkl->dnl", slabs, full, precision=highest).reshape(state.shape)


def pack(matrices):
    qkv, out, up, down = matrices
    count = lax.axis_size("ctx")
    rows = up.shape[0]
    low = lambda v: v.astype(bf16)
    four = jnp.concatenate([low(qkv), low(out).T[None]], axis=0)
    attn = four.reshape(4, rows, count, -1).transpose(2, 1, 0, 3).reshape(count, rows, -1)
    up_cut = low(up).reshape(rows, count, -1).transpose(1, 0, 2)
    down_cut = low(down).T.reshape(rows, count, -1).transpose(1, 0, 2)
    return attn, up_cut, down_cut


def unpack(attn, up, down):
    count, rows, _ = up.shape
    four = attn.reshape(count, rows, 4, -1).transpose(2, 1, 0, 3).reshape(4, rows, -1)
    flat = lambda v: v.transpose(1, 0, 2).reshape(rows, -1)
    return four[:3], four[3].T, flat(up), flat(down).T


def over_ctx(stack):
    return lax.all_to_all(stack, "ctx", split_axis=0, concat_axis=0, tiled=True)


def to_blocks(stack):
    moved = over_ctx(stack)
    return moved.reshape(-1, moved.shape[-1])


def from_blocks(block):
    return over_ctx(block.reshape(lax.axis_size("ctx"), -1, block.shape[-1]))


def sum_everywhere(vector):
    if lax.axis_size("ctx") != 4 or lax.axis_size("fsdp") != 4:
        return lax.psum(vector, ("fsdp", "ctx", "tp"))
    vector = vector + swap_core(vector)
    vector = vector + swap_ctx(vector, 1)
    vector = vector + swap_ctx(vector, 2)
    vector = vector + swap_fsdp(vector, 1)
    return vector + swap_fsdp(vector, 2)


def body(
    inputs,
    segment_ids,
    cotangent,
    w_qkv,
    w_out,
    w_up,
    w_down,
    bias_qv,
    bias_up,
    bias_res,
    norm_gain,
    norm_shift,
    moment_qkv,
    moment_out,
    moment_up,
    moment_down,
    moment_bqv,
    moment_bup,
    moment_bres,
    moment_gain,
    moment_shift,
):
    count_c = lax.axis_size("ctx")
    count_f = lax.axis_size("fsdp")
    c = lax.axis_index("ctx")
    t = lax.axis_index("tp")
    rows = inputs.shape[2]
    width = inputs.shape[3]
    length = rows * count_c
    token_total = inputs.shape[0] * inputs.shape[1] * count_f * length
    e = w_qkv.shape[2] // count_c
    u = w_up.shape[1] // count_c

    own_micro = lambda v: lax.dynamic_index_in_dim(v, t, 0, keepdims=False)[0]
    row_low = own_micro(inputs)
    row_values = row_low.astype(f32)
    upper = own_micro(cotangent).astype(f32)
    segments = own_micro(segment_ids)
    index = jnp.arange(count_c)
    order = index ^ c if count_c == 4 else index
    place = (segments * (length + HALF + 1) + jnp.arange(length, dtype=jnp.int32)).reshape(count_c, rows)
    place = jnp.take(place, order, axis=0).reshape(length)

    weights = [to_blocks(s) for s in pack((w_qkv, w_out, w_up, w_down))]
    moments = [to_blocks(s) for s in pack((moment_qkv, moment_out, moment_up, moment_down))]
    gathered = [lax.all_gather(w, "fsdp", axis=0, tiled=True) for w in weights]
    attn_w, up_w, down_w = [(g, swap_core(g)) for g in gathered]

    bias_q = lax.dynamic_slice_in_dim(bias_qv, c * e, e, 1)
    bias_u = lax.dynamic_slice_in_dim(bias_up, c * u, u, 0)
    small = jnp.concatenate([bias_q.reshape(-1), bias_u])
    small_pair = (small, swap_core(small))
    cores = range(2)

    xs = jnp.concatenate(spread(row_low), axis=0)
    qkv = []
    for i in cores:
        shift = jnp.concatenate([small_pair[i][:e], jnp.zeros((e,), f32), small_pair[i][e : 2 * e]])
        qkv.append((mm(xs, attn_w[i][:, : 3 * e], (1, 0)) + shift).astype(bf16))
    context = [attend_forward(qkv[i], place) for i in cores]
    part = sum(mm(context[i], attn_w[i][:, 3 * e :], (1, 1)) for i in cores).astype(bf16)
    attended = collect(part) + bias_res[0]
    first, first_unit, first_inverse = layer_norm(row_values + attended, norm_gain[0], norm_shift[0])
    first_all = jnp.concatenate(spread(first.astype(bf16)), axis=0)
    pre_act = [mm(first_all, up_w[i], (1, 0)) + small_pair[i][2 * e :] for i in cores]
    active = [gelu_tanh(p).astype(bf16) for p in pre_act]
    part = sum(mm(active[i], down_w[i], (1, 1)) for i in cores).astype(bf16)
    branch = collect(part) + bias_res[1]
    out_rows, second_unit, second_inverse = layer_norm(first + branch, norm_gain[1], norm_shift[1])
    out_rows = out_rows.astype(bf16)

    grad_second, gain_second, shift_second = layer_norm_back(
        upper, second_unit, second_inverse, norm_gain[1]
    )
    grad_branch = grad_second.astype(bf16)
    branch_all = jnp.concatenate(spread(grad_branch), axis=0)
    grad_pre = []
    for i in cores:
        grad_act = mm(branch_all, down_w[i], (1, 0))
        grad_pre.append(jax.vjp(gelu_tanh, pre_act[i])[1](grad_act)[0].astype(bf16))
    part = sum(mm(grad_pre[i], up_w[i], (1, 1)) for i in cores).astype(bf16)
    term_down = [mm(branch_all, active[i], (0, 0)) for i in cores]
    term_up = [mm(first_all, grad_pre[i], (0, 0)) for i in cores]
    grad_first_out = grad_second + collect(part)
    grad_first, gain_first, shift_first = layer_norm_back(
        grad_first_out, first_unit, first_inverse, norm_gain[0]
    )
    grad_attended = grad_first.astype(bf16)
    attended_all = jnp.concatenate(spread(grad_attended), axis=0)
    grad_qkv_low = []
    for i in cores:
        grad_context = mm(attended_all, attn_w[i][:, 3 * e :], (1, 0)).astype(bf16)
        grad_qkv_low.append(attend_backward(qkv[i], grad_context, place))
    part = sum(mm(grad_qkv_low[i], attn_w[i][:, : 3 * e], (1, 1)) for i in cores).astype(bf16)
    term_attn = [
        jnp.concatenate(
            [mm(xs, grad_qkv_low[i], (0, 0)), mm(attended_all, context[i], (0, 0))], axis=1
        )
        for i in cores
    ]
    input_rows = grad_first + collect(part)

    both = lambda own, other: jnp.stack([jnp.where(t == m, own, other) for m in range(2)])[:, None]
    layer_out = both(out_rows, swap_core(out_rows))
    input_grad = both(input_rows, swap_core(input_rows))

    def to_owner(terms):
        total = terms[0] + swap_core(terms[1].astype(bf16)).astype(f32)
        return lax.psum_scatter(total.astype(bf16), "fsdp", scatter_dimension=0, tiled=True)

    sums = [to_owner(term) for term in (term_attn, term_up, term_down)]
    grads = [g.astype(f32) for g in unpack(*[from_blocks(s) for s in sums])]
    orthos = []
    for total, moment in zip(sums, moments):
        state = decay_rate * moment.astype(f32) + total.astype(f32)
        orthos.append(from_blocks(orthogonal(state).astype(bf16)))
    orthos = [o.astype(f32) for o in unpack(*orthos)]
    step_scale = matrix_rate * math.sqrt(width / HDIM)
    states = [
        decay_rate * m + g
        for m, g in zip((moment_qkv, moment_out, moment_up, moment_down), grads)
    ]
    masters = [w - step_scale * o for w, o in zip((w_qkv, w_out, w_up, w_down), orthos)]

    qv_sums = []
    for i in cores:
        sums_i = jnp.sum(grad_qkv_low[i].astype(f32), axis=0)
        qv_sums.append(jnp.stack([sums_i[:e], sums_i[2 * e :]]))
    up_sums = [jnp.sum(g.astype(f32), axis=0) for g in grad_pre]
    side = lambda pair: [jnp.where(t == m, pair[0], pair[1]) for m in range(2)]
    bqv_all = jnp.stack(
        [
            lax.dynamic_update_slice_in_dim(jnp.zeros((2, count_c * e), f32), v, c * e, 1)
            for v in side(qv_sums)
        ]
    )
    bup_all = jnp.stack(
        [
            lax.dynamic_update_slice_in_dim(jnp.zeros((count_c * u,), f32), v, c * u, 0)
            for v in side(up_sums)
        ]
    )
    rest = jnp.stack(
        [
            jnp.sum(grad_attended.astype(f32), axis=0),
            jnp.sum(grad_branch.astype(f32), axis=0),
            gain_first,
            gain_second,
            shift_first,
            shift_second,
        ]
    )
    flat = sum_everywhere(
        jnp.concatenate([bqv_all.reshape(-1), bup_all.reshape(-1), rest.reshape(-1)])
    )
    cut = bqv_all.size
    cut_two = cut + bup_all.size
    grad_bqv = lax.dynamic_index_in_dim(flat[:cut].reshape(bqv_all.shape), t, 0, keepdims=False)
    grad_bup = lax.dynamic_index_in_dim(flat[cut:cut_two].reshape(bup_all.shape), t, 0, keepdims=False)
    rest = flat[cut_two:].reshape(3, 2, width)
    vector_grads = (grad_bqv, grad_bup, rest[0], rest[1], rest[2])
    vector_states = [
        decay_rate * m + g
        for m, g in zip(
            (moment_bqv, moment_bup, moment_bres, moment_gain, moment_shift), vector_grads
        )
    ]
    vector_step = 1.0 / math.sqrt(token_total)
    vector_masters = [
        v - vector_step * s
        for v, s in zip((bias_qv, bias_up, bias_res, norm_gain, norm_shift), vector_states)
    ]
    return (
        layer_out,
        input_grad,
        *grads,
        *vector_grads,
        *states,
        *vector_states,
        *masters,
        *vector_masters,
    )


def solution(mesh):
    rows = P(None, "fsdp", "ctx", None)
    matrices = (
        P(None, ("fsdp", "ctx"), "tp"),
        P("tp", ("fsdp", "ctx")),
        P(("fsdp", "ctx"), "tp"),
        P("tp", ("fsdp", "ctx")),
    )
    vectors = (P(None, "tp"), P("tp"), P(), P(), P())
    return jax.shard_map(
        body,
        mesh=mesh,
        in_specs=(rows, P(None, "fsdp", None), rows, *matrices, *vectors, *matrices, *vectors),
        out_specs=(rows, rows, *((*matrices, *vectors) * 3)),
        check_vma=False,
    )
```

time: 3430 us -> 928 us (0.27)
  waiting for transfers between devices: 2670 us -> 352 us
  matrix products: 410 us -> 161 us
  Pallas kernels: 0 us -> 45.1 us
  local copies, waits for them, and re-layouts: 146 us -> 105 us
  starting transfers between devices: 72.9 us -> 110 us
  blocking collectives: 0 us -> 35.3 us
    reduce_scatter x4 -> x3, waiting for transfers between devices: 1650 us -> 0.01 us  [to_owner(): lax.psum_scatter(total.astype(bf16), 'fsdp', scatter_dimension=0, tiled=T...]
    all_gather x4 -> x3, waiting for transfers between devices: 577 us -> 69.3 us  [body(): gathered = [lax.all_gather(w, 'fsdp', axis=0, tiled=True) for w in weights]]
    dot_general x51 -> x30, matrix products: 410 us -> 161 us  [the longest x24 143 us: mm(): lax.dot_general(left, right, ((dims[:1], dims[1:]), ((), ())), preferred_...]
    psum x5 -> x0, waiting for transfers between devices: 223 us -> none  [the longest x1 125 us: body(): lax.psum((vector_sums[0], vector_sums[1], vector_sums[2], vector_sums[3],...]
    ppermute x16 -> x64, waiting for transfers between devices: 159 us -> 231 us  [the longest x34 205 us: swap_ctx(): return lax.ppermute(value, 'ctx', xor_pairs(4, mask))]
    pallas_call x0 -> x7, Pallas kernels: none -> 45.1 us  [the longest x2 21 us: attend_backward(): pl.pallas_call(lambda *refs: attend_back_kernel(256, *refs), out_shape=(o...]
    all_to_all x0 -> x2, blocking collectives: none -> 35.3 us  [over_ctx(): return lax.all_to_all(stack, 'ctx', split_axis=0, concat_axis=0, tiled=True)]
    ppermute x16 -> x64, starting transfers between devices: 45.5 us -> 70 us  [the longest x34 38.8 us: swap_ctx(): return lax.ppermute(value, 'ctx', xor_pairs(4, mask))]
  transfers between devices with their start and end apart: 31 -> 80, of which waited for: 19 -> 43; matrix products, arithmetic and copies ran while one was open for 11% -> 31% of each run, Pallas kernels for 0% -> 5%
where the time goes in v1:
time: 928 us; the launch traced here: 920 us
  waiting for transfers between devices  352 us (38%)
  matrix products  161 us (17%)
  starting transfers between devices  110 us (12%)
  local copies, waits for them, and re-layouts  105 us (11%)
  other arithmetic  95.4 us (10%)
  Pallas kernels  45.1 us (5%)
  blocking collectives  35.3 us (4%)
  between operations  16.7 us (2%)
    ppermute x34, waiting for transfers between devices, swap_ctx(): return lax.ppermute(value, 'ctx', xor_pairs(4, mask))  205 us
    dot_general x24, matrix products, mm(): lax.dot_general(left, right, ((dims[:1], dims[1:]), ((), ())), preferred_...  143 us
    all_gather x3, waiting for transfers between devices, body(): gathered = [lax.all_gather(w, 'fsdp', axis=0, tiled=True) for w in weights]  69.3 us
    all_to_all x10, waiting for transfers between devices, over_ctx(): return lax.all_to_all(stack, 'ctx', split_axis=0, concat_axis=0, tiled=True)  50.9 us
    all_to_all x10, starting transfers between devices, over_ctx(): return lax.all_to_all(stack, 'ctx', split_axis=0, concat_axis=0, tiled=True)  40 us
    unnamed x199, local copies, waits for them, and re-layouts  39.2 us
    ppermute x34, starting transfers between devices, swap_ctx(): return lax.ppermute(value, 'ctx', xor_pairs(4, mask))  38.8 us
    all_to_all x2, blocking collectives, over_ctx(): return lax.all_to_all(stack, 'ctx', split_axis=0, concat_axis=0, tiled=True)  35.3 us
  transfers between devices with their start and end apart: 80, of which 43 were waited for; matrix products, arithmetic and copies ran while one was open for 31% of the time, Pallas kernels for 5%

profile of v1, /device:TPU:0, one launch (start us, length us, event | category | flops | bytes accessed | tf_op | source)
XLA Modules:
  0.0 920.2 jit_solution(10522177746072195574)
XLA Ops:
  10.3 19.2 %all_to_all.60 = bf16[4,128,1024]{1,2,0:T(8,128)(2,1)S(1)} all-to-all(bf16[4,128,1024]{1,2,0:T(8,128)(2,1)S(1)} %bitcast.355), channel_id=1, replica_groups=mesh['fsdp'=4,'ctx'=4,'tp'=2] {'ctx'}, dimensions={0} | all-to-all | bytes 2097152 | tf_op jit(solution)/shard_map/all_to_all | solution.py:283
  31.7 16.0 %all_to_all.61 = bf16[4,128,1024]{1,2,0:T(8,128)(2,1)} all-to-all(bf16[4,128,1024]{1,2,0:T(8,128)(2,1)S(1)} %bitcast.348), channel_id=1, replica_groups=mesh['fsdp'=4,'ctx'=4,'tp'=2] {'ctx'}, dimensions={0} | all-to-all | bytes 2097152 | tf_op jit(solution)/shard_map/all_to_all | solution.py:283
  50.1 61.4 %all-gather.4.cloned.1.call-done = bf16[2048,1024]{1,0:T(8,128)(2,1)} async-done(((bf16[512,1024]{1,0:T(8,128)(2,1)}), bf16[2048,1024]{1,0:T(8,128)(2,1)}) %all-gather.4.cloned.1.call-update) | async-done | bytes 4194320 | tf_op jit(solution)/shard_map/all_gather | solution.py:351
  123.4 16.6 %collective-permute-done = bf16[256,2048]{1,0:T(8,128)(2,1)} collective-permute-done((bf16[256,2048]{1,0:T(8,128)(2,1)S(1)}, bf16[256,2048]{1,0:T(8,128)(2,1)}, u32[]{:S(2)}, u32[]{:S(2)}) %collective-permute-start) | collective-permute-done | bytes 1048608 | tf_op jit(solution)/shard_map/ppermute | solution.py:38
  143.5 9.3 %all-to-all-done.2 = bf16[4,128,1024]{1,2,0:T(8,128)(2,1)S(1)} async-done(((bf16[4,128,1024]{1,2,0:T(8,128)(2,1)}), bf16[4,128,1024]{1,2,0:T(8,128)(2,1)S(1)}, u32[]{:S(2)}, u32[]{:S(2)}) %all-to-all-start.2) | async-done | bytes 1048608 | tf_op jit(solution)/shard_map/all_to_all | solution.py:283
  168.7 5.6 add_convert_fusion.7.refs_0_.refs_1_.refs_2_
  174.4 5.7 attend_forward.2
  182.5 5.3 add_convert_fusion.6.refs_0_.refs_1_.refs_2_
  187.8 5.9 attend_forward.3
  202.2 20.7 %collective-permute-done.6 = bf16[256,2048]{1,0:T(8,128)(2,1)S(1)} collective-permute-done((bf16[256,2048]{1,0:T(8,128)(2,1)}, bf16[256,2048]{1,0:T(8,128)(2,1)S(1)}, u32[]{:S(2)}, u32[]{:S(2)}) %collective-permute-start.6) | collective-permute-done | bytes 1048608 | tf_op jit(solution)/shard_map/ppermute | solution.py:38
  227.3 10.5 %collective-permute-done.7 = bf16[128,2048]{1,0:T(8,128)(2,1)S(1)} collective-permute-done((bf16[128,2048]{1,0:T(8,128)(2,1)S(1)}, bf16[128,2048]{1,0:T(8,128)(2,1)S(1)}, u32[]{:S(2)}, u32[]{:S(2)}) %collective-permute-start.7) | collective-permute-done | bytes 524320 | tf_op jit(solution)/shard_map/ppermute | solution.py:38
  243.0 20.3 %collective-permute-done.10 = bf16[256,2048]{1,0:T(8,128)(2,1)S(1)} collective-permute-done((bf16[256,2048]{1,0:T(8,128)(2,1)}, bf16[256,2048]{1,0:T(8,128)(2,1)S(1)}, u32[]{:S(2)}, u32[]{:S(2)}) %collective-permute-start.10) | collective-permute-done | bytes 1048608 | tf_op jit(solution)/shard_map/ppermute | solution.py:38
  266.6 7.9 all-gather.8.cloned.1.call-done
  282.8 7.2 collective-permute-done.13
  290.8 6.6 fusion.123
  297.5 9.9 %fusion.124 = f32[1024,1024]{1,0:T(8,128)} fusion(bf16[1024,2048]{1,0:T(8,128)(2,1)S(1)} %copy-done.53, bf16[2048,1024]{1,0:T(8,128)(2,1)} %collective-permute-done.14), kind=kOutput, calls=%fused_computation.301 | convolution fusion | flops 4294967296 | bytes 12582912 | tf_op jit(solution)/shard_map/dot_general | solution.py:46
  307.4 7.6 fusion.99
  317.0 9.4 %add_convert_fusion.4 = bf16[1024,2048]{1,0:T(8,128)(2,1)S(1)} fusion(f32[1024,2048]{1,0:T(8,128)} %fusion.99, bf16[2048,1024]{1,0:T(8,128)(2,1)S(1)} %collective-permute-done.15, f32[1024,1024]{1,0:T(8,128)} %fusion.124, f32[1024]{0:T(1024)S(1)} %slice.493), kind=kOutput, calls=%fused_computation.7 | convolution fusion | flops 4309647360 | bytes 20975616 | tf_op jit(solution)/shard_map/dot_general | solution.py:46
  330.0 21.6 %collective-permute-done.16 = bf16[256,2048]{1,0:T(8,128)(2,1)S(1)} collective-permute-done((bf16[256,2048]{1,0:T(8,128)(2,1)S(1)}, bf16[256,2048]{1,0:T(8,128)(2,1)S(1)}, u32[]{:S(2)}, u32[]{:S(2)}) %collective-permute-start.16) | collective-permute-done | bytes 1048608 | tf_op jit(solution)/shard_map/ppermute | solution.py:38
  356.0 10.1 %collective-permute-done.17 = bf16[128,2048]{1,0:T(8,128)(2,1)S(1)} collective-permute-done((bf16[128,2048]{1,0:T(8,128)(2,1)S(1)}, bf16[128,2048]{1,0:T(8,128)(2,1)S(1)}, u32[]{:S(2)}, u32[]{:S(2)}) %collective-permute-start.17) | collective-permute-done | bytes 524320 | tf_op jit(solution)/shard_map/ppermute | solution.py:38
  374.8 20.1 %collective-permute-done.21 = bf16[256,2048]{1,0:T(8,128)(2,1)} collective-permute-done((bf16[256,2048]{1,0:T(8,128)(2,1)}, bf16[256,2048]{1,0:T(8,128)(2,1)}, u32[]{:S(2)}, u32[]{:S(2)}) %collective-permute-start.21) | collective-permute-done | bytes 1048608 | tf_op jit(solution)/shard_map/ppermute | solution.py:38
  409.4 7.3 convert_reduce_fusion
  416.7 6.5 convolution_convert_fusion.1
  423.2 7.2 convert_reduce_fusion.1
  430.4 6.8 fusion.125
  437.3 8.2 add_convert_fusion.3
  448.5 9.2 convolution_convert_fusion
  458.2 8.6 collective-permute-done.25
  473.2 6.4 collective-permute-done.26
  488.9 7.9 add_convert_fusion.1
  498.4 6.9 collective-permute-done.29
  519.8 10.6 %attend_backward.2 = (bf16[1024,256]{1,0:T(8,128)(2,1)S(1)}, bf16[1024,256]{1,0:T(8,128)(2,1)S(1)}, bf16[1024,256]{1,0:T(8,128)(2,1)S(1)}) custom-call(bf16[1024,768]{1,0:T(8,128)(2,1)S(1)} %copy-done.3, bf16[1024,768]{1,0:T(8,128)(2,1)S(1)} %copy-done.3, bf16[1024,768]{1,0:T(8,128)(2,1)S(1)} %copy-done.3, ...), custom_call_target="tpu_custom_call" | custom-call | flops 2684354560 | bytes 3670016 | tf_op jit(solution)/shard_map/attend_backward/pallas_call | solution.py:173
  533.1 10.5 %attend_backward.3 = (bf16[1024,256]{1,0:T(8,128)(2,1)S(1)}, bf16[1024,256]{1,0:T(8,128)(2,1)S(1)}, bf16[1024,256]{1,0:T(8,128)(2,1)S(1)}) custom-call(bf16[1024,768]{1,0:T(8,128)(2,1)S(1)} %copy-done.1, bf16[1024,768]{1,0:T(8,128)(2,1)S(1)} %copy-done.1, bf16[1024,768]{1,0:T(8,128)(2,1)S(1)} %copy-done.1, ...), custom_call_target="tpu_custom_call" | custom-call | flops 2684354560 | bytes 3670016 | tf_op jit(solution)/shard_map/attend_backward/pallas_call | solution.py:173
  543.8 6.0 fusion.18
  549.7 7.1 add_convert_fusion.2
  561.5 8.4 add_convert_fusion
  586.4 7.0 collective-permute-done.42
  594.2 5.5 fusion.126
  599.6 12.4 %collective-permute-done.43 = f32[24576]{0:T(1024)S(1)} collective-permute-done((f32[24576]{0:T(1024)S(1)}, f32[24576]{0:T(1024)S(1)}, u32[]{:S(2)}, u32[]{:S(2)}) %collective-permute-start.43) | collective-permute-done | bytes 98336 | tf_op jit(solution)/shard_map/ppermute | solution.py:38
  612.4 7.6 collective-permute-done.44
  623.3 9.7 %collective-permute-done.45 = f32[24576]{0:T(1024)S(1)} collective-permute-done((f32[24576]{0:T(1024)S(1)}, f32[24576]{0:T(1024)S(1)}, u32[]{:S(2)}, u32[]{:S(2)}) %collective-permute-start.45) | collective-permute-done | bytes 98336 | tf_op jit(solution)/shard_map/ppermute | solution.py:42
  639.2 10.1 %collective-permute-done.34 = bf16[128,2048]{1,0:T(8,128)(2,1)S(1)} collective-permute-done((bf16[128,2048]{1,0:T(8,128)(2,1)}, bf16[128,2048]{1,0:T(8,128)(2,1)S(1)}, u32[]{:S(2)}, u32[]{:S(2)}) %collective-permute-start.34) | collective-permute-done | bytes 524320 | tf_op jit(solution)/shard_map/ppermute | solution.py:38
  654.1 6.4 fusion
  667.3 11.4 %all-to-all-done.4 = bf16[4,128,1024]{2,1,0:T(8,128)(2,1)S(1)} async-done(((bf16[4,128,1024]{2,1,0:T(8,128)(2,1)}), bf16[4,128,1024]{2,1,0:T(8,128)(2,1)S(1)}, u32[]{:S(2)}, u32[]{:S(2)}) %all-to-all-start.4) | async-done | bytes 1048608 | tf_op jit(solution)/shard_map/all_to_all | solution.py:283
  687.8 8.4 all-to-all-done.5
  714.9 8.9 all-to-all-done.8
  837.0 6.6 collective-permute-start.48
  896.2 8.0 all-to-all-done.7
  (550 shorter events, 387.3 us)
Async XLA Ops:
  7.2 104.3 %all-gather.4.cloned.1.call-start = ((), (), s32[]{:S(2)}) async-start(), calls=%async_computation.15 | async-start | bytes 5242880 | tf_op jit(solution)/shard_map/all_gather | solution.py:351
  30.9 171.3 %all-gather.6.cloned.1.call-start = ((), (), s32[]{:S(2)}) async-start(), calls=%async_computation.16 | async-start | bytes 5242880 | tf_op jit(solution)/shard_map/all_gather | solution.py:351
  111.5 69.9 %collective-permute-start.4 = (bf16[2048,1024]{1,0:T(8,128)(2,1)}, bf16[2048,1024]{1,0:T(8,128)(2,1)}, u32[]{:S(2)}, u32[]{:S(2)}) collective-permute-start(bf16[2048,1024]{1,0:T(8,128)(2,1)} %all-gather.4.cloned.1.call-done), channel_id=1, source_target_pairs={{0,1},{1,0},{2,3},{3,2},{4,5},{5,4},{6,7},{7,6},{8,9},{9,8},{10,11... | collective-permute-start | bytes 12582920 | tf_op jit(solution)/shard_map/ppermute | solution.py:34
  114.0 26.1 %collective-permute-start = (bf16[256,2048]{1,0:T(8,128)(2,1)S(1)}, bf16[256,2048]{1,0:T(8,128)(2,1)}, u32[]{:S(2)}, u32[]{:S(2)}) collective-permute-start(bf16[256,2048]{1,0:T(8,128)(2,1)S(1)} %get-tuple-element.194), channel_id=1, source_target_pairs={{0,2},{2,0},{4,6},{6,4},{1,3},{3,1},{5,7},{7,5},{8,10},{10,8},{12,... | collective-permute-start | bytes 3145736 | tf_op jit(solution)/shard_map/ppermute | solution.py:38
  115.5 38.6 %collective-permute-start.1 = (bf16[256,2048]{1,0:T(8,128)(2,1)S(1)}, bf16[256,2048]{1,0:T(8,128)(2,1)}, u32[]{:S(2)}, u32[]{:S(2)}) collective-permute-start(bf16[256,2048]{1,0:T(8,128)(2,1)S(1)} %get-tuple-element.194), channel_id=1, source_target_pairs={{0,4},{2,6},{4,0},{6,2},{1,5},{3,7},{5,1},{7,3},{8,12},{10,14},{12... | collective-permute-start | bytes 3145736 | tf_op jit(solution)/shard_map/ppermute | solution.py:38
  118.8 34.0 %all-to-all-start.2 = ((bf16[4,128,1024]{1,2,0:T(8,128)(2,1)}), bf16[4,128,1024]{1,2,0:T(8,128)(2,1)S(1)}, u32[]{:S(2)}, u32[]{:S(2)}) async-start(bf16[4,128,1024]{1,2,0:T(8,128)(2,1)} %bitcast.18), calls=%async_computation.2 | async-start | bytes 2097152 | tf_op jit(solution)/shard_map/all_to_all | solution.py:283
  122.3 152.2 %all-gather.8.cloned.1.call-start = ((), (), s32[]{:S(2)}) async-start(), calls=%async_computation.17 | async-start | bytes 5242880 | tf_op jit(solution)/shard_map/all_gather | solution.py:351
  141.9 21.4 %collective-permute-start.2 = (bf16[128,2048]{1,0:T(8,128)(2,1)}, bf16[128,2048]{1,0:T(8,128)(2,1)}, u32[]{:S(2)}, u32[]{:S(2)}) collective-permute-start(bf16[128,2048]{1,0:T(8,128)(2,1)} %slice.470), channel_id=1, source_target_pairs={{0,4},{2,6},{4,0},{6,2},{1,5},{3,7},{5,1},{7,3},{8,12},{10,14},{12... | collective-permute-start | bytes 1572872 | tf_op jit(solution)/shard_map/ppermute | solution.py:38
  154.0 507.8 %reduce-scatter.6.cloned.1.call-start = ((), (), s32[]{:S(2)}) async-start(), calls=%async_computation.19 | async-start | bytes 5242880 | tf_op jit(solution)/shard_map/reduce_scatter | solution.py:414
  198.9 24.1 %collective-permute-start.6 = (bf16[256,2048]{1,0:T(8,128)(2,1)}, bf16[256,2048]{1,0:T(8,128)(2,1)S(1)}, u32[]{:S(2)}, u32[]{:S(2)}) collective-permute-start(bf16[256,2048]{1,0:T(8,128)(2,1)} %pad_maximum_fusion.1), channel_id=1, source_target_pairs={{0,2},{2,0},{4,6},{6,4},{1,3},{3,1},{5,7},{7,5},{8,10},{10,8},{12,... | collective-permute-start | bytes 3145736 | tf_op jit(solution)/shard_map/ppermute | solution.py:38
  201.5 24.0 %collective-permute-start.8 = (bf16[256,2048]{1,0:T(8,128)(2,1)}, bf16[256,2048]{1,0:T(8,128)(2,1)S(1)}, u32[]{:S(2)}, u32[]{:S(2)}) collective-permute-start(bf16[256,2048]{1,0:T(8,128)(2,1)} %pad_maximum_fusion.2), channel_id=1, source_target_pairs={{0,4},{2,6},{4,0},{6,2},{1,5},{3,7},{5,1},{7,3},{8,12},{10,14},{12... | collective-permute-start | bytes 3145736 | tf_op jit(solution)/shard_map/ppermute | solution.py:38
  202.2 95.3 %collective-permute-start.14 = (bf16[2048,1024]{1,0:T(8,128)(2,1)}, bf16[2048,1024]{1,0:T(8,128)(2,1)}, u32[]{:S(2)}, u32[]{:S(2)}) collective-permute-start(bf16[2048,1024]{1,0:T(8,128)(2,1)} %all-gather.6.cloned.1.call-done), channel_id=1, source_target_pairs={{0,1},{1,0},{2,3},{3,2},{4,5},{5,4},{6,7},{7,6},{8,9},{9,8},{10,11... | collective-permute-start | bytes 12582920 | tf_op jit(solution)/shard_map/ppermute | solution.py:34
  241.1 22.3 %collective-permute-start.10 = (bf16[256,2048]{1,0:T(8,128)(2,1)}, bf16[256,2048]{1,0:T(8,128)(2,1)S(1)}, u32[]{:S(2)}, u32[]{:S(2)}) collective-permute-start(bf16[256,2048]{1,0:T(8,128)(2,1)} %get-tuple-element.190), channel_id=1, source_target_pairs={{0,2},{2,0},{4,6},{6,4},{1,3},{3,1},{5,7},{7,5},{8,10},{10,8},{12,... | collective-permute-start | bytes 3145736 | tf_op jit(solution)/shard_map/ppermute | solution.py:38
  241.3 33.1 %collective-permute-start.11 = (bf16[256,2048]{1,0:T(8,128)(2,1)}, bf16[256,2048]{1,0:T(8,128)(2,1)}, u32[]{:S(2)}, u32[]{:S(2)}) collective-permute-start(bf16[256,2048]{1,0:T(8,128)(2,1)} %get-tuple-element.190), channel_id=1, source_target_pairs={{0,4},{2,6},{4,0},{6,2},{1,5},{3,7},{5,1},{7,3},{8,12},{10,14},{12... | collective-permute-start | bytes 3145736 | tf_op jit(solution)/shard_map/ppermute | solution.py:38
  274.5 40.5 %collective-permute-start.15 = (bf16[2048,1024]{1,0:T(8,128)(2,1)}, bf16[2048,1024]{1,0:T(8,128)(2,1)S(1)}, u32[]{:S(2)}, u32[]{:S(2)}) collective-permute-start(bf16[2048,1024]{1,0:T(8,128)(2,1)} %all-gather.8.cloned.1.call-done), channel_id=1, source_target_pairs={{0,1},{1,0},{2,3},{3,2},{4,5},{5,4},{6,7},{7,6},{8,9},{9,8},{10,11... | collective-permute-start | bytes 12582920 | tf_op jit(solution)/shard_map/ppermute | solution.py:34
  326.8 24.9 %collective-permute-start.16 = (bf16[256,2048]{1,0:T(8,128)(2,1)S(1)}, bf16[256,2048]{1,0:T(8,128)(2,1)S(1)}, u32[]{:S(2)}, u32[]{:S(2)}) collective-permute-start(bf16[256,2048]{1,0:T(8,128)(2,1)S(1)} %pad_maximum_fusion.3), channel_id=1, source_target_pairs={{0,2},{2,0},{4,6},{6,4},{1,3},{3,1},{5,7},{7,5},{8,10},{10,8},{12,... | collective-permute-start | bytes 3145736 | tf_op jit(solution)/shard_map/ppermute | solution.py:38
  328.5 24.6 %collective-permute-start.18 = (bf16[256,2048]{1,0:T(8,128)(2,1)S(1)}, bf16[256,2048]{1,0:T(8,128)(2,1)S(1)}, u32[]{:S(2)}, u32[]{:S(2)}) collective-permute-start(bf16[256,2048]{1,0:T(8,128)(2,1)S(1)} %pad_maximum_fusion.4), channel_id=1, source_target_pairs={{0,4},{2,6},{4,0},{6,2},{1,5},{3,7},{5,1},{7,3},{8,12},{10,14},{12... | collective-permute-start | bytes 3145736 | tf_op jit(solution)/shard_map/ppermute | solution.py:38
  372.2 22.7 %collective-permute-start.21 = (bf16[256,2048]{1,0:T(8,128)(2,1)}, bf16[256,2048]{1,0:T(8,128)(2,1)}, u32[]{:S(2)}, u32[]{:S(2)}) collective-permute-start(bf16[256,2048]{1,0:T(8,128)(2,1)} %get-tuple-element.178), channel_id=1, source_target_pairs={{0,2},{2,0},{4,6},{6,4},{1,3},{3,1},{5,7},{7,5},{8,10},{10,8},{12,... | collective-permute-start | bytes 3145736 | tf_op jit(solution)/shard_map/ppermute | solution.py:38
  372.9 25.2 %collective-permute-start.22 = (bf16[256,2048]{1,0:T(8,128)(2,1)}, bf16[256,2048]{1,0:T(8,128)(2,1)}, u32[]{:S(2)}, u32[]{:S(2)}) collective-permute-start(bf16[256,2048]{1,0:T(8,128)(2,1)} %get-tuple-element.178), channel_id=1, source_target_pairs={{0,4},{2,6},{4,0},{6,2},{1,5},{3,7},{5,1},{7,3},{8,12},{10,14},{12... | collective-permute-start | bytes 3145736 | tf_op jit(solution)/shard_map/ppermute | solution.py:38
  445.9 20.8 %collective-permute-start.25 = (bf16[256,2048]{1,0:T(8,128)(2,1)S(1)}, bf16[256,2048]{1,0:T(8,128)(2,1)S(1)}, u32[]{:S(2)}, u32[]{:S(2)}) collective-permute-start(bf16[256,2048]{1,0:T(8,128)(2,1)S(1)} %pad_maximum_fusion.5), channel_id=1, source_target_pairs={{0,2},{2,0},{4,6},{6,4},{1,3},{3,1},{5,7},{7,5},{8,10},{10,8},{12,... | collective-permute-start | bytes 3145736 | tf_op jit(solution)/shard_map/ppermute | solution.py:38
  447.0 22.8 %collective-permute-start.27 = (bf16[256,2048]{1,0:T(8,128)(2,1)S(1)}, bf16[256,2048]{1,0:T(8,128)(2,1)S(1)}, u32[]{:S(2)}, u32[]{:S(2)}) collective-permute-start(bf16[256,2048]{1,0:T(8,128)(2,1)S(1)} %pad_maximum_fusion.6), channel_id=1, source_target_pairs={{0,4},{2,6},{4,0},{6,2},{1,5},{3,7},{5,1},{7,3},{8,12},{10,14},{12... | collective-permute-start | bytes 3145736 | tf_op jit(solution)/shard_map/ppermute | solution.py:38
  448.5 40.4 %collective-permute-start.39 = (bf16[2048,1024]{1,0:T(8,128)(2,1)S(1)}, bf16[2048,1024]{1,0:T(8,128)(2,1)}, u32[]{:S(2)}, u32[]{:S(2)}) collective-permute-start(bf16[2048,1024]{1,0:T(8,128)(2,1)S(1)} %copy-done.80), channel_id=1, source_target_pairs={{0,1},{1,0},{2,3},{3,2},{4,5},{5,4},{6,7},{7,6},{8,9},{9,8},{10,11... | collective-permute-start | bytes 12582920 | tf_op jit(solution)/shard_map/ppermute | solution.py:34
  457.7 102.3 %collective-permute-start.40 = (bf16[2048,1024]{1,0:T(8,128)(2,1)}, bf16[2048,1024]{1,0:T(8,128)(2,1)}, u32[]{:S(2)}, u32[]{:S(2)}) collective-permute-start(bf16[2048,1024]{1,0:T(8,128)(2,1)} %convolution_convert_fusion), channel_id=1, source_target_pairs={{0,1},{1,0},{2,3},{3,2},{4,5},{5,4},{6,7},{7,6},{8,9},{9,8},{10,11... | collective-permute-start | bytes 12582920 | tf_op jit(solution)/shard_map/ppermute | solution.py:34
  487.2 18.1 %collective-permute-start.29 = (bf16[256,2048]{1,0:T(8,128)(2,1)}, bf16[256,2048]{1,0:T(8,128)(2,1)S(1)}, u32[]{:S(2)}, u32[]{:S(2)}) collective-permute-start(bf16[256,2048]{1,0:T(8,128)(2,1)} %get-tuple-element.180), channel_id=1, source_target_pairs={{0,2},{2,0},{4,6},{6,4},{1,3},{3,1},{5,7},{7,5},{8,10},{10,8},{12,... | collective-permute-start | bytes 3145736 | tf_op jit(solution)/shard_map/ppermute | solution.py:38
  488.3 19.6 %collective-permute-start.30 = (bf16[256,2048]{1,0:T(8,128)(2,1)}, bf16[256,2048]{1,0:T(8,128)(2,1)S(1)}, u32[]{:S(2)}, u32[]{:S(2)}) collective-permute-start(bf16[256,2048]{1,0:T(8,128)(2,1)} %get-tuple-element.180), channel_id=1, source_target_pairs={{0,4},{2,6},{4,0},{6,2},{1,5},{3,7},{5,1},{7,3},{8,12},{10,14},{12... | collective-permute-start | bytes 3145736 | tf_op jit(solution)/shard_map/ppermute | solution.py:38
  488.9 20.4 %collective-permute-start.20 = (bf16[256,2048]{1,0:T(8,128)(2,1)}, bf16[256,2048]{1,0:T(8,128)(2,1)}, u32[]{:S(2)}, u32[]{:S(2)}) collective-permute-start(bf16[256,2048]{1,0:T(8,128)(2,1)} %get-tuple-element.221), channel_id=1, source_target_pairs={{0,1},{1,0},{2,3},{3,2},{4,5},{5,4},{6,7},{7,6},{8,9},{9,8},{10,11... | collective-permute-start | bytes 3145736 | tf_op jit(solution)/shard_map/ppermute | solution.py:34
  496.8 170.6 %reduce-scatter.8.cloned.1.call-start = ((), (), s32[]{:S(2)}) async-start(), calls=%async_computation.20 | async-start | bytes 5242880 | tf_op jit(solution)/shard_map/reduce_scatter | solution.py:414
  569.9 208.0 %reduce-scatter.4.cloned.1.call-start = ((), (), s32[]{:S(2)}) async-start(), calls=%async_computation.18 | async-start | bytes 5242880 | tf_op jit(solution)/shard_map/reduce_scatter | solution.py:414
  571.3 61.6 %collective-permute-start.33 = (bf16[256,2048]{1,0:T(8,128)(2,1)S(1)}, bf16[256,2048]{1,0:T(8,128)(2,1)S(1)}, u32[]{:S(2)}, u32[]{:S(2)}) collective-permute-start(bf16[256,2048]{1,0:T(8,128)(2,1)S(1)} %pad_maximum_fusion.7), channel_id=1, source_target_pairs={{0,2},{2,0},{4,6},{6,4},{1,3},{3,1},{5,7},{7,5},{8,10},{10,8},{12,... | collective-permute-start | bytes 3145736 | tf_op jit(solution)/shard_map/ppermute | solution.py:38
  583.6 69.3 %collective-permute-start.38 = (bf16[2048,1024]{0,1:T(8,128)(2,1)}, bf16[2048,1024]{0,1:T(8,128)(2,1)}, u32[]{:S(2)}, u32[]{:S(2)}) collective-permute-start(bf16[2048,1024]{0,1:T(8,128)(2,1)} %pad_maximum_fusion), channel_id=1, source_target_pairs={{0,1},{1,0},{2,3},{3,2},{4,5},{5,4},{6,7},{7,6},{8,9},{9,8},{10,11... | collective-permute-start | bytes 12582920 | tf_op jit(solution)/shard_map/ppermute | solution.py:34
  584.9 48.3 %collective-permute-start.35 = (bf16[256,2048]{1,0:T(8,128)(2,1)S(1)}, bf16[256,2048]{1,0:T(8,128)(2,1)S(1)}, u32[]{:S(2)}, u32[]{:S(2)}) collective-permute-start(bf16[256,2048]{1,0:T(8,128)(2,1)S(1)} %pad_maximum_fusion.8), channel_id=1, source_target_pairs={{0,4},{2,6},{4,0},{6,2},{1,5},{3,7},{5,1},{7,3},{8,12},{10,14},{12... | collective-permute-start | bytes 3145736 | tf_op jit(solution)/shard_map/ppermute | solution.py:38
  593.4 18.7 %collective-permute-start.43 = (f32[24576]{0:T(1024)S(1)}, f32[24576]{0:T(1024)S(1)}, u32[]{:S(2)}, u32[]{:S(2)}) collective-permute-start(f32[24576]{0:T(1024)S(1)} %add.438), channel_id=1, source_target_pairs={{0,4},{2,6},{4,0},{6,2},{1,5},{3,7},{5,1},{7,3},{8,12},{10,14},{12... | collective-permute-start | bytes 294920 | tf_op jit(solution)/shard_map/ppermute | solution.py:38
  652.8 30.2 %collective-permute-start.37 = (f32[256,2048]{1,0:T(8,128)S(1)}, f32[256,2048]{1,0:T(8,128)}, u32[]{:S(2)}, u32[]{:S(2)}) collective-permute-start(f32[256,2048]{1,0:T(8,128)S(1)} %maximum_add_fusion.4), channel_id=1, source_target_pairs={{0,1},{1,0},{2,3},{3,2},{4,5},{5,4},{6,7},{7,6},{8,9},{9,8},{10,11... | collective-permute-start | bytes 6291464 | tf_op jit(solution)/shard_map/ppermute | solution.py:34
  661.9 16.8 %all-to-all-start.4 = ((bf16[4,128,1024]{2,1,0:T(8,128)(2,1)}), bf16[4,128,1024]{2,1,0:T(8,128)(2,1)S(1)}, u32[]{:S(2)}, u32[]{:S(2)}) async-start(bf16[4,128,1024]{2,1,0:T(8,128)(2,1)} %bitcast.346), calls=%async_computation.6 | async-start | bytes 2097152 | tf_op jit(solution)/shard_map/all_to_all | solution.py:283
  678.7 17.5 %all-to-all-start.5 = ((bf16[4,128,1024]{2,1,0:T(8,128)(2,1)}), bf16[4,128,1024]{2,1,0:T(8,128)(2,1)}, u32[]{:S(2)}, u32[]{:S(2)}) async-start(bf16[4,128,1024]{2,1,0:T(8,128)(2,1)} %bitcast.347), calls=%async_computation.8 | async-start | bytes 2097152 | tf_op jit(solution)/shard_map/all_to_all | solution.py:283
  724.7 18.4 %all-to-all-start.10 = ((bf16[4,128,1024]{1,2,0:T(8,128)(2,1)}), bf16[4,128,1024]{1,2,0:T(8,128)(2,1)}, u32[]{:S(2)}, u32[]{:S(2)}) async-start(bf16[4,128,1024]{1,2,0:T(8,128)(2,1)} %bitcast.99), calls=%async_computation.13 | async-start | bytes 2097152 | tf_op jit(solution)/shard_map/all_to_all | solution.py:283
  738.7 18.9 %collective-permute-start.54 = (f32[2,128,128]{2,1,0:T(8,128)}, f32[2,128,128]{2,1,0:T(8,128)S(1)}, u32[]{:S(2)}, u32[]{:S(2)}) collective-permute-start(f32[2,128,128]{2,1,0:T(8,128)} %get-tuple-element.242), channel_id=1, source_target_pairs={{0,24},{8,16},{16,8},{24,0},{1,25},{9,17},{17,9},{25,1},{2,26},{10... | collective-permute-start | bytes 393224 | tf_op jit(solution)/shard_map/ppermute | solution.py:42
  763.8 20.9 %collective-permute-start.55 = (f32[2,128,128]{2,1,0:T(8,128)S(1)}, f32[2,128,128]{2,1,0:T(8,128)}, u32[]{:S(2)}, u32[]{:S(2)}) collective-permute-start(f32[2,128,128]{2,1,0:T(8,128)S(1)} %polynomials.4), channel_id=1, source_target_pairs={{0,8},{8,0},{16,24},{24,16},{1,9},{9,1},{17,25},{25,17},{2,10},{10... | collective-permute-start | bytes 393224 | tf_op jit(solution)/shard_map/ppermute | solution.py:42
  764.8 24.3 %collective-permute-start.56 = (f32[2,128,128]{2,1,0:T(8,128)S(1)}, f32[2,128,128]{2,1,0:T(8,128)}, u32[]{:S(2)}, u32[]{:S(2)}) collective-permute-start(f32[2,128,128]{2,1,0:T(8,128)S(1)} %polynomials.4), channel_id=1, source_target_pairs={{0,16},{8,24},{16,0},{24,8},{1,17},{9,25},{17,1},{25,9},{2,18},{10... | collective-permute-start | bytes 393224 | tf_op jit(solution)/shard_map/ppermute | solution.py:42
  767.7 22.9 %collective-permute-start.57 = (f32[2,128,128]{2,1,0:T(8,128)S(1)}, f32[2,128,128]{2,1,0:T(8,128)}, u32[]{:S(2)}, u32[]{:S(2)}) collective-permute-start(f32[2,128,128]{2,1,0:T(8,128)S(1)} %polynomials.4), channel_id=1, source_target_pairs={{0,24},{8,16},{16,8},{24,0},{1,25},{9,17},{17,9},{25,1},{2,26},{10... | collective-permute-start | bytes 393224 | tf_op jit(solution)/shard_map/ppermute | solution.py:42
  774.6 48.0 %collective-permute-start.61 = (f32[2,128,128]{2,1,0:T(8,128)S(1)}, f32[2,128,128]{2,1,0:T(8,128)}, u32[]{:S(2)}, u32[]{:S(2)}) collective-permute-start(f32[2,128,128]{2,1,0:T(8,128)S(1)} %polynomials.5), channel_id=1, source_target_pairs={{0,8},{8,0},{16,24},{24,16},{1,9},{9,1},{17,25},{25,17},{2,10},{10... | collective-permute-start | bytes 393224 | tf_op jit(solution)/shard_map/ppermute | solution.py:42
  774.7 48.9 %collective-permute-start.62 = (f32[2,128,128]{2,1,0:T(8,128)S(1)}, f32[2,128,128]{2,1,0:T(8,128)S(1)}, u32[]{:S(2)}, u32[]{:S(2)}) collective-permute-start(f32[2,128,128]{2,1,0:T(8,128)S(1)} %polynomials.5), channel_id=1, source_target_pairs={{0,16},{8,24},{16,0},{24,8},{1,17},{9,25},{17,1},{25,9},{2,18},{10... | collective-permute-start | bytes 393224 | tf_op jit(solution)/shard_map/ppermute | solution.py:42
  784.7 39.1 %collective-permute-start.63 = (f32[2,128,128]{2,1,0:T(8,128)S(1)}, f32[2,128,128]{2,1,0:T(8,128)}, u32[]{:S(2)}, u32[]{:S(2)}) collective-permute-start(f32[2,128,128]{2,1,0:T(8,128)S(1)} %polynomials.5), channel_id=1, source_target_pairs={{0,24},{8,16},{16,8},{24,0},{1,25},{9,17},{17,9},{25,1},{2,26},{10... | collective-permute-start | bytes 393224 | tf_op jit(solution)/shard_map/ppermute | solution.py:42
  827.9 23.6 %all-to-all-start.9 = ((bf16[4,128,1024]{1,2,0:T(8,128)(2,1)}), bf16[4,128,1024]{1,2,0:T(8,128)(2,1)S(1)}, u32[]{:S(2)}, u32[]{:S(2)}) async-start(bf16[4,128,1024]{1,2,0:T(8,128)(2,1)} %copy.177), calls=%async_computation.12 | async-start | bytes 2097152 | tf_op jit(solution)/shard_map/all_to_all | solution.py:283
  837.0 29.3 %collective-permute-start.48 = (f32[2,128,128]{2,1,0:T(8,128)}, f32[2,128,128]{2,1,0:T(8,128)S(1)}, u32[]{:S(2)}, u32[]{:S(2)}) collective-permute-start(f32[2,128,128]{2,1,0:T(8,128)} %get-tuple-element.245), channel_id=1, source_target_pairs={{0,24},{8,16},{16,8},{24,0},{1,25},{9,17},{17,9},{25,1},{2,26},{10... | collective-permute-start | bytes 393224 | tf_op jit(solution)/shard_map/ppermute | solution.py:42
  843.6 22.7 %collective-permute-start.47 = (f32[2,128,128]{2,1,0:T(8,128)}, f32[2,128,128]{2,1,0:T(8,128)S(1)}, u32[]{:S(2)}, u32[]{:S(2)}) collective-permute-start(f32[2,128,128]{2,1,0:T(8,128)} %get-tuple-element.246), channel_id=1, source_target_pairs={{0,16},{8,24},{16,0},{24,8},{1,17},{9,25},{17,1},{25,9},{2,18},{10... | collective-permute-start | bytes 393224 | tf_op jit(solution)/shard_map/ppermute | solution.py:42
  843.6 22.7 %collective-permute-start.46 = (f32[2,128,128]{2,1,0:T(8,128)S(1)}, f32[2,128,128]{2,1,0:T(8,128)}, u32[]{:S(2)}, u32[]{:S(2)}) collective-permute-start(f32[2,128,128]{2,1,0:T(8,128)S(1)} %get-tuple-element.244), channel_id=1, source_target_pairs={{0,8},{8,0},{16,24},{24,16},{1,9},{9,1},{17,25},{25,17},{2,10},{10... | collective-permute-start | bytes 393224 | tf_op jit(solution)/shard_map/ppermute | solution.py:42
  852.5 37.9 %all-to-all-start.11 = ((bf16[4,128,1024]{1,2,0:T(8,128)(2,1)}), bf16[4,128,1024]{1,2,0:T(8,128)(2,1)S(1)}, u32[]{:S(2)}, u32[]{:S(2)}) async-start(bf16[4,128,1024]{1,2,0:T(8,128)(2,1)} %copy.185), calls=%async_computation.14 | async-start | bytes 2097152 | tf_op jit(solution)/shard_map/all_to_all | solution.py:283
  (117 other events, 1179.3 us)
Sparse Core Ops, SparseCore 0:
  31.0 80.4 all-gather.3
  113.7 79.2 all-gather.5
  195.1 79.2 all-gather.7
  496.9 74.7 reduce-scatter.5
  573.9 81.4 reduce-scatter.7
  660.7 76.6 reduce-scatter.3

commit v2 on v1

v2 whole, which is shorter than its diff:
```python
import math

import jax
import jax.numpy as jnp
from jax import lax
from jax.experimental import pallas as pl
from jax.experimental.pallas import tpu as pltpu
from jax.sharding import PartitionSpec as P

HDIM = 128
NS_STEPS = 5
HALF = 512

bf16 = jnp.bfloat16
f32 = jnp.float32
highest = lax.Precision.HIGHEST
norm_epsilon = 1e-05
ortho_epsilon = 1e-07
coef_first = 3.4445
coef_second = -4.775
coef_third = 2.0315
decay_rate = 0.5
matrix_rate = 0.25
masked_value = -1e30

CORE = [(0, 1), (1, 0)]


def xor_pairs(size, mask):
    return [(i, i ^ mask) for i in range(size)]


def swap_core(value):
    return lax.ppermute(value, "tp", CORE)


def swap_ctx(value, mask):
    return lax.ppermute(value, "ctx", xor_pairs(4, mask))


def swap_fsdp(value, mask):
    return lax.ppermute(value, "fsdp", xor_pairs(4, mask))


def mm(left, right, dims):
    return lax.dot_general(left, right, ((dims[:1], dims[1:]), ((), ())), preferred_element_type=f32)


def spread(own):
    if lax.axis_size("ctx") != 4:
        whole = lax.all_gather(own, "ctx", axis=0, tiled=False)
        return [whole[i] for i in range(whole.shape[0])]
    half = own.shape[0] // 2
    from_x = swap_ctx(own, 1)
    from_y = swap_ctx(own, 2)
    top = swap_ctx(from_x[:half], 2)
    low = swap_ctx(from_y[half:], 1)
    return [own, from_x, from_y, jnp.concatenate([top, low], axis=0)]


def collect(partial):
    count = lax.axis_size("ctx")
    rows = partial.shape[0] // count
    if count != 4:
        return lax.psum_scatter(partial, "ctx", scatter_dimension=0, tiled=True).astype(f32)
    half = rows // 2
    part = [partial[k * rows : (k + 1) * rows] for k in range(4)]
    over_x = swap_ctx(jnp.concatenate([part[1][:half], part[3][:half]], axis=0), 1).astype(f32)
    over_y = swap_ctx(jnp.concatenate([part[2][half:], part[3][half:]], axis=0), 2).astype(f32)
    then_y = swap_ctx((part[2][:half].astype(f32) + over_x[half:]).astype(bf16), 2)
    then_x = swap_ctx((part[1][half:].astype(f32) + over_y[half:]).astype(bf16), 1)
    own = part[0].astype(f32)
    return jnp.concatenate(
        [
            own[:half] + over_x[:half] + then_y.astype(f32),
            own[half:] + over_y[:half] + then_x.astype(f32),
        ],
        axis=0,
    )


def layer_norm(values, gain_row, shift_row):
    center = values - jnp.mean(values, axis=-1, keepdims=True)
    inverse = lax.rsqrt(jnp.mean(center * center, axis=-1, keepdims=True) + norm_epsilon)
    normed = center * inverse
    return (normed * gain_row + shift_row, normed, inverse)


def layer_norm_back(grad_upper, normed, inverse, gain_row):
    grad_normed = grad_upper * gain_row
    mean_grad = jnp.mean(grad_normed, axis=-1, keepdims=True)
    mean_dot = jnp.mean(grad_normed * normed, axis=-1, keepdims=True)
    return inverse * (grad_normed - mean_grad - normed * mean_dot)


def gelu_tanh(values):
    return jax.nn.gelu(values, approximate=True)


MESH = pl.DeviceIdType.MESH


def remote(source, target, send, receive, axis, index):
    return pltpu.make_async_remote_copy(
        src_ref=source,
        dst_ref=target,
        send_sem=send,
        recv_sem=receive,
        device_id={axis: index},
        device_id_type=MESH,
    )


def greet(axis_indices):
    barrier = pltpu.get_barrier_semaphore()
    for axis, index in axis_indices:
        pl.semaphore_signal(barrier, inc=1, device_id={axis: index}, device_id_type=MESH)
    pl.semaphore_wait(barrier, len(axis_indices))


class RowSums:
    def __init__(self, part, from_x, from_y, then_y, then_x, to_y, to_x, send, receive):
        self.part, self.send, self.receive = part, send, receive
        self.from_x, self.from_y, self.then_y, self.then_x = from_x, from_y, then_y, then_x
        self.to_y, self.to_x = to_y, to_x
        self.pieces, self.count = to_y.shape[:2]
        self.span = [pl.ds(j * self.count, self.count) for j in range(self.pieces)]
        c = lax.axis_index("ctx")
        self.x_side = c + 1 - 2 * (c % 2)
        self.y_side = c + 2 - 4 * (c // 2)
        self.one, self.two = [], []

    def copy(self, stage, j, source, target, side):
        copy = remote(source, target, self.send.at[stage, j], self.receive.at[stage, j], "ctx", side)
        copy.start()
        return copy

    def first(self):
        for j in range(self.pieces):
            self.one.append(
                (
                    self.copy(0, j, self.part.at[:, 1, 0, self.span[j]], self.from_x.at[j], self.x_side),
                    self.copy(1, j, self.part.at[1, :, 1, self.span[j]], self.from_y.at[j], self.y_side),
                )
            )

    def second(self):
        for j in range(self.pieces):
            at = self.span[j]
            self.one[j][0].wait_recv()
            value = self.part[1, 0, 0, at].astype(f32) + self.from_x[j, 1].astype(f32)
            self.to_y[j] = value.astype(bf16)
            over_y = self.copy(2, j, self.to_y.at[j], self.then_y.at[j], self.y_side)
            self.one[j][1].wait_recv()
            value = self.part[0, 1, 1, at].astype(f32) + self.from_y[j, 1].astype(f32)
            self.to_x[j] = value.astype(bf16)
            over_x = self.copy(3, j, self.to_x.at[j], self.then_x.at[j], self.x_side)
            self.two.append((over_y, over_x))

    def third(self, j):
        at = self.span[j]
        self.two[j][0].wait_recv()
        self.two[j][1].wait_recv()
        top = self.part[0, 0, 0, at].astype(f32) + self.from_x[j, 0].astype(f32)
        low = self.part[0, 0, 1, at].astype(f32) + self.from_y[j, 0].astype(f32)
        top = top + self.then_y[j].astype(f32)
        low = low + self.then_x[j].astype(f32)
        return at, jnp.concatenate([top, low], axis=0)

    def end(self):
        for pair in (*self.one, *self.two):
            for one in pair:
                one.wait_send()


def row_scratch(half, width, pieces=4):
    count = half // pieces
    return [
        pltpu.VMEM((pieces, 2, count, width), bf16),
        pltpu.VMEM((pieces, 2, count, width), bf16),
        *[pltpu.VMEM((pieces, count, width), bf16)] * 4,
        pltpu.SemaphoreType.DMA((4, pieces)),
        pltpu.SemaphoreType.DMA((4, pieces)),
    ]


def exchange_kernel(step, n_in, n_vec, n_out, n_sum, *refs):
    part = refs[0]
    ins = refs[1 : 1 + n_in]
    vectors = refs[1 + n_in : 1 + n_in + n_vec]
    rest = refs[1 + n_in + n_vec :]
    whole = rest[0]
    outs = rest[1 : 1 + n_out]
    sums_ref = rest[1 + n_out]
    own, send, receive, local = rest[2 + n_out : 6 + n_out]
    row_sums = RowSums(part, *rest[6 + n_out :])
    x_side, y_side, span, count = row_sums.x_side, row_sums.y_side, row_sums.span, row_sums.count
    greet([("ctx", x_side), ("ctx", y_side)])

    def copy(stage, j, source, target, side):
        one = remote(source, target, send.at[stage, j], receive.at[stage, j], "ctx", side)
        one.start()
        return one

    row_sums.first()
    row_sums.second()
    params = [v[...] for v in vectors]
    third, fourth, kept = [], [], []
    totals = None
    for j in range(row_sums.pieces):
        at, total = row_sums.third(j)
        both = lambda ref: jnp.concatenate([ref[0, at], ref[1, at]], axis=0)
        sent, rows, sums = step(total, [both(r) for r in ins], params)
        own[0, at] = sent[:count]
        own[1, at] = sent[count:]
        third.append(
            (
                copy(0, j, own.at[:, at], whole.at[1, :, at], x_side),
                copy(1, j, own.at[:, at], whole.at[2, :, at], y_side),
            )
        )
        keep = pltpu.make_async_copy(own.at[:, at], whole.at[0, :, at], local.at[j])
        keep.start()
        kept.append(keep)
        for out, value in zip(outs, rows):
            out[0, at] = value[:count]
            out[1, at] = value[count:]
        totals = sums if totals is None else [a + b for a, b in zip(totals, sums)]
    for k in range(n_sum):
        sums_ref[k : k + 1] = totals[k]
    for j, at in enumerate(span):
        third[j][0].wait_recv()
        over_y = copy(2, j, whole.at[1, 0, at], whole.at[3, 0, at], y_side)
        third[j][1].wait_recv()
        over_x = copy(3, j, whole.at[2, 1, at], whole.at[3, 1, at], x_side)
        fourth.append((over_y, over_x))
    row_sums.end()
    for pair in third:
        for one in pair:
            one.wait_send()
    for pair in fourth:
        for one in pair:
            one.wait()
    for one in kept:
        one.wait()


def exchange(name, number, step, part, ins, vectors, out_types, n_sum):
    rows, width = ins[0].shape
    if lax.axis_size("ctx") != 4 or rows % 128:
        sent, outs, sums = step(collect(part), ins, vectors)
        return jnp.concatenate(spread(sent), axis=0), outs, sums
    pieces = 4
    half = rows // 2
    vmem = pl.BlockSpec(memory_space=pltpu.VMEM)
    halves = lambda v: v.reshape(2, half, width)
    whole, *outs, sums = pl.pallas_call(
        lambda *refs: exchange_kernel(step, len(ins), len(vectors), len(out_types), n_sum, *refs),
        out_shape=[
            jax.ShapeDtypeStruct((4, 2, half, width), bf16),
            *[jax.ShapeDtypeStruct((2, half, width), d) for d in out_types],
            jax.ShapeDtypeStruct((8, width), f32),
        ],
        in_specs=[vmem] * (1 + len(ins) + len(vectors)),
        out_specs=[pl.BlockSpec(memory_space=pl.ANY), *[vmem] * (len(out_types) + 1)],
        scratch_shapes=[
            pltpu.VMEM((2, half, width), bf16),
            pltpu.SemaphoreType.DMA((4, pieces)),
            pltpu.SemaphoreType.DMA((4, pieces)),
            pltpu.SemaphoreType.DMA((pieces,)),
            *row_scratch(half, width, pieces),
        ],
        compiler_params=pltpu.CompilerParams(
            collective_id=number, has_side_effects=True, vmem_limit_bytes=36 << 20
        ),
        cost_estimate=pl.CostEstimate(
            flops=60 * rows * width, bytes_accessed=130 << 20, transcendentals=0
        ),
        name=name,
    )(part.reshape(2, 2, 2, half, width), *map(halves, ins), *vectors)
    return (
        whole.reshape(4 * rows, width),
        [o.reshape(rows, width) for o in outs],
        [sums[k : k + 1] for k in range(n_sum)],
    )


def column_sum(values):
    return jnp.sum(values, axis=0, keepdims=True)


def first_step(total, rows, vectors):
    bias, gain, shift = vectors
    first, unit, inverse = layer_norm(rows[0].astype(f32) + total + bias, gain, shift)
    return first.astype(bf16), [unit, jnp.broadcast_to(inverse, unit.shape)], []


def second_step(total, rows, vectors):
    bias, gain_one, shift_one, gain, shift = vectors
    first = rows[0] * gain_one + shift_one
    out, unit, inverse = layer_norm(first + total + bias, gain, shift)
    upper = rows[1].astype(f32)
    grad = layer_norm_back(upper, unit, inverse, gain)
    low = grad.astype(bf16)
    sums = [column_sum(upper * unit), column_sum(upper), column_sum(low.astype(f32))]
    return low, [out.astype(bf16), grad], sums


def third_step(total, rows, vectors):
    (gain,) = vectors
    unit, inverse, upper = rows
    upper = upper + total
    grad = layer_norm_back(upper, unit, inverse, gain)
    low = grad.astype(bf16)
    sums = [column_sum(upper * unit), column_sum(upper), column_sum(low.astype(f32))]
    return low, [grad], sums


def block_weights(query, keys, place_rows, place_cols):
    scores = mm(query, keys, (1, 1))
    scores = jnp.where(jnp.abs(place_rows - place_cols) <= HALF, scores, masked_value)
    top = jnp.max(scores, axis=-1, keepdims=True)
    weights = jnp.exp((scores - top) * HDIM**-0.5)
    return weights, 1.0 / jnp.sum(weights, axis=-1, keepdims=True)


def attend_kernel(block, q_ref, k_ref, v_ref, rows_ref, cols_ref, out_ref):
    for start in range(0, q_ref.shape[0], block):
        span = pl.ds(start, block)
        weights, inverse = block_weights(q_ref[span, :], k_ref[...], rows_ref[span, :], cols_ref[...])
        out_ref[span, :] = (mm(weights.astype(bf16), v_ref[...], (1, 0)) * inverse).astype(bf16)


def attend_forward(qkv, place):
    length = qkv.shape[0]
    heads = qkv.shape[1] // (3 * HDIM)
    piece = lambda which: pl.BlockSpec((length, HDIM), lambda h, w=which: (0, w * heads + h))
    return pl.pallas_call(
        lambda *refs: attend_kernel(256, *refs),
        out_shape=jax.ShapeDtypeStruct((length, heads * HDIM), bf16),
        grid=(heads,),
        in_specs=[
            piece(0),
            piece(1),
            piece(2),
            pl.BlockSpec((length, 1), lambda h: (0, 0)),
            pl.BlockSpec((1, length), lambda h: (0, 0)),
        ],
        out_specs=pl.BlockSpec((length, HDIM), lambda h: (0, h)),
        compiler_params=pltpu.CompilerParams(vmem_limit_bytes=40 << 20),
        cost_estimate=pl.CostEstimate(
            flops=4 * heads * length * length * HDIM,
            bytes_accessed=8 * heads * length * HDIM,
            transcendentals=heads * length * length,
        ),
        name="attend_forward",
    )(qkv, qkv, qkv, place[:, None], place[None, :])


def attend_back_kernel(
    block, heads, q_ref, k_ref, v_ref, up_ref, rows_ref, cols_ref, out_ref, sum_k, sum_v
):
    scale = HDIM**-0.5
    head = pl.program_id(0)
    column = lambda which: pl.ds(pl.multiple_of((which * heads + head) * HDIM, HDIM), HDIM)
    for start in range(0, q_ref.shape[0], block):
        span = pl.ds(start, block)
        query = q_ref[span, :]
        upper = up_ref[span, :]
        weights, inverse = block_weights(query, k_ref[...], rows_ref[span, :], cols_ref[...])
        probs = weights * inverse
        grad_probs = mm(upper, v_ref[...], (1, 1))
        inner = jnp.sum(probs * grad_probs, axis=-1, keepdims=True)
        grad_scores = (probs * (grad_probs - inner)).astype(bf16)
        out_ref[span, column(0)] = (mm(grad_scores, k_ref[...], (1, 0)) * scale).astype(bf16)
        add_k = mm(grad_scores, query, (0, 0))
        add_v = mm(probs.astype(bf16), upper, (0, 0))
        if start == 0:
            sum_k[...] = add_k
            sum_v[...] = add_v
        else:
            sum_k[...] += add_k
            sum_v[...] += add_v
    out_ref[:, column(1)] = (sum_k[...] * scale).astype(bf16)
    out_ref[:, column(2)] = sum_v[...].astype(bf16)


def attend_backward(qkv, upper, place):
    length = qkv.shape[0]
    heads = qkv.shape[1] // (3 * HDIM)
    piece = lambda which: pl.BlockSpec((length, HDIM), lambda h, w=which: (0, w * heads + h))
    return pl.pallas_call(
        lambda *refs: attend_back_kernel(256, heads, *refs),
        out_shape=jax.ShapeDtypeStruct(qkv.shape, bf16),
        grid=(heads,),
        in_specs=[
            piece(0),
            piece(1),
            piece(2),
            piece(0),
            pl.BlockSpec((length, 1), lambda h: (0, 0)),
            pl.BlockSpec((1, length), lambda h: (0, 0)),
        ],
        out_specs=pl.BlockSpec(qkv.shape, lambda h: (0, 0)),
        scratch_shapes=[pltpu.VMEM((length, HDIM), f32), pltpu.VMEM((length, HDIM), f32)],
        compiler_params=pltpu.CompilerParams(vmem_limit_bytes=48 << 20),
        cost_estimate=pl.CostEstimate(
            flops=10 * heads * length * length * HDIM,
            bytes_accessed=14 * heads * length * HDIM,
            transcendentals=heads * length * length,
        ),
        name="attend_backward",
    )(qkv, qkv, qkv, upper, place[:, None], place[None, :])


def gram_of(moment_ref, total_ref, n):
    span = pl.ds(n * HDIM, HDIM)
    state = decay_rate * moment_ref[:, span].astype(f32) + total_ref[:, span].astype(f32)
    return lax.dot_general(
        state, state, (((0,), (0,)), ((), ())), precision=highest, preferred_element_type=f32
    )


def gram_kernel(moment_ref, total_ref, out_ref):
    for n in range(out_ref.shape[0]):
        out_ref[n] = gram_of(moment_ref, total_ref, n)


def apply_kernel(moment_ref, total_ref, factor_ref, out_ref):
    for n in range(factor_ref.shape[0]):
        span = pl.ds(n * HDIM, HDIM)
        state = decay_rate * moment_ref[:, span].astype(f32) + total_ref[:, span].astype(f32)
        out_ref[:, span] = jnp.dot(
            state, factor_ref[n], precision=highest, preferred_element_type=f32
        ).astype(bf16)


def whole_call(kernel, name, out, *operands, flops):
    vmem = pl.BlockSpec(memory_space=pltpu.VMEM)
    return pl.pallas_call(
        kernel,
        out_shape=out,
        in_specs=[vmem] * len(operands),
        out_specs=vmem,
        compiler_params=pltpu.CompilerParams(vmem_limit_bytes=32 << 20),
        cost_estimate=pl.CostEstimate(
            flops=flops, bytes_accessed=sum(o.size * o.dtype.itemsize for o in operands), transcendentals=0
        ),
        name=name,
    )(*operands)


def polynomial(grams):
    width = grams[0].shape[0]
    same = lax.broadcasted_iota(jnp.int32, (width, width), 0) == lax.broadcasted_iota(
        jnp.int32, (width, width), 1
    )
    unit = same.astype(f32)
    dot = lambda a, b: jnp.dot(a, b, precision=highest, preferred_element_type=f32)
    scaled, totals = [], []
    for gram in grams:
        square = jnp.sum(jnp.sum(gram * unit, axis=1, keepdims=True), axis=0, keepdims=True)
        inverse = 1.0 / (jnp.sqrt(square) + ortho_epsilon)
        scaled.append(gram * (inverse * inverse))
        totals.append(unit * inverse)
    for step in range(NS_STEPS):
        squares = [dot(g, g) for g in scaled]
        polys = [
            coef_first * unit + coef_second * g + coef_third * s for g, s in zip(scaled, squares)
        ]
        totals = [dot(q, p) for q, p in zip(totals, polys)]
        if step + 1 < NS_STEPS:
            halves = [dot(g, p) for g, p in zip(scaled, polys)]
            scaled = [dot(p, h) for p, h in zip(polys, halves)]
    return totals


def polynomial_kernel(gram_ref, out_ref):
    for n, total in enumerate(polynomial([gram_ref[n] for n in range(gram_ref.shape[0])])):
        out_ref[n] = total


def slab_kernel(groups, with_rows, *refs):
    moments, totals, refs = refs[:groups], refs[groups : 2 * groups], refs[2 * groups :]
    if with_rows:
        part, base, vector, refs = refs[0], refs[1], refs[2], refs[3:]
    grads, orthos, refs = refs[:groups], refs[groups : 2 * groups], refs[2 * groups :]
    if with_rows:
        summed, vector_out, refs = refs[0], refs[1], refs[2:]
    grams, pieces, factors, stage, send_c, receive_c, send_f, receive_f, local = refs[:9]
    rows = totals[0].shape[0] // 4
    each_group = totals[0].shape[1] // HDIM
    count = grams.shape[0]
    c = lax.axis_index("ctx")
    f = lax.axis_index("fsdp")
    sides = [(c + i) % 4 for i in range(4)]
    planes = [(f + i) % 4 for i in range(4)]
    peers = [("ctx", sides[i]) for i in (1, 2, 3)] + [("fsdp", planes[i]) for i in (1, 2, 3)]
    if with_rows:
        t = lax.axis_index("tp")
        partners = [
            ("tp", 1 - t),
            ("ctx", c + 1 - 2 * (c % 2)),
            ("ctx", c + 2 - 4 * (c // 2)),
            ("fsdp", f + 1 - 2 * (f % 2)),
            ("fsdp", f + 2 - 4 * (f // 2)),
        ]
        peers.append(partners[0])
        sent_v, got_v, send_v, receive_v = refs[9:13]
        sent_v[0] = vector[...]
    greet(peers)

    def vector_start(k):
        one = remote(sent_v.at[k], got_v.at[k], send_v.at[k], receive_v.at[k], *partners[k])
        one.start()
        vector_copies.append(one)

    def vector_next(k):
        if not with_rows:
            return
        vector_copies[k].wait_recv()
        if k < 4:
            sent_v[k + 1] = sent_v[k] + got_v[k]
            vector_start(k + 1)
        else:
            vector_out[...] = sent_v[k] + got_v[k]
            for one in vector_copies:
                one.wait_send()

    vector_copies = []
    place = lambda index: pl.ds(pl.multiple_of(index * rows, rows), rows)
    started = []

    def begin(copy):
        copy.start()
        started.append(copy)

    def to_side(source, target, kind, i):
        begin(
            remote(
                source, target, send_c.at[kind, i - 1], receive_c.at[kind, i - 1], "ctx", sides[i]
            )
        )

    if with_rows:
        vector_start(0)
        sum_rows = RowSums(part, *refs[13:])
        sum_rows.first()
    for g in range(groups):
        for i in (3, 1, 2):
            to_side(totals[g].at[place(sides[i])], grads[g].at[c], g, i)
        begin(pltpu.make_async_copy(totals[g].at[place(c)], grads[g].at[c], local.at[0, g]))

    size = min(each_group, count // 2)
    batches = range(count // size)
    each = size // 4

    def to_planes(kind, b, source, target):
        copies = []
        for i in (1, 2, 3):
            sems = send_f.at[2 * b + kind, i - 1], receive_f.at[2 * b + kind, i - 1]
            one = remote(source(i), target(i), *sems, "fsdp", planes[i])
            one.start()
            copies.append(one)
        return copies

    summing, sharing = [], []
    for b in batches:
        first = b * size
        for n in range(first, first + size):
            g = n // each_group
            grams[n] = gram_of(moments[g], totals[g], n % each_group)
        summing.append(
            to_planes(
                0,
                b,
                lambda i: grams.at[pl.ds(first + planes[i] * each, each)],
                lambda i: pieces.at[i - 1, pl.ds(b * each, each)],
            )
        )
    vector_next(0)
    if with_rows:
        sum_rows.second()
    for b in batches:
        own = b * size + f * each
        sums = [grams[own + n] for n in range(each)]
        for i in (1, 2, 3):
            summing[b][i - 1].wait()
            sums = [s + pieces[i - 1, b * each + n] for n, s in enumerate(sums)]
        for n, total in enumerate(polynomial(sums)):
            factors[own + n] = total
        part_of = lambda i: factors.at[pl.ds(own, each)]
        sharing.append(to_planes(1, b, part_of, part_of))
        vector_next(1 + b)
    if with_rows:
        for j in range(sum_rows.pieces):
            span, total = sum_rows.third(j)
            for h in range(2):
                value = total[h * sum_rows.count : (h + 1) * sum_rows.count]
                summed[h, span] = base[h, span] + value
    vector_next(3)
    for b in batches:
        for one in sharing[b]:
            one.wait()
        g, first = b * size // each_group, b * size % each_group
        wide = pl.ds(first * HDIM, size * HDIM)
        for i in (3, 1, 2, 0):
            span = place(sides[i])
            for n in range(first, first + size):
                column = pl.ds(n * HDIM, HDIM)
                state = decay_rate * moments[g][span, column].astype(f32)
                state = state + totals[g][span, column].astype(f32)
                stage[g, i, :, column] = jnp.dot(
                    state, factors[g * each_group + n], precision=highest, preferred_element_type=f32
                ).astype(bf16)
            source, target = stage.at[g, i, :, wide], orthos[g].at[c, :, wide]
            if i:
                to_side(source, target, groups + b, i)
            else:
                begin(pltpu.make_async_copy(source, target, local.at[1, b]))
    vector_next(4)
    for one in started:
        one.wait()
    if with_rows:
        sum_rows.end()


def gradients_and_orthogonal(name, number, moments, totals, part=None, base=None, vector=None):
    rows, columns = totals[0].shape
    groups = len(totals)
    count = groups * columns // HDIM
    flops = 2 * 6 * rows * columns * HDIM * groups
    vmem = pl.BlockSpec(memory_space=pltpu.VMEM)
    with_rows = part is not None
    if lax.axis_size("fsdp") == 4 and lax.axis_size("ctx") == 4 and count in (8, 16) and groups == count // 8:
        blocks = jax.ShapeDtypeStruct((4, rows // 4, columns), bf16)
        anywhere = pl.BlockSpec(memory_space=pl.ANY)
        out_shape, out_specs = [blocks] * (2 * groups), [anywhere] * (2 * groups)
        operands, more = [*moments, *totals], []
        if with_rows:
            height, width = base.shape
            half = height // 2
            lines = vector.size // HDIM
            operands += [part.reshape(2, 2, 2, half, width), base.reshape(2, half, width)]
            operands.append(vector.reshape(lines, HDIM))
            out_shape.append(jax.ShapeDtypeStruct((2, half, width), f32))
            out_shape.append(jax.ShapeDtypeStruct((lines, HDIM), f32))
            out_specs += [vmem, vmem]
            more = [
                pltpu.VMEM((5, lines, HDIM), f32),
                pltpu.VMEM((5, lines, HDIM), f32),
                pltpu.SemaphoreType.DMA((5,)),
                pltpu.SemaphoreType.DMA((5,)),
                *row_scratch(half, width),
            ]
        outs = pl.pallas_call(
            lambda *refs: slab_kernel(groups, with_rows, *refs),
            out_shape=out_shape,
            in_specs=[vmem] * len(operands),
            out_specs=out_specs,
            scratch_shapes=[
                pltpu.VMEM((count, HDIM, HDIM), f32),
                pltpu.VMEM((3, count // 4, HDIM, HDIM), f32),
                pltpu.VMEM((count, HDIM, HDIM), f32),
                pltpu.VMEM((groups, 4, rows // 4, columns), bf16),
                pltpu.SemaphoreType.DMA((groups + 2, 3)),
                pltpu.SemaphoreType.DMA((groups + 2, 3)),
                pltpu.SemaphoreType.DMA((4, 3)),
                pltpu.SemaphoreType.DMA((4, 3)),
                pltpu.SemaphoreType.DMA((2, 2)),
                *more,
            ],
            compiler_params=pltpu.CompilerParams(
                collective_id=number, has_side_effects=True, vmem_limit_bytes=40 << 20
            ),
            cost_estimate=pl.CostEstimate(
                flops=3 * flops, bytes_accessed=100 << 20, transcendentals=0
            ),
            name=name,
        )(*operands)
        pairs = [(outs[g], outs[groups + g]) for g in range(groups)]
        if with_rows:
            return pairs, outs[-2].reshape(base.shape), outs[-1].reshape(vector.shape)
        return pairs, None, None
    pairs = []
    shape = jax.ShapeDtypeStruct((count // groups, HDIM, HDIM), f32)
    for moment, total in zip(moments, totals):
        grams = whole_call(gram_kernel, "grams", shape, moment, total, flops=flops)
        full = whole_call(
            polynomial_kernel, "polynomials", shape, lax.psum(grams, "fsdp"), flops=flops
        )
        own = jax.ShapeDtypeStruct((rows, columns), bf16)
        ortho = whole_call(apply_kernel, "apply", own, moment, total, full, flops=flops)
        pairs.append((from_blocks(total), from_blocks(ortho)))
    if with_rows:
        return pairs, base + collect(part), lax.psum(vector, ("fsdp", "ctx", "tp"))
    return pairs, None, None


def pack(matrices):
    qkv, out, up, down = matrices
    count = lax.axis_size("ctx")
    rows = up.shape[0]
    low = lambda v: v.astype(bf16)
    four = jnp.concatenate([low(qkv), low(out).T[None]], axis=0)
    attn = four.reshape(4, rows, count, -1).transpose(2, 1, 0, 3).reshape(count, rows, -1)
    up_cut = low(up).reshape(rows, count, -1).transpose(1, 0, 2)
    down_cut = low(down).T.reshape(rows, count, -1).transpose(1, 0, 2)
    return attn, up_cut, down_cut


def finish(name, scale, grads, orthos, moments, weights):
    count, rows, columns = grads.shape
    three = [len(s.shape) == 3 for s in weights]
    tall = [len(s.shape) == 2 and s.shape[0] != rows for s in weights]
    number = len(weights)
    wide = columns // 4 if any(three) else columns
    specs = []
    for is_three, is_tall in zip(three, tall):
        if is_three:
            specs.append(pl.BlockSpec((3, rows, wide), lambda i: (0, 0, i)))
        elif is_tall:
            specs.append(pl.BlockSpec((wide, rows), lambda i: (i, 0)))
        else:
            specs.append(pl.BlockSpec((rows, wide), lambda i: (0, i)))

    def kernel(grad_ref, ortho_ref, *refs):
        for j in range(number):
            moment, weight = refs[j], refs[number + j]
            grad_out, state_out, master_out = refs[2 * number + 3 * j : 2 * number + 3 * j + 3]
            for w in range(3) if three[j] else (None,):
                start = (3 if w is None and any(three) else w or 0) * wide
                cut = lambda ref: ref[0, :, start : start + wide].astype(f32)
                grad, ortho = cut(grad_ref), cut(ortho_ref)
                if tall[j]:
                    grad, ortho = grad.T, ortho.T
                at = ... if w is None else w
                grad_out[at] = grad
                state_out[at] = decay_rate * moment[at] + grad
                master_out[at] = weight[at] - scale * ortho

    outs = pl.pallas_call(
        kernel,
        out_shape=[jax.ShapeDtypeStruct(s.shape, f32) for s in weights for _ in range(3)],
        grid=(count,),
        in_specs=[*[pl.BlockSpec((1, rows, columns), lambda i: (i, 0, 0))] * 2, *specs, *specs],
        out_specs=[spec for spec in specs for _ in range(3)],
        compiler_params=pltpu.CompilerParams(vmem_limit_bytes=32 << 20),
        cost_estimate=pl.CostEstimate(
            flops=4 * grads.size, bytes_accessed=24 * grads.size, transcendentals=0
        ),
        name=name,
    )(grads, orthos, *moments, *weights)
    return outs[0::3], outs[1::3], outs[2::3]


def over_ctx(stack):
    return lax.all_to_all(stack, "ctx", split_axis=0, concat_axis=0, tiled=True)


def to_blocks(stack):
    moved = over_ctx(stack)
    return moved.reshape(-1, moved.shape[-1])


def from_blocks(block):
    return over_ctx(block.reshape(lax.axis_size("ctx"), -1, block.shape[-1]))


def body(
    inputs,
    segment_ids,
    cotangent,
    w_qkv,
    w_out,
    w_up,
    w_down,
    bias_qv,
    bias_up,
    bias_res,
    norm_gain,
    norm_shift,
    moment_qkv,
    moment_out,
    moment_up,
    moment_down,
    moment_bqv,
    moment_bup,
    moment_bres,
    moment_gain,
    moment_shift,
):
    count_c = lax.axis_size("ctx")
    count_f = lax.axis_size("fsdp")
    c = lax.axis_index("ctx")
    t = lax.axis_index("tp")
    rows = inputs.shape[2]
    width = inputs.shape[3]
    length = rows * count_c
    token_total = inputs.shape[0] * inputs.shape[1] * count_f * length
    e = w_qkv.shape[2] // count_c
    u = w_up.shape[1] // count_c

    own_micro = lambda v: lax.dynamic_index_in_dim(v, t, 0, keepdims=False)[0]
    row_low = own_micro(inputs)
    upper = own_micro(cotangent)
    segments = own_micro(segment_ids)
    index = jnp.arange(count_c)
    order = index ^ c if count_c == 4 else index
    place = (segments * (length + HALF + 1) + jnp.arange(length, dtype=jnp.int32)).reshape(count_c, rows)
    place = jnp.take(place, order, axis=0).reshape(length)

    after = lambda value, *others: lax.optimization_barrier((value, *others))[0]
    attn_stack, up_stack, down_stack = pack((w_qkv, w_out, w_up, w_down))
    attn_block = to_blocks(attn_stack)
    gather_z = lambda v: lax.all_gather(v, "fsdp", axis=0, tiled=True)
    xs = jnp.concatenate(spread(after(row_low, attn_block)), axis=0)
    both_block = to_blocks(after(jnp.concatenate([up_stack, down_stack], axis=2), xs))
    up_block, down_block = both_block[:, :u], both_block[:, u:]
    attn_g, up_g, down_g = map(gather_z, (attn_block, up_block, down_block))
    moment_stack = jnp.concatenate(pack((moment_qkv, moment_out, moment_up, moment_down)), axis=2)
    moment_stack = after(moment_stack, both_block)
    attn_g = after(attn_g, moment_stack)
    attn_w = (attn_g, swap_core(attn_g))

    bias_q = lax.dynamic_slice_in_dim(bias_qv, c * e, e, 1)
    bias_u = lax.dynamic_slice_in_dim(bias_up, c * u, u, 0)
    small = jnp.concatenate([bias_q.reshape(-1), bias_u])
    small_pair = (small, swap_core(small))
    cores = range(2)

    qkv = []
    for i in cores:
        shift = jnp.concatenate([small_pair[i][:e], jnp.zeros((e,), f32), small_pair[i][e : 2 * e]])
        qkv.append((mm(xs, attn_w[i][:, : 3 * e], (1, 0)) + shift).astype(bf16))
    context = [attend_forward(qkv[i], place) for i in cores]
    part = sum(mm(context[i], attn_w[i][:, 3 * e :], (1, 1)) for i in cores).astype(bf16)
    row = lambda matrix, index: matrix[index : index + 1]
    first_all, (first_unit, first_inverse), _ = exchange(
        "first_rows",
        1,
        first_step,
        part,
        [row_low],
        [row(bias_res, 0), row(norm_gain, 0), row(norm_shift, 0)],
        [f32, f32],
        0,
    )
    moment_block = to_blocks(after(moment_stack, first_all))
    moments = [moment_block[:, : 4 * e], moment_block[:, 4 * e : 4 * e + u], moment_block[:, 4 * e + u :]]
    up_g = after(up_g, first_all)
    up_w = (up_g, swap_core(up_g))
    pre_act = [mm(first_all, up_w[i], (1, 0)) + small_pair[i][2 * e :] for i in cores]
    active = [gelu_tanh(p).astype(bf16) for p in pre_act]
    down_g = after(down_g, moment_block, *active)
    down_w = (down_g, swap_core(down_g))
    part = sum(mm(active[i], down_w[i], (1, 1)) for i in cores).astype(bf16)
    branch_all, (out_rows, grad_second), second_sums = exchange(
        "second_rows",
        2,
        second_step,
        part,
        [first_unit, upper],
        [row(bias_res, 1), row(norm_gain, 0), row(norm_shift, 0), row(norm_gain, 1), row(norm_shift, 1)],
        [bf16, f32],
        3,
    )

    def pair_sum(terms):
        return (terms[0] + swap_core(terms[1].astype(bf16)).astype(f32)).astype(bf16)

    scatter_z = lambda v: lax.psum_scatter(v, "fsdp", scatter_dimension=0, tiled=True)
    term_down = [None, mm(branch_all, active[1], (0, 0)).astype(bf16)]
    term_down[0] = mm(after(branch_all, term_down[1]), active[0], (0, 0))
    branch_all, *term_down = lax.optimization_barrier((branch_all, *term_down))
    down_sum = pair_sum(term_down)

    def before_gelu(i, rows):
        return jax.vjp(gelu_tanh, pre_act[i])[1](mm(rows, down_w[i], (1, 0)))[0].astype(bf16)

    grad_pre = [before_gelu(0, branch_all)]
    branch_all, down_sum, grad_pre[0] = lax.optimization_barrier((branch_all, down_sum, grad_pre[0]))
    grad_pre.append(before_gelu(1, branch_all))
    part = sum(mm(grad_pre[i], up_w[i], (1, 1)) for i in cores).astype(bf16)
    term_up = [None, mm(first_all, grad_pre[1], (0, 0)).astype(bf16)]
    term_up[0] = mm(after(first_all, term_up[1]), grad_pre[0], (0, 0))
    part, up_sum = lax.optimization_barrier((part, pair_sum(term_up)))
    attended_all, (grad_first,), first_sums = exchange(
        "third_rows",
        3,
        third_step,
        part,
        [first_unit, first_inverse, grad_second],
        [row(norm_gain, 0)],
        [f32],
        3,
    )
    grad_qkv_low, term_attn = [None, None], [None, None]
    rows_for = attended_all
    for i in (1, 0):
        grad_context = mm(rows_for, attn_w[i][:, 3 * e :], (1, 0)).astype(bf16)
        grad_qkv_low[i] = attend_backward(qkv[i], grad_context, place)
        term_attn[i] = jnp.concatenate(
            [mm(xs, grad_qkv_low[i], (0, 0)), mm(rows_for, context[i], (0, 0))], axis=1
        )
        if i:
            term_attn[i] = term_attn[i].astype(bf16)
            rows_for = after(attended_all, term_attn[i])
    attn_sum = pair_sum(term_attn)
    *lows, attn_sum = lax.optimization_barrier((*grad_qkv_low, attn_sum))
    part = sum(mm(lows[i], attn_w[i][:, : 3 * e], (1, 1)) for i in cores).astype(bf16)

    qv_sums = []
    for i in cores:
        sums_i = jnp.sum(grad_qkv_low[i].astype(f32), axis=0)
        qv_sums.append(jnp.stack([sums_i[:e], sums_i[2 * e :]]))
    up_sums = [jnp.sum(g.astype(f32), axis=0) for g in grad_pre]
    side = lambda pair: [jnp.where(t == m, pair[0], pair[1]) for m in range(2)]
    bqv_all = jnp.stack(
        [
            lax.dynamic_update_slice_in_dim(jnp.zeros((2, count_c * e), f32), v, c * e, 1)
            for v in side(qv_sums)
        ]
    )
    bup_all = jnp.stack(
        [
            lax.dynamic_update_slice_in_dim(jnp.zeros((count_c * u,), f32), v, c * u, 0)
            for v in side(up_sums)
        ]
    )
    rest = jnp.concatenate(
        [
            first_sums[2],
            second_sums[2],
            first_sums[0],
            second_sums[0],
            first_sums[1],
            second_sums[1],
        ],
        axis=0,
    )
    flat = jnp.concatenate([bqv_all.reshape(-1), bup_all.reshape(-1), rest.reshape(-1)])

    down_total, up_total, attn_total = map(scatter_z, (down_sum, up_sum, attn_sum))
    step_scale = matrix_rate * math.sqrt(width / HDIM)
    (up_blocks, down_blocks), input_rows, flat = gradients_and_orthogonal(
        "feed_forward_slabs",
        4,
        (moments[1], moments[2]),
        (up_total, down_total),
        part,
        grad_first,
        flat,
    )
    attn_total = after(attn_total, input_rows)
    (attn_blocks,), *_ = gradients_and_orthogonal("attention_slabs", 5, moments[:1], (attn_total,))
    up_done = finish("up_finish", step_scale, *up_blocks, (moment_up,), (w_up,))
    down_done = finish("down_finish", step_scale, *down_blocks, (moment_down,), (w_down,))
    attn_done = finish(
        "attention_finish", step_scale, *attn_blocks, (moment_qkv, moment_out), (w_qkv, w_out)
    )
    grads, states, masters = [
        [*attn_done[k], *up_done[k], *down_done[k]] for k in range(3)
    ]

    both = lambda own, other: jnp.stack([jnp.where(t == m, own, other) for m in range(2)])[:, None]
    layer_out = both(out_rows, swap_core(out_rows))
    input_grad = both(input_rows, swap_core(input_rows))

    cut = bqv_all.size
    cut_two = cut + bup_all.size
    grad_bqv = lax.dynamic_index_in_dim(flat[:cut].reshape(bqv_all.shape), t, 0, keepdims=False)
    grad_bup = lax.dynamic_index_in_dim(flat[cut:cut_two].reshape(bup_all.shape), t, 0, keepdims=False)
    rest = flat[cut_two:].reshape(3, 2, width)
    vector_grads = (grad_bqv, grad_bup, rest[0], rest[1], rest[2])
    vector_states = [
        decay_rate * m + g
        for m, g in zip(
            (moment_bqv, moment_bup, moment_bres, moment_gain, moment_shift), vector_grads
        )
    ]
    vector_step = 1.0 / math.sqrt(token_total)
    vector_masters = [
        v - vector_step * s
        for v, s in zip((bias_qv, bias_up, bias_res, norm_gain, norm_shift), vector_states)
    ]
    return (
        layer_out,
        input_grad,
        *grads,
        *vector_grads,
        *states,
        *vector_states,
        *masters,
        *vector_masters,
    )


def solution(mesh):
    rows = P(None, "fsdp", "ctx", None)
    matrices = (
        P(None, ("fsdp", "ctx"), "tp"),
        P("tp", ("fsdp", "ctx")),
        P(("fsdp", "ctx"), "tp"),
        P("tp", ("fsdp", "ctx")),
    )
    vectors = (P(None, "tp"), P("tp"), P(), P(), P())
    return jax.shard_map(
        body,
        mesh=mesh,
        in_specs=(rows, P(None, "fsdp", None), rows, *matrices, *vectors, *matrices, *vectors),
        out_specs=(rows, rows, *((*matrices, *vectors) * 3)),
        check_vma=False,
    )
```

time: 928 us -> 792 us (0.85)
  Pallas kernels: 45.1 us -> 408 us
  waiting for transfers between devices: 352 us -> 48.1 us
  starting transfers between devices: 110 us -> 10.3 us
  other arithmetic: 95.4 us -> 44.3 us
  local copies, waits for them, and re-layouts: 105 us -> 68.7 us
  matrix products: 161 us -> 147 us
  blocking collectives: 35.3 us -> 44.8 us
    pallas_call x5 -> x10, Pallas kernels: 33.4 us -> 397 us  [the longest x3 214 us: exchange(): pl.pallas_call(lambda *refs: exchange_kernel(step, len(ins), len(vectors)...]
    ppermute x34 -> x4, waiting for transfers between devices: 205 us -> 24.4 us  [swap_ctx(): return lax.ppermute(value, 'ctx', xor_pairs(4, mask))]
    all_gather x3, waiting for transfers between devices: 69.3 us -> 15.3 us  [body(): gather_z = lambda v: lax.all_gather(v, 'fsdp', axis=0, tiled=True)]
    all_to_all x10 -> x1, waiting for transfers between devices: 50.9 us -> 0.44 us  [over_ctx(): return lax.all_to_all(stack, 'ctx', split_axis=0, concat_axis=0, tiled=True)]
    all_to_all x10 -> x1, starting transfers between devices: 40 us -> 4.66 us  [over_ctx(): return lax.all_to_all(stack, 'ctx', split_axis=0, concat_axis=0, tiled=True)]
    ppermute x34 -> x4, starting transfers between devices: 38.8 us -> 3.46 us  [swap_ctx(): return lax.ppermute(value, 'ctx', xor_pairs(4, mask))]
    ppermute x20 -> x0, starting transfers between devices: 30.2 us -> none  [swap_fsdp(): return lax.ppermute(value, 'fsdp', xor_pairs(4, mask))]
    ppermute x20 -> x0, waiting for transfers between devices: 26.3 us -> none  [swap_fsdp(): return lax.ppermute(value, 'fsdp', xor_pairs(4, mask))]
  transfers between devices with their start and end apart: 80 -> 20, of which waited for: 43 -> 7; matrix products, arithmetic and copies ran while one was open for 31% -> 24% of each run, Pallas kernels for 5% -> 38%
where the time goes in v2:
time: 792 us; the launch traced here: 786 us
  Pallas kernels  408 us (52%)
  matrix products  147 us (19%)
  local copies, waits for them, and re-layouts  68.7 us (9%)
  waiting for transfers between devices  48.1 us (6%)
  blocking collectives  44.8 us (6%)
  other arithmetic  44.3 us (6%)
  between operations  15.7 us (2%)
  starting transfers between devices  10.3 us (1%)
    pallas_call x3, Pallas kernels, exchange(): pl.pallas_call(lambda *refs: exchange_kernel(step, len(ins), len(vectors)...  214 us
    pallas_call x2, Pallas kernels, gradients_and_orthogonal(): pl.pallas_call(lambda *refs: slab_kernel(groups, with_rows, *refs), out_s...  153 us
    dot_general x24, matrix products, mm(): lax.dot_general(left, right, ((dims[:1], dims[1:]), ((), ())), preferred_...  147 us
    all_to_all x2, blocking collectives, over_ctx(): return lax.all_to_all(stack, 'ctx', split_axis=0, concat_axis=0, tiled=True)  44.8 us
    unnamed x188, local copies, waits for them, and re-layouts  43.2 us
    ppermute x4, waiting for transfers between devices, swap_ctx(): return lax.ppermute(value, 'ctx', xor_pairs(4, mask))  24.4 us
    pallas_call x2, Pallas kernels, attend_backward(): pl.pallas_call(lambda *refs: attend_back_kernel(256, heads, *refs), out_s...  20.4 us
  transfers between devices with their start and end apart: 20, of which 7 were waited for; matrix products, arithmetic and copies ran while one was open for 24% of the time, Pallas kernels for 38%

profile of v2, /device:TPU:0, one launch (start us, length us, event | category | flops | bytes accessed | tf_op | source)
XLA Modules:
  0.0 786.3 jit_solution(3618677228960263545)
XLA Ops:
  10.5 19.1 %all_to_all.15 = bf16[4,128,1024]{1,2,0:T(8,128)(2,1)S(1)} all-to-all(bf16[4,128,1024]{1,2,0:T(8,128)(2,1)S(1)} %bitcast.167), channel_id=1, replica_groups=mesh['fsdp'=4,'ctx'=4,'tp'=2] {'ctx'}, dimensions={0} | all-to-all | bytes 2097152 | tf_op jit(solution)/shard_map/all_to_all | solution.py:758
  38.3 16.3 %collective-permute-done = bf16[256,2048]{1,0:T(8,128)(2,1)} collective-permute-done((bf16[256,2048]{1,0:T(8,128)(2,1)S(1)}, bf16[256,2048]{1,0:T(8,128)(2,1)}, u32[]{:S(2)}, u32[]{:S(2)}) %collective-permute-start) | collective-permute-done | bytes 1048608 | tf_op jit(solution)/shard_map/ppermute | solution.py:38
  61.4 5.6 collective-permute-done.2
  71.6 25.7 %all_to_all.16 = bf16[4,128,2048]{1,2,0:T(8,128)(2,1)} all-to-all(bf16[4,128,2048]{1,2,0:T(8,128)(2,1)S(1)} %pad_maximum_fusion.2), channel_id=1, replica_groups=mesh['fsdp'=4,'ctx'=4,'tp'=2] {'ctx'}, dimensions={0} | all-to-all | bytes 4194304 | tf_op jit(solution)/shard_map/all_to_all | solution.py:758
  97.3 3.9 copy.80
  101.2 3.1 fusion.40
  124.8 3.7 collective-permute-done.5
  128.6 6.6 add_convert_fusion.7.refs_0_.refs_1_.refs_2_
  135.2 5.6 attend_forward.2
  140.9 2.7 fusion.32
  143.6 5.3 add_convert_fusion.6.refs_0_.refs_1_.refs_2_
  149.0 5.5 attend_forward.3
  157.1 71.4 %first_rows.1 = (bf16[4,2,128,2048]{3,2,1,0:T(8,128)(2,1)S(1)}, f32[2,128,2048]{2,1,0:T(8,128)S(1)}, f32[2,128,2048]{2,1,0:T(8,128)S(1)}, f32[8,2048]{1,0:T(8,128)}) custom-call(bf16[2,2,2,128,2048]{4,3,2,1,0:T(8,128)(2,1)S(1)} %bitcast.136, bf16[2,128,2048]{2,1,0:T(8,128)(2,1)S(1)} %bitcast.141, f32[1,2048]{1,0:T(1,128)S(1)} %get-tuple-element.170.refs_2_, ...), custom_call_target="tpu_custom_call" | custom-call | flops 31457280 | bytes 136314880 | tf_op jit(solution)/shard_map/first_rows/pallas_call | solution.py:257
  233.1 4.7 all-to-all-start.2
  237.9 11.5 %multiply_convert_fusion.1 = (bf16[1024,1024]{1,0:T(8,128)(2,1)}, f32[1024,1024]{1,0:T(8,128)}) fusion(f32[1024]{0:T(1024)S(1)} %dynamic_slice.28, bf16[1024,2048]{1,0:T(8,128)(2,1)} %bitcast.151, bf16[2048,1024]{1,0:T(8,128)(2,1)} %all-gather.6.cloned.1.call-done), kind=kOutput, calls=%fused_computation.32 | convolution fusion | flops 4305453056 | bytes 14684160 | tf_op jit(solution)/shard_map/dot_general | solution.py:46
  249.4 9.8 %multiply_convert_fusion = (bf16[1024,1024]{1,0:T(8,128)(2,1)}, f32[1024,1024]{1,0:T(8,128)}) fusion(f32[1024]{0:T(1024)S(1)} %slice.183, bf16[1024,2048]{1,0:T(8,128)(2,1)S(1)} %bitcast.152, bf16[2048,1024]{1,0:T(8,128)(2,1)} %collective-permute-done.6), kind=kOutput, calls=%fused_computation.31 | convolution fusion | flops 4305453056 | bytes 14684160 | tf_op jit(solution)/shard_map/dot_general | solution.py:46
  259.2 15.3 %all-gather.8.cloned.1.call-done = bf16[2048,1024]{1,0:T(8,128)(2,1)} async-done(((bf16[512,1024]{1,0:T(8,128)(2,1)}), bf16[2048,1024]{1,0:T(8,128)(2,1)}) %all-gather.8.cloned.1.call-update) | async-done | bytes 4194320 | tf_op jit(solution)/shard_map/all_gather | solution.py:816
  276.3 10.9 %fusion.50 = f32[1024,2048]{1,0:T(8,128)} fusion(bf16[1024,1024]{1,0:T(8,128)(2,1)} %get-tuple-element.183, bf16[2048,1024]{1,0:T(8,128)(2,1)} %all-gather.8.cloned.1.call-done), kind=kOutput, calls=%fused_computation.123 | convolution fusion | flops 4294967296 | bytes 14680064 | tf_op jit(solution)/shard_map/dot_general | solution.py:46
  287.2 8.5 %add_convert_fusion.4 = bf16[1024,2048]{1,0:T(8,128)(2,1)S(1)} fusion(f32[1024,2048]{1,0:T(8,128)} %fusion.50, bf16[1024,1024]{1,0:T(8,128)(2,1)S(1)} %copy-done.86, bf16[2048,1024]{1,0:T(8,128)(2,1)S(1)} %collective-permute-done.7), kind=kOutput, calls=%fused_computation.7 | convolution fusion | flops 4299161600 | bytes 18874368 | tf_op jit(solution)/shard_map/dot_general | solution.py:46
  295.7 71.7 %second_rows.1 = (bf16[4,2,128,2048]{3,2,1,0:T(8,128)(2,1)S(1)}, bf16[2,128,2048]{2,1,0:T(8,128)(2,1)S(1)}, f32[2,128,2048]{2,1,0:T(8,128)S(1)}, f32[8,2048]{1,0:T(8,128)S(1)}) custom-call(bf16[2,2,2,128,2048]{4,3,2,1,0:T(8,128)(2,1)S(1)} %bitcast.143, f32[2,128,2048]{2,1,0:T(8,128)S(1)} %copy-done.9, bf16[2,128,2048]{2,1,0:T(8,128)(2,1)S(1)} %bitcast.144, ...), custom_call_target="tpu_custom_call" | custom-call | flops 31457280 | bytes 136314880 | tf_op jit(solution)/shard_map/second_rows/pallas_call | solution.py:257
  367.5 5.1 convolution_convert_fusion.1
  372.6 6.8 fusion.51
  379.5 8.0 %fusion.7 = bf16[1024,1024]{1,0:T(8,128)(2,1)} fusion(f32[1024,1024]{1,0:T(8,128)S(1)} %copy-done.84, f32[1024]{0:T(1024)S(1)} %dynamic_slice.28, bf16[1024,2048]{1,0:T(8,128)(2,1)S(1)} %bitcast.161, bf16[2048,1024]{1,0:T(8,128)(2,1)S(1)} %copy-done.82), kind=kOutput, calls=%fused_computation.19 | convolution fusion | flops 4316987392 | bytes 14684160 | tf_op jit(solution)/shard_map/dot_general | solution.py:46
  387.5 7.0 add_convert_fusion.3
  394.5 11.7 %convert_reduce_fusion = (f32[1024]{0:T(1024)S(1)}, bf16[1024,1024]{1,0:T(8,128)(2,1)S(1)}) fusion(f32[1024,1024]{1,0:T(8,128)} %get-tuple-element.186, f32[1024]{0:T(1024)S(1)} %slice.183, bf16[1024,2048]{1,0:T(8,128)(2,1)} %bitcast.162, bf16[2048,1024]{1,0:T(8,128)(2,1)} %copy-done.83), kind=kOutput, calls=%fused_computation.29 | convolution fusion | flops 4319083520 | bytes 14688256 | tf_op jit(solution)/shard_map/dot_general | solution.py:46
  406.2 6.4 convolution_convert_fusion
  413.2 9.2 %fusion.52 = f32[1024,2048]{1,0:T(8,128)} fusion(bf16[1024,1024]{1,0:T(8,128)(2,1)S(1)} %get-tuple-element.145, bf16[2048,1024]{1,0:T(8,128)(2,1)} %collective-permute-done.6), kind=kOutput, calls=%fused_computation.125 | convolution fusion | flops 4294967296 | bytes 14680064 | tf_op jit(solution)/shard_map/dot_general | solution.py:46
  422.4 8.4 %add_convert_fusion.2 = bf16[1024,2048]{1,0:T(8,128)(2,1)} fusion(f32[1024,2048]{1,0:T(8,128)} %fusion.52, bf16[1024,1024]{1,0:T(8,128)(2,1)S(1)} %copy-done.56, bf16[2048,1024]{1,0:T(8,128)(2,1)S(1)} %copy-done.81), kind=kOutput, calls=%fused_computation.5 | convolution fusion | flops 4299161600 | bytes 18874368 | tf_op jit(solution)/shard_map/dot_general | solution.py:46
  430.8 6.3 add_convert_fusion.1
  444.2 70.6 %third_rows.1 = (bf16[4,2,128,2048]{3,2,1,0:T(8,128)(2,1)S(1)}, f32[2,128,2048]{2,1,0:T(8,128)S(1)}, f32[8,2048]{1,0:T(8,128)S(1)}) custom-call(bf16[2,2,2,128,2048]{4,3,2,1,0:T(8,128)(2,1)S(1)} %bitcast.142, f32[2,128,2048]{2,1,0:T(8,128)S(1)} %copy-done.10, f32[2,128,2048]{2,1,0:T(8,128)S(1)} %copy-done.21, f32[2,128,2048]{2,1,0:T(8,128)S(1)} %copy-done.23, ...), custom_call_target="tpu_custom_call" | custom-call | flops 31457280 | bytes 136314880 | tf_op jit(solution)/shard_map/third_rows/pallas_call | solution.py:257
  514.8 3.3 convolution_convert_fusion.5.refs_3_
  518.1 10.2 %attend_backward.2 = bf16[1024,768]{1,0:T(8,128)(2,1)S(1)} custom-call(bf16[1024,768]{1,0:T(8,128)(2,1)S(1)} %add_convert_fusion.6.refs_0_.refs_1_.refs_2_, bf16[1024,768]{1,0:T(8,128)(2,1)S(1)} %add_convert_fusion.6.refs_0_.refs_1_.refs_2_, bf16[1024,768]{1,0:T(8,128)(2,1)S(1)} %add_convert_fusion.6.refs_0_.refs_1_.refs_2_, ...), custom_call_target="tpu_custom_call" | custom-call | flops 2684354560 | bytes 3670016 | tf_op jit(solution)/shard_map/attend_backward/pallas_call | solution.py:392
  531.1 3.9 convolution_convert_fusion.2
  538.3 3.8 fusion.39
  542.1 4.1 collective-permute-done.8
  546.2 2.7 select_bitcast_fusion.3
  551.5 10.2 %attend_backward.3 = bf16[1024,768]{1,0:T(8,128)(2,1)S(1)} custom-call(bf16[1024,768]{1,0:T(8,128)(2,1)S(1)} %copy-done.3, bf16[1024,768]{1,0:T(8,128)(2,1)S(1)} %copy-done.3, bf16[1024,768]{1,0:T(8,128)(2,1)S(1)} %copy-done.3, bf16[1024,256]{1,0:T(8,128)(2,1)S(1)} %convolution_convert_fusion.4.refs_3_, s32[1024,1]{1,0:T(8,128)S(1)} %bitcast.140, ...), custom_call_target="tpu_custom_call" | custom-call | flops 2684354560 | bytes 3670016 | tf_op jit(solution)/shard_map/attend_backward/pallas_call | solution.py:392
  564.4 3.7 fusion.53
  568.1 4.6 fusion
  573.9 2.8 maximum_bitcast_fusion.1
  579.7 5.5 fusion.15
  585.2 5.0 add_convert_fusion
  593.9 115.6 %feed_forward_slabs.1 = (bf16[4,128,1024]{2,1,0:T(8,128)(2,1)S(1)}, bf16[4,128,1024]{2,1,0:T(8,128)(2,1)S(1)}, bf16[4,128,1024]{2,1,0:T(8,128)(2,1)S(1)}, bf16[4...) custom-call(bf16[512,1024]{1,0:T(8,128)(2,1)S(1)} %copy-done.33, ...), custom_call_target="tpu_custom_call" | custom-call | flops 4831838208 | bytes 104857600 | tf_op jit(solution)/shard_map/feed_forward_slabs/pallas_call | solution.py:656
  719.9 3.1 down_finish.1
  726.2 3.2 up_finish.1
  732.0 2.7 select_bitcast_fusion.1
  738.3 37.7 %attention_slabs.1 = (bf16[4,128,1024]{2,1,0:T(8,128)(2,1)S(1)}, bf16[4,128,1024]{2,1,0:T(8,128)(2,1)S(1)}) custom-call(bf16[512,1024]{1,0:T(8,128)(2,1)S(1)} %copy-done.31, bf16[512,1024]{1,0:T(8,128)(2,1)S(1)} %copy-done.51), custom_call_target="tpu_custom_call" | custom-call | flops 2415919104 | bytes 104857600 | tf_op jit(solution)/shard_map/attention_slabs/pallas_call | solution.py:656
  776.1 3.1 attention_finish.1
  (309 shorter events, 99.1 us)
Async XLA Ops:
  7.2 23.8 %copy-start = (bf16[2,1,256,2048]{3,2,1,0:T(8,128)(2,1)S(1)}, bf16[2,1,256,2048]{3,2,1,0:T(8,128)(2,1)}, u32[]{:S(2)}) copy-start(bf16[2,1,256,2048]{3,2,1,0:T(8,128)(2,1)} %param.21) | copy-start | bytes 6291460
  7.2 114.2 %all-gather.4.cloned.1.call-start = ((), (), s32[]{:S(2)}) async-start(), calls=%async_computation.6 | async-start | bytes 5242880 | tf_op jit(solution)/shard_map/all_gather | solution.py:816
  30.9 202.2 %all-gather.6.cloned.1.call-start = ((), (), s32[]{:S(2)}) async-start(), calls=%async_computation.7 | async-start | bytes 5242880 | tf_op jit(solution)/shard_map/all_gather | solution.py:816
  31.0 23.5 %collective-permute-start = (bf16[256,2048]{1,0:T(8,128)(2,1)S(1)}, bf16[256,2048]{1,0:T(8,128)(2,1)}, u32[]{:S(2)}, u32[]{:S(2)}) collective-permute-start(bf16[256,2048]{1,0:T(8,128)(2,1)S(1)} %fusion.95), channel_id=1, source_target_pairs={{0,2},{2,0},{4,6},{6,4},{1,3},{3,1},{5,7},{7,5},{8,10},{10,8},{12,... | collective-permute-start | bytes 3145736 | tf_op jit(solution)/shard_map/ppermute | solution.py:38
  32.0 25.1 %collective-permute-start.1 = (bf16[256,2048]{1,0:T(8,128)(2,1)S(1)}, bf16[256,2048]{1,0:T(8,128)(2,1)}, u32[]{:S(2)}, u32[]{:S(2)}) collective-permute-start(bf16[256,2048]{1,0:T(8,128)(2,1)S(1)} %fusion.95), channel_id=1, source_target_pairs={{0,4},{2,6},{4,0},{6,2},{1,5},{3,7},{5,1},{7,3},{8,12},{10,14},{12... | collective-permute-start | bytes 3145736 | tf_op jit(solution)/shard_map/ppermute | solution.py:38
  55.7 11.3 %collective-permute-start.2 = (bf16[128,2048]{1,0:T(8,128)(2,1)S(1)}, bf16[128,2048]{1,0:T(8,128)(2,1)S(1)}, u32[]{:S(2)}, u32[]{:S(2)}) collective-permute-start(bf16[128,2048]{1,0:T(8,128)(2,1)S(1)} %slice.175), channel_id=1, source_target_pairs={{0,4},{2,6},{4,0},{6,2},{1,5},{3,7},{5,1},{7,3},{8,12},{10,14},{12... | collective-permute-start | bytes 1572872 | tf_op jit(solution)/shard_map/ppermute | solution.py:38
  58.2 11.3 %collective-permute-start.3 = (bf16[128,2048]{1,0:T(8,128)(2,1)S(1)}, bf16[128,2048]{1,0:T(8,128)(2,1)S(1)}, u32[]{:S(2)}, u32[]{:S(2)}) collective-permute-start(bf16[128,2048]{1,0:T(8,128)(2,1)S(1)} %slice.176), channel_id=1, source_target_pairs={{0,2},{2,0},{4,6},{6,4},{1,3},{3,1},{5,7},{7,5},{8,10},{10,8},{12,... | collective-permute-start | bytes 1572872 | tf_op jit(solution)/shard_map/ppermute | solution.py:38
  104.3 170.2 %all-gather.8.cloned.1.call-start = ((), (), s32[]{:S(2)}) async-start(), calls=%async_computation.8 | async-start | bytes 5242880 | tf_op jit(solution)/shard_map/all_gather | solution.py:816
  121.4 22.2 %collective-permute-start.4 = (bf16[2048,1024]{1,0:T(8,128)(2,1)}, bf16[2048,1024]{1,0:T(8,128)(2,1)}, u32[]{:S(2)}, u32[]{:S(2)}) collective-permute-start(bf16[2048,1024]{1,0:T(8,128)(2,1)} %all-gather.4.cloned.1.call-done), channel_id=1, source_target_pairs={{0,1},{1,0},{2,3},{3,2},{4,5},{5,4},{6,7},{7,6},{8,9},{9,8},{10,11... | collective-permute-start | bytes 12582920 | tf_op jit(solution)/shard_map/ppermute | solution.py:34
  122.1 6.4 collective-permute-start.5
  233.1 16.3 %collective-permute-start.6 = (bf16[2048,1024]{1,0:T(8,128)(2,1)}, bf16[2048,1024]{1,0:T(8,128)(2,1)}, u32[]{:S(2)}, u32[]{:S(2)}) collective-permute-start(bf16[2048,1024]{1,0:T(8,128)(2,1)} %all-gather.6.cloned.1.call-done), channel_id=1, source_target_pairs={{0,1},{1,0},{2,3},{3,2},{4,5},{5,4},{6,7},{7,6},{8,9},{9,8},{10,11... | collective-permute-start | bytes 12582920 | tf_op jit(solution)/shard_map/ppermute | solution.py:34
  233.1 41.8 %all-to-all-start.2 = ((bf16[4,128,3072]{2,1,0:T(8,128)(2,1)}), bf16[4,128,3072]{2,1,0:T(8,128)(2,1)}, u32[]{:S(2)}, u32[]{:S(2)}) async-start(bf16[4,128,3072]{2,1,0:T(8,128)(2,1)} %pad_maximum_fusion.1), calls=%async_computation.2 | async-start | bytes 6291456 | tf_op jit(solution)/shard_map/all_to_all | solution.py:758
  237.8 352.4 %reduce-scatter.6.cloned.1.call-start = ((), (), s32[]{:S(2)}) async-start(), calls=%async_computation.10 | async-start | bytes 5242880 | tf_op jit(solution)/shard_map/reduce_scatter | solution.py:872
  237.9 11.5 %copy-start.43 = (bf16[4,2,128,2048]{3,2,1,0:T(8,128)(2,1)S(1)}, bf16[4,2,128,2048]{3,2,1,0:T(8,128)(2,1)}, u32[]{:S(2)}) copy-start(bf16[4,2,128,2048]{3,2,1,0:T(8,128)(2,1)} %copy-done.42) | copy-start | bytes 12582916
  274.9 12.2 %collective-permute-start.7 = (bf16[2048,1024]{1,0:T(8,128)(2,1)}, bf16[2048,1024]{1,0:T(8,128)(2,1)S(1)}, u32[]{:S(2)}, u32[]{:S(2)}) collective-permute-start(bf16[2048,1024]{1,0:T(8,128)(2,1)} %all-gather.8.cloned.1.call-done), channel_id=1, source_target_pairs={{0,1},{1,0},{2,3},{3,2},{4,5},{5,4},{6,7},{7,6},{8,9},{9,8},{10,11... | collective-permute-start | bytes 12582920 | tf_op jit(solution)/shard_map/ppermute | solution.py:34
  276.3 10.9 %copy-start.86 = (bf16[1024,1024]{1,0:T(8,128)(2,1)S(1)}, bf16[1024,1024]{1,0:T(8,128)(2,1)}, u32[]{:S(2)}) copy-start(bf16[1024,1024]{1,0:T(8,128)(2,1)} %get-tuple-element.185) | copy-start | bytes 6291460
  295.7 71.7 %copy-start.87 = (bf16[1024,1024]{1,0:T(8,128)(2,1)S(1)}, bf16[1024,1024]{1,0:T(8,128)(2,1)}, u32[]{:S(2)}) copy-start(bf16[1024,1024]{1,0:T(8,128)(2,1)} %get-tuple-element.185) | copy-start | bytes 6291460
  367.4 12.0 %copy-start.47 = (bf16[4,2,128,2048]{3,2,1,0:T(8,128)(2,1)}, bf16[4,2,128,2048]{3,2,1,0:T(8,128)(2,1)S(1)}, u32[]{:S(2)}) copy-start(bf16[4,2,128,2048]{3,2,1,0:T(8,128)(2,1)S(1)} %get-tuple-element.91) | copy-start | bytes 12582916
  379.4 8.0 %collective-permute-start.9 = (bf16[2048,1024]{1,0:T(8,128)(2,1)S(1)}, bf16[2048,1024]{1,0:T(8,128)(2,1)S(1)}, u32[]{:S(2)}, u32[]{:S(2)}) collective-permute-start(bf16[2048,1024]{1,0:T(8,128)(2,1)S(1)} %convolution_convert_fusion.1), channel_id=1, source_target_pairs={{0,1},{1,0},{2,3},{3,2},{4,5},{5,4},{6,7},{7,6},{8,9},{9,8},{10,11... | collective-permute-start | bytes 12582920 | tf_op jit(solution)/shard_map/ppermute | solution.py:34
  394.5 195.8 %reduce-scatter.4.cloned.1.call-start = ((), (), s32[]{:S(2)}) async-start(), calls=%async_computation.9 | async-start | bytes 5242880 | tf_op jit(solution)/shard_map/reduce_scatter | solution.py:872
  394.5 11.7 %copy-start.44 = (bf16[4,2,128,2048]{3,2,1,0:T(8,128)(2,1)S(1)}, bf16[4,2,128,2048]{3,2,1,0:T(8,128)(2,1)}, u32[]{:S(2)}) copy-start(bf16[4,2,128,2048]{3,2,1,0:T(8,128)(2,1)} %copy-done.42) | copy-start | bytes 12582916
  412.7 9.7 %copy-start.56 = (bf16[1024,1024]{1,0:T(8,128)(2,1)S(1)}, bf16[1024,1024]{1,0:T(8,128)(2,1)}, u32[]{:S(2)}) copy-start(bf16[1024,1024]{1,0:T(8,128)(2,1)} %fusion.7) | copy-start | bytes 6291460
  412.7 9.7 %copy-start.81 = (bf16[2048,1024]{1,0:T(8,128)(2,1)S(1)}, bf16[2048,1024]{1,0:T(8,128)(2,1)}, u32[]{:S(2)}) copy-start(bf16[2048,1024]{1,0:T(8,128)(2,1)} %all-gather.6.cloned.1.call-done) | copy-start | bytes 12582916
  412.7 18.1 %collective-permute-start.10 = (bf16[2048,1024]{1,0:T(8,128)(2,1)}, bf16[2048,1024]{1,0:T(8,128)(2,1)S(1)}, u32[]{:S(2)}, u32[]{:S(2)}) collective-permute-start(bf16[2048,1024]{1,0:T(8,128)(2,1)} %convolution_convert_fusion), channel_id=1, source_target_pairs={{0,1},{1,0},{2,3},{3,2},{4,5},{5,4},{6,7},{7,6},{8,9},{9,8},{10,11... | collective-permute-start | bytes 12582920 | tf_op jit(solution)/shard_map/ppermute | solution.py:34
  437.2 299.9 %reduce-scatter.8.cloned.1.call-start = ((), (), s32[]{:S(2)}) async-start(), calls=%async_computation.11 | async-start | bytes 5242880 | tf_op jit(solution)/shard_map/reduce_scatter | solution.py:872
  514.8 13.6 %copy-start.45 = (bf16[4,2,128,2048]{3,2,1,0:T(8,128)(2,1)}, bf16[4,2,128,2048]{3,2,1,0:T(8,128)(2,1)S(1)}, u32[]{:S(2)}) copy-start(bf16[4,2,128,2048]{3,2,1,0:T(8,128)(2,1)S(1)} %get-tuple-element.104) | copy-start | bytes 12582916
  514.8 13.6 %copy-start.48 = (f32[2,128,2048]{2,1,0:T(8,128)}, f32[2,128,2048]{2,1,0:T(8,128)S(1)}, u32[]{:S(2)}) copy-start(f32[2,128,2048]{2,1,0:T(8,128)S(1)} %get-tuple-element.108.refs_5_) | copy-start | bytes 6291460
  537.7 30.4 %collective-permute-start.11 = (bf16[2048,1024]{1,0:T(8,128)(2,1)}, bf16[2048,1024]{1,0:T(8,128)(2,1)}, u32[]{:S(2)}, u32[]{:S(2)}) collective-permute-start(bf16[2048,1024]{1,0:T(8,128)(2,1)} %pad_maximum_fusion), channel_id=1, source_target_pairs={{0,1},{1,0},{2,3},{3,2},{4,5},{5,4},{6,7},{7,6},{8,9},{9,8},{10,11... | collective-permute-start | bytes 12582920 | tf_op jit(solution)/shard_map/ppermute | solution.py:34
  537.7 8.4 %collective-permute-start.8 = (bf16[256,2048]{1,0:T(8,128)(2,1)S(1)}, bf16[256,2048]{1,0:T(8,128)(2,1)}, u32[]{:S(2)}, u32[]{:S(2)}) collective-permute-start(bf16[256,2048]{1,0:T(8,128)(2,1)S(1)} %bitcast.145), channel_id=1, source_target_pairs={{0,1},{1,0},{2,3},{3,2},{4,5},{5,4},{6,7},{7,6},{8,9},{9,8},{10,11... | collective-permute-start | bytes 3145736 | tf_op jit(solution)/shard_map/ppermute | solution.py:34
  538.2 10.6 %copy-start.46 = (bf16[4,2,128,2048]{3,2,1,0:T(8,128)(2,1)S(1)}, bf16[4,2,128,2048]{3,2,1,0:T(8,128)(2,1)}, u32[]{:S(2)}) copy-start(bf16[4,2,128,2048]{3,2,1,0:T(8,128)(2,1)} %copy-done.45) | copy-start | bytes 12582916
  551.4 10.2 %copy-start.16 = (bf16[1024,256]{1,0:T(8,128)(2,1)S(1)}, bf16[1024,256]{1,0:T(8,128)(2,1)}, u32[]{:S(2)}) copy-start(bf16[1024,256]{1,0:T(8,128)(2,1)} %copy-done.15) | copy-start | bytes 1572868
  593.9 119.5 %copy-start.74 = (f32[2,1024]{1,0:T(2,128)S(1)}, f32[2,1024]{1,0:T(2,128)}, u32[]{:S(2)}) copy-start(f32[2,1024]{1,0:T(2,128)} %param.28) | copy-start | bytes 24580
  593.9 119.5 %copy-start.79 = (f32[2,1024]{1,0:T(2,128)S(1)}, f32[2,1024]{1,0:T(2,128)}, u32[]{:S(2)}) copy-start(f32[2,1024]{1,0:T(2,128)} %param.37) | copy-start | bytes 24580
  713.4 18.6 %collective-permute-start.12 = (f32[256,2048]{1,0:T(8,128)}, f32[256,2048]{1,0:T(8,128)}, u32[]{:S(2)}, u32[]{:S(2)}) collective-permute-start(f32[256,2048]{1,0:T(8,128)} %bitcast.44), channel_id=1, source_target_pairs={{0,1},{1,0},{2,3},{3,2},{4,5},{5,4},{6,7},{7,6},{8,9},{9,8},{10,11... | collective-permute-start | bytes 6291464 | tf_op jit(solution)/shard_map/ppermute | solution.py:34
  714.1 15.9 %copy-start.64 = (f32[2,2048]{1,0:T(2,128)}, f32[2,2048]{1,0:T(2,128)S(1)}, u32[]{:S(2)}) copy-start(f32[2,2048]{1,0:T(2,128)S(1)} %squeeze.31) | copy-start | bytes 49156
  714.2 16.5 %copy-start.65 = (f32[2,2048]{1,0:T(2,128)}, f32[2,2048]{1,0:T(2,128)S(1)}, u32[]{:S(2)}) copy-start(f32[2,2048]{1,0:T(2,128)S(1)} %squeeze.30) | copy-start | bytes 49156
  714.2 17.1 %copy-start.66 = (f32[2,2048]{1,0:T(2,128)}, f32[2,2048]{1,0:T(2,128)S(1)}, u32[]{:S(2)}) copy-start(f32[2,2048]{1,0:T(2,128)S(1)} %squeeze.29) | copy-start | bytes 49156
  719.9 10.2 %copy-start.69 = (f32[2,2048]{1,0:T(2,128)S(1)}, f32[2,2048]{1,0:T(2,128)}, u32[]{:S(2)}) copy-start(f32[2,2048]{1,0:T(2,128)} %param.32) | copy-start | bytes 49156
  719.9 10.2 %copy-start.76 = (f32[2,2048]{1,0:T(2,128)S(1)}, f32[2,2048]{1,0:T(2,128)}, u32[]{:S(2)}) copy-start(f32[2,2048]{1,0:T(2,128)} %param.41) | copy-start | bytes 49156
  719.9 10.8 %copy-start.71 = (f32[2,2048]{1,0:T(2,128)S(1)}, f32[2,2048]{1,0:T(2,128)}, u32[]{:S(2)}) copy-start(f32[2,2048]{1,0:T(2,128)} %param.31) | copy-start | bytes 49156
  719.9 10.8 %copy-start.77 = (f32[2,2048]{1,0:T(2,128)S(1)}, f32[2,2048]{1,0:T(2,128)}, u32[]{:S(2)}) copy-start(f32[2,2048]{1,0:T(2,128)} %param.40) | copy-start | bytes 49156
  719.9 11.4 %copy-start.63 = (f32[2,2048]{1,0:T(2,128)S(1)}, f32[2,2048]{1,0:T(2,128)}, u32[]{:S(2)}) copy-start(f32[2,2048]{1,0:T(2,128)} %param.30) | copy-start | bytes 49156
  719.9 11.4 %copy-start.78 = (f32[2,2048]{1,0:T(2,128)S(1)}, f32[2,2048]{1,0:T(2,128)}, u32[]{:S(2)}) copy-start(f32[2,2048]{1,0:T(2,128)} %param.39) | copy-start | bytes 49156
  738.3 37.8 %copy-start.11 = (f32[3,128,1024]{2,1,0:T(8,128)S(1)}, f32[3,128,1024]{2,1,0:T(8,128)}, u32[]{:S(2)}) copy-start(f32[3,128,1024]{2,1,0:T(8,128)} %refs_2_.1) | copy-start | bytes 4718596
  738.3 37.8 %copy-start.12 = (f32[3,128,1024]{2,1,0:T(8,128)S(1)}, f32[3,128,1024]{2,1,0:T(8,128)}, u32[]{:S(2)}) copy-start(f32[3,128,1024]{2,1,0:T(8,128)} %refs_0_.3) | copy-start | bytes 4718596
  738.3 37.8 %copy-start.17 = (f32[1024,128]{1,0:T(8,128)S(1)}, f32[1024,128]{1,0:T(8,128)}, u32[]{:S(2)}) copy-start(f32[1024,128]{1,0:T(8,128)} %refs_3_.1) | copy-start | bytes 1572868
  738.3 37.8 %copy-start.19 = (f32[1024,128]{1,0:T(8,128)S(1)}, f32[1024,128]{1,0:T(8,128)}, u32[]{:S(2)}) copy-start(f32[1024,128]{1,0:T(8,128)} %refs_1_.3) | copy-start | bytes 1572868
  738.3 40.9 %copy-start.1 = (bf16[2,1,256,2048]{3,2,1,0:T(8,128)(2,1)S(1)}, bf16[2,1,256,2048]{3,2,1,0:T(8,128)(2,1)}, u32[]{:S(2)}) copy-start(bf16[2,1,256,2048]{3,2,1,0:T(8,128)(2,1)} %param.21) | copy-start | bytes 6291460
  (60 other events, 208.3 us)
Sparse Core Ops, SparseCore 0:
  31.0 80.4 all-gather.3
  113.7 79.2 all-gather.5
  195.2 79.2 all-gather.7
  394.6 76.5 reduce-scatter.5
  473.5 77.2 reduce-scatter.3
  572.9 110.7 reduce-scatter.7

commit v3 on v2

--- a/solution.py
+++ b/solution.py
@@ -118,6 +118,30 @@
     pl.semaphore_wait(barrier, len(axis_indices))
 
 
+def staged(kernel, count, n_in, n_out):
+    def run(*refs):
+        given, others, rest = refs[:count], refs[count : n_in + n_out], refs[n_in + n_out :]
+        slots, sems, rest = rest[:count], rest[count], rest[count + 1 :]
+        copies = [pltpu.make_async_copy(g, v, sems.at[k]) for k, (g, v) in enumerate(zip(given, slots))]
+        for one in copies:
+            one.start()
+
+        def ready(first, last):
+            for one in copies[first:last]:
+                one.wait()
+
+        kernel(given, ready, *slots, *others, *rest)
+
+    return run
+
+
+def slots_for(operands):
+    return [
+        *[pltpu.VMEM(o.shape, o.dtype) for o in operands],
+        pltpu.SemaphoreType.DMA((len(operands),)),
+    ]
+
+
 class RowSums:
     def __init__(self, part, from_x, from_y, then_y, then_x, to_y, to_x, send, receive):
         self.part, self.send, self.receive = part, send, receive
@@ -135,12 +159,12 @@
         copy.start()
         return copy
 
-    def first(self):
+    def first(self, part):
         for j in range(self.pieces):
             self.one.append(
                 (
-                    self.copy(0, j, self.part.at[:, 1, 0, self.span[j]], self.from_x.at[j], self.x_side),
-                    self.copy(1, j, self.part.at[1, :, 1, self.span[j]], self.from_y.at[j], self.y_side),
+                    self.copy(0, j, part.at[:, 1, 0, self.span[j]], self.from_x.at[j], self.x_side),
+                    self.copy(1, j, part.at[1, :, 1, self.span[j]], self.from_y.at[j], self.y_side),
                 )
             )
 
@@ -184,7 +208,7 @@
     ]
 
 
-def exchange_kernel(step, n_in, n_vec, n_out, n_sum, *refs):
+def exchange_kernel(step, n_in, n_vec, n_out, n_sum, given, ready, *refs):
     part = refs[0]
     ins = refs[1 : 1 + n_in]
     vectors = refs[1 + n_in : 1 + n_in + n_vec]
@@ -202,8 +226,10 @@
         one.start()
         return one
 
-    row_sums.first()
+    row_sums.first(given[0])
+    ready(0, 1)
     row_sums.second()
+    ready(1, 1 + n_in)
     params = [v[...] for v in vectors]
     third, fourth, kept = [], [], []
     totals = None
@@ -254,16 +280,24 @@
     half = rows // 2
     vmem = pl.BlockSpec(memory_space=pltpu.VMEM)
     halves = lambda v: v.reshape(2, half, width)
+    anywhere = pl.BlockSpec(memory_space=pl.ANY)
+    operands = [part.reshape(2, 2, 2, half, width), *map(halves, ins)]
+    n_in = len(operands) + len(vectors)
+
+    def kernel(*refs):
+        exchange_kernel(step, len(ins), len(vectors), len(out_types), n_sum, *refs)
+
     whole, *outs, sums = pl.pallas_call(
-        lambda *refs: exchange_kernel(step, len(ins), len(vectors), len(out_types), n_sum, *refs),
+        staged(kernel, len(operands), n_in, 2 + len(out_types)),
         out_shape=[
             jax.ShapeDtypeStruct((4, 2, half, width), bf16),
             *[jax.ShapeDtypeStruct((2, half, width), d) for d in out_types],
             jax.ShapeDtypeStruct((8, width), f32),
         ],
-        in_specs=[vmem] * (1 + len(ins) + len(vectors)),
-        out_specs=[pl.BlockSpec(memory_space=pl.ANY), *[vmem] * (len(out_types) + 1)],
+        in_specs=[*[anywhere] * len(operands), *[vmem] * len(vectors)],
+        out_specs=[anywhere, *[vmem] * (len(out_types) + 1)],
         scratch_shapes=[
+            *slots_for(operands),
             pltpu.VMEM((2, half, width), bf16),
             pltpu.SemaphoreType.DMA((4, pieces)),
             pltpu.SemaphoreType.DMA((4, pieces)),
@@ -271,13 +305,13 @@
             *row_scratch(half, width, pieces),
         ],
         compiler_params=pltpu.CompilerParams(
-            collective_id=number, has_side_effects=True, vmem_limit_bytes=36 << 20
+            collective_id=number, has_side_effects=True, vmem_limit_bytes=56 << 20
         ),
         cost_estimate=pl.CostEstimate(
             flops=60 * rows * width, bytes_accessed=130 << 20, transcendentals=0
         ),
         name=name,
-    )(part.reshape(2, 2, 2, half, width), *map(halves, ins), *vectors)
+    )(*operands, *vectors)
     return (
         whole.reshape(4 * rows, width),
         [o.reshape(rows, width) for o in outs],
@@ -480,35 +514,133 @@
         out_ref[n] = total
 
 
-def slab_kernel(groups, with_rows, *refs):
-    moments, totals, refs = refs[:groups], refs[groups : 2 * groups], refs[2 * groups :]
-    if with_rows:
-        part, base, vector, refs = refs[0], refs[1], refs[2], refs[3:]
-    grads, orthos, refs = refs[:groups], refs[groups : 2 * groups], refs[2 * groups :]
-    if with_rows:
-        summed, vector_out, refs = refs[0], refs[1], refs[2:]
-    grams, pieces, factors, stage, send_c, receive_c, send_f, receive_f, local = refs[:9]
-    rows = totals[0].shape[0] // 4
+def summed_polynomials(moments, totals, grams, pieces, send, receive, keep, between):
     each_group = totals[0].shape[1] // HDIM
     count = grams.shape[0]
+    size = min(each_group, count // 2)
+    each = size // 4
+    f = lax.axis_index("fsdp")
+    planes = [(f + i) % 4 for i in range(4)]
+    batches = range(count // size)
+    copies = []
+    for b in batches:
+        first = b * size
+        for n in range(first, first + size):
+            g = n // each_group
+            grams[n] = gram_of(moments[g], totals[g], n % each_group)
+        copies.append([])
+        for i in (1, 2, 3):
+            one = remote(
+                grams.at[pl.ds(first + planes[i] * each, each)],
+                pieces.at[i - 1, pl.ds(b * each, each)],
+                send.at[b, i - 1],
+                receive.at[b, i - 1],
+                "fsdp",
+                planes[i],
+            )
+            one.start()
+            copies[b].append(one)
+    between()
+    for b in batches:
+        sums = [grams[b * size + f * each + n] for n in range(each)]
+        for i in (1, 2, 3):
+            copies[b][i - 1].wait()
+            sums = [s + pieces[i - 1, b * each + n] for n, s in enumerate(sums)]
+        for n, value in enumerate(polynomial(sums)):
+            keep(b, n, value)
+        yield b
+
+
+def rows_to_owners(totals, targets, send, receive, local, first=0):
+    rows = totals[0].shape[0] // 4
     c = lax.axis_index("ctx")
-    f = lax.axis_index("fsdp")
-    sides = [(c + i) % 4 for i in range(4)]
-    planes = [(f + i) % 4 for i in range(4)]
-    peers = [("ctx", sides[i]) for i in (1, 2, 3)] + [("fsdp", planes[i]) for i in (1, 2, 3)]
-    if with_rows:
-        t = lax.axis_index("tp")
-        partners = [
-            ("tp", 1 - t),
-            ("ctx", c + 1 - 2 * (c % 2)),
-            ("ctx", c + 2 - 4 * (c // 2)),
-            ("fsdp", f + 1 - 2 * (f % 2)),
-            ("fsdp", f + 2 - 4 * (f // 2)),
-        ]
-        peers.append(partners[0])
-        sent_v, got_v, send_v, receive_v = refs[9:13]
-        sent_v[0] = vector[...]
-    greet(peers)
+    copies = []
+    for g, (total, target) in enumerate(zip(totals, targets)):
+        for i in (3, 1, 2, 0):
+            side = (c + i) % 4
+            source = total.at[pl.ds(pl.multiple_of(side * rows, rows), rows)]
+            if i:
+                sems = send.at[first + g, i - 1], receive.at[first + g, i - 1]
+                copies.append(remote(source, target.at[c], *sems, "ctx", side))
+            else:
+                copies.append(pltpu.make_async_copy(source, target.at[c], local.at[0, g]))
+            copies[-1].start()
+    return copies
+
+
+class Chain:
+    def __init__(self, b, size, factors, send, receive):
+        self.b, self.size, self.factors, self.send, self.receive_sem = b, size, factors, send, receive
+        self.f = lax.axis_index("fsdp")
+
+    def copy(self, up, k, block, plane):
+        each = self.size // 4
+        ref = self.factors.at[pl.ds(self.b * self.size + block * each, each)]
+        at = 2 * self.b + up, k
+        return remote(ref, ref, self.send.at[at], self.receive_sem.at[at], "fsdp", plane)
+
+    def leaving(self, up, k):
+        f = self.f
+        return self.copy(up, k, f - k, f + 1) if up else self.copy(up, k, f + k, f - 1)
+
+    def coming(self, up, k):
+        f = self.f
+        return self.copy(up, k, f - 1 - k, f - 1) if up else self.copy(up, k, f + 1 + k, f + 1)
+
+    def leaves(self, up, k):
+        f = self.f
+        return jnp.logical_and(f < 3, f >= k) if up else jnp.logical_and(f > 0, f + k <= 3)
+
+    def comes(self, up, k):
+        return self.f >= k + 1 if up else self.f <= 2 - k
+
+    def start(self, k):
+        for up in (1, 0):
+            pl.when(self.leaves(up, k))(lambda up=up: self.leaving(up, k).start())
+
+    def receive(self, k):
+        for up in (1, 0):
+            pl.when(self.comes(up, k))(lambda up=up: self.coming(up, k).wait_recv())
+
+    def end(self):
+        for k in range(3):
+            for up in (1, 0):
+                pl.when(self.leaves(up, k))(lambda up=up: self.leaving(up, k).wait_send())
+
+
+def all_sides():
+    c, f, t = (lax.axis_index(axis) for axis in ("ctx", "fsdp", "tp"))
+    over = [(axis, (at + i) % 4) for axis, at in (("ctx", c), ("fsdp", f)) for i in (1, 2, 3)]
+    return [*over, ("tp", 1 - t)]
+
+
+def share_core(share, shared, send, receive, local):
+    t = lax.axis_index("tp")
+    copies = [
+        remote(share, shared.at[t], send.at[0], receive.at[0], "tp", 1 - t),
+        pltpu.make_async_copy(share, shared.at[t], local.at[0]),
+    ]
+    for one in copies:
+        one.start()
+    return copies
+
+
+def feed_forward_kernel(given, ready, *refs):
+    moments, totals, (part, base, vector), refs = refs[:2], refs[2:4], refs[4:7], refs[7:]
+    share, refs = refs[0], refs[1:]
+    (out, *grads), (shared, summed, vector_out), refs = refs[:3], refs[3:6], refs[6:]
+    factors, send_c, receive_c, local, send_t, receive_t, local_t, send_f, receive_f = refs[:9]
+    gram_refs, (sent_v, got_v, send_v, receive_v), row_refs = refs[9:13], refs[13:17], refs[17:]
+    c, f, t = (lax.axis_index(axis) for axis in ("ctx", "fsdp", "tp"))
+    partners = [
+        ("tp", 1 - t),
+        ("ctx", c + 1 - 2 * (c % 2)),
+        ("ctx", c + 2 - 4 * (c // 2)),
+        ("fsdp", f + 1 - 2 * (f % 2)),
+        ("fsdp", f + 2 - 4 * (f // 2)),
+    ]
+    greet(all_sides())
+    vector_copies = []
 
     def vector_start(k):
         one = remote(sent_v.at[k], got_v.at[k], send_v.at[k], receive_v.at[k], *partners[k])
@@ -516,185 +648,237 @@
         vector_copies.append(one)
 
     def vector_next(k):
-        if not with_rows:
-            return
         vector_copies[k].wait_recv()
         if k < 4:
             sent_v[k + 1] = sent_v[k] + got_v[k]
             vector_start(k + 1)
         else:
             vector_out[...] = sent_v[k] + got_v[k]
-            for one in vector_copies:
-                one.wait_send()
-
-    vector_copies = []
-    place = lambda index: pl.ds(pl.multiple_of(index * rows, rows), rows)
-    started = []
-
-    def begin(copy):
-        copy.start()
-        started.append(copy)
-
-    def to_side(source, target, kind, i):
-        begin(
-            remote(
-                source, target, send_c.at[kind, i - 1], receive_c.at[kind, i - 1], "ctx", sides[i]
-            )
-        )
-
-    if with_rows:
-        vector_start(0)
-        sum_rows = RowSums(part, *refs[13:])
-        sum_rows.first()
-    for g in range(groups):
-        for i in (3, 1, 2):
-            to_side(totals[g].at[place(sides[i])], grads[g].at[c], g, i)
-        begin(pltpu.make_async_copy(totals[g].at[place(c)], grads[g].at[c], local.at[0, g]))
-
-    size = min(each_group, count // 2)
-    batches = range(count // size)
+
+    sum_rows = RowSums(part, *row_refs)
+    sum_rows.first(given[4])
+    ready(0, 8)
+    started = rows_to_owners(totals, grads, send_c, receive_c, local)
+    started += share_core(share, shared, send_t, receive_t, local_t)
+    sent_v[0] = vector[...]
+    vector_start(0)
+    size = totals[0].shape[1] // HDIM
     each = size // 4
-
-    def to_planes(kind, b, source, target):
-        copies = []
-        for i in (1, 2, 3):
-            sems = send_f.at[2 * b + kind, i - 1], receive_f.at[2 * b + kind, i - 1]
-            one = remote(source(i), target(i), *sems, "fsdp", planes[i])
-            one.start()
-            copies.append(one)
-        return copies
-
-    summing, sharing = [], []
-    for b in batches:
-        first = b * size
-        for n in range(first, first + size):
-            g = n // each_group
-            grams[n] = gram_of(moments[g], totals[g], n % each_group)
-        summing.append(
-            to_planes(
-                0,
-                b,
-                lambda i: grams.at[pl.ds(first + planes[i] * each, each)],
-                lambda i: pieces.at[i - 1, pl.ds(b * each, each)],
-            )
-        )
-    vector_next(0)
-    if with_rows:
+    chains = [Chain(b, size, factors, send_f, receive_f) for b in range(2)]
+
+    def keep(b, n, value):
+        factors[b * size + f * each + n] = value
+
+    def between():
+        vector_next(0)
         sum_rows.second()
-    for b in batches:
-        own = b * size + f * each
-        sums = [grams[own + n] for n in range(each)]
-        for i in (1, 2, 3):
-            summing[b][i - 1].wait()
-            sums = [s + pieces[i - 1, b * each + n] for n, s in enumerate(sums)]
-        for n, total in enumerate(polynomial(sums)):
-            factors[own + n] = total
-        part_of = lambda i: factors.at[pl.ds(own, each)]
-        sharing.append(to_planes(1, b, part_of, part_of))
-        vector_next(1 + b)
-    if with_rows:
-        for j in range(sum_rows.pieces):
-            span, total = sum_rows.third(j)
-            for h in range(2):
-                value = total[h * sum_rows.count : (h + 1) * sum_rows.count]
-                summed[h, span] = base[h, span] + value
-    vector_next(3)
-    for b in batches:
-        for one in sharing[b]:
-            one.wait()
-        g, first = b * size // each_group, b * size % each_group
+        vector_next(1)
+
+    for b in summed_polynomials(moments, totals, *gram_refs, keep, between):
+        chains[b].start(0)
+    vector_next(2)
+    for j in range(sum_rows.pieces):
+        span, total = sum_rows.third(j)
+        for h in range(2):
+            value = total[h * sum_rows.count : (h + 1) * sum_rows.count]
+            summed[h, span] = base[h, span] + value
+    for k in range(3):
+        for chain in chains:
+            chain.receive(k)
+            if k < 2:
+                chain.start(k + 1)
+        if k == 0:
+            vector_next(3)
+    out[...] = factors[...]
+    vector_next(4)
+    for chain in chains:
+        chain.end()
+    for one in vector_copies:
+        one.wait_send()
+    for one in started:
+        one.wait()
+    sum_rows.end()
+
+
+def last_kernel(given, ready, *refs):
+    moments, totals, (others, share), refs = refs[:3], refs[3:6], refs[6:8], refs[8:]
+    orthos, (grads, shared), refs = refs[:3], refs[3:5], refs[5:]
+    factors, stage, send_c, receive_c, local, send_t, receive_t, local_t, send_f, receive_f = refs[:10]
+    gram_refs = refs[10:]
+    rows = totals[0].shape[0] // 4
+    count = totals[0].shape[1] // HDIM
+    c, f = lax.axis_index("ctx"), lax.axis_index("fsdp")
+    greet(all_sides())
+    ready(0, 8)
+    started = rows_to_owners(totals[:1], [grads], send_c, receive_c, local)
+    started += share_core(share, shared, send_t, receive_t, local_t)
+
+    def send_ortho(g, first, size, kind, factor):
         wide = pl.ds(first * HDIM, size * HDIM)
         for i in (3, 1, 2, 0):
-            span = place(sides[i])
+            side = (c + i) % 4
+            span = pl.ds(pl.multiple_of(side * rows, rows), rows)
             for n in range(first, first + size):
                 column = pl.ds(n * HDIM, HDIM)
                 state = decay_rate * moments[g][span, column].astype(f32)
                 state = state + totals[g][span, column].astype(f32)
                 stage[g, i, :, column] = jnp.dot(
-                    state, factors[g * each_group + n], precision=highest, preferred_element_type=f32
+                    state, factor(n), precision=highest, preferred_element_type=f32
                 ).astype(bf16)
             source, target = stage.at[g, i, :, wide], orthos[g].at[c, :, wide]
             if i:
-                to_side(source, target, groups + b, i)
+                sems = send_c.at[kind, i - 1], receive_c.at[kind, i - 1]
+                copy = remote(source, target, *sems, "ctx", side)
             else:
-                begin(pltpu.make_async_copy(source, target, local.at[1, b]))
-    vector_next(4)
+                copy = pltpu.make_async_copy(source, target, local.at[0, kind])
+            copy.start()
+            started.append(copy)
+
+    def between():
+        for g in (1, 2):
+            send_ortho(g, 0, count, g, lambda n: others[(g - 1) * count + n])
+
+    size = count // 2
+    each = size // 4
+    chains = [Chain(b, size, factors, send_f, receive_f) for b in range(2)]
+
+    def keep(b, n, value):
+        factors[b * size + f * each + n] = value
+
+    for b in summed_polynomials(moments[:1], totals[:1], *gram_refs, keep, between):
+        chains[b].start(0)
+    for k in range(2):
+        for chain in chains:
+            chain.receive(k)
+            chain.start(k + 1)
+    for b, chain in enumerate(chains):
+        chain.receive(2)
+        send_ortho(0, b * size, size, 3 + b, lambda n: factors[n])
+    for chain in chains:
+        chain.end()
     for one in started:
         one.wait()
-    if with_rows:
-        sum_rows.end()
-
-
-def gradients_and_orthogonal(name, number, moments, totals, part=None, base=None, vector=None):
+
+
+def fits_planes(columns):
+    return lax.axis_size("fsdp") == 4 and lax.axis_size("ctx") == 4 and columns == 8 * HDIM
+
+
+def polynomials_over_planes(moment, total):
+    count = total.shape[1] // HDIM
+    flops = 12 * total.size * HDIM
+    shape = jax.ShapeDtypeStruct((count, HDIM, HDIM), f32)
+    grams = whole_call(gram_kernel, "grams", shape, moment, total, flops=flops)
+    summed = lax.psum(grams, "fsdp")
+    return whole_call(polynomial_kernel, "polynomials", shape, summed, flops=flops)
+
+
+def shared_by_cores(share):
+    other, t = swap_core(share), lax.axis_index("tp")
+    return jnp.stack([jnp.where(t == m, share, other) for m in range(2)])
+
+
+def feed_forward_slabs(moments, totals, share, part, base, vector):
     rows, columns = totals[0].shape
-    groups = len(totals)
-    count = groups * columns // HDIM
-    flops = 2 * 6 * rows * columns * HDIM * groups
+    if not fits_planes(columns):
+        factors = [polynomials_over_planes(m, v) for m, v in zip(moments, totals)]
+        summed = lax.psum(vector, ("fsdp", "ctx", "tp"))
+        blocks = [from_blocks(v) for v in totals]
+        return factors, blocks, shared_by_cores(share), base + collect(part), summed
+    count = 2 * columns // HDIM
     vmem = pl.BlockSpec(memory_space=pltpu.VMEM)
-    with_rows = part is not None
-    if lax.axis_size("fsdp") == 4 and lax.axis_size("ctx") == 4 and count in (8, 16) and groups == count // 8:
-        blocks = jax.ShapeDtypeStruct((4, rows // 4, columns), bf16)
-        anywhere = pl.BlockSpec(memory_space=pl.ANY)
-        out_shape, out_specs = [blocks] * (2 * groups), [anywhere] * (2 * groups)
-        operands, more = [*moments, *totals], []
-        if with_rows:
-            height, width = base.shape
-            half = height // 2
-            lines = vector.size // HDIM
-            operands += [part.reshape(2, 2, 2, half, width), base.reshape(2, half, width)]
-            operands.append(vector.reshape(lines, HDIM))
-            out_shape.append(jax.ShapeDtypeStruct((2, half, width), f32))
-            out_shape.append(jax.ShapeDtypeStruct((lines, HDIM), f32))
-            out_specs += [vmem, vmem]
-            more = [
-                pltpu.VMEM((5, lines, HDIM), f32),
-                pltpu.VMEM((5, lines, HDIM), f32),
-                pltpu.SemaphoreType.DMA((5,)),
-                pltpu.SemaphoreType.DMA((5,)),
-                *row_scratch(half, width),
-            ]
-        outs = pl.pallas_call(
-            lambda *refs: slab_kernel(groups, with_rows, *refs),
-            out_shape=out_shape,
-            in_specs=[vmem] * len(operands),
-            out_specs=out_specs,
-            scratch_shapes=[
-                pltpu.VMEM((count, HDIM, HDIM), f32),
-                pltpu.VMEM((3, count // 4, HDIM, HDIM), f32),
-                pltpu.VMEM((count, HDIM, HDIM), f32),
-                pltpu.VMEM((groups, 4, rows // 4, columns), bf16),
-                pltpu.SemaphoreType.DMA((groups + 2, 3)),
-                pltpu.SemaphoreType.DMA((groups + 2, 3)),
-                pltpu.SemaphoreType.DMA((4, 3)),
-                pltpu.SemaphoreType.DMA((4, 3)),
-                pltpu.SemaphoreType.DMA((2, 2)),
-                *more,
-            ],
-            compiler_params=pltpu.CompilerParams(
-                collective_id=number, has_side_effects=True, vmem_limit_bytes=40 << 20
-            ),
-            cost_estimate=pl.CostEstimate(
-                flops=3 * flops, bytes_accessed=100 << 20, transcendentals=0
-            ),
-            name=name,
-        )(*operands)
-        pairs = [(outs[g], outs[groups + g]) for g in range(groups)]
-        if with_rows:
-            return pairs, outs[-2].reshape(base.shape), outs[-1].reshape(vector.shape)
-        return pairs, None, None
-    pairs = []
-    shape = jax.ShapeDtypeStruct((count // groups, HDIM, HDIM), f32)
-    for moment, total in zip(moments, totals):
-        grams = whole_call(gram_kernel, "grams", shape, moment, total, flops=flops)
-        full = whole_call(
-            polynomial_kernel, "polynomials", shape, lax.psum(grams, "fsdp"), flops=flops
-        )
-        own = jax.ShapeDtypeStruct((rows, columns), bf16)
-        ortho = whole_call(apply_kernel, "apply", own, moment, total, full, flops=flops)
-        pairs.append((from_blocks(total), from_blocks(ortho)))
-    if with_rows:
-        return pairs, base + collect(part), lax.psum(vector, ("fsdp", "ctx", "tp"))
-    return pairs, None, None
+    anywhere = pl.BlockSpec(memory_space=pl.ANY)
+    block = jax.ShapeDtypeStruct((4, rows // 4, columns), bf16)
+    half, width = base.shape[0] // 2, base.shape[1]
+    lines = vector.size // HDIM
+    dma = pltpu.SemaphoreType.DMA
+    operands = [
+        *moments,
+        *totals,
+        part.reshape(2, 2, 2, half, width),
+        base.reshape(2, half, width),
+        vector.reshape(lines, HDIM),
+        share,
+    ]
+    factors, up, down, shared, summed, vector_sum = pl.pallas_call(
+        staged(feed_forward_kernel, 8, 8, 6),
+        out_shape=[
+            jax.ShapeDtypeStruct((count, HDIM, HDIM), f32),
+            block,
+            block,
+            jax.ShapeDtypeStruct((2, *share.shape), share.dtype),
+            jax.ShapeDtypeStruct((2, half, width), f32),
+            jax.ShapeDtypeStruct((lines, HDIM), f32),
+        ],
+        in_specs=[anywhere] * 8,
+        out_specs=[vmem, anywhere, anywhere, anywhere, vmem, vmem],
+        scratch_shapes=[
+            *slots_for(operands),
+            pltpu.VMEM((count, HDIM, HDIM), f32),
+            *[dma((2, 3))] * 2,
+            dma((1, 2)),
+            *[dma((1,))] * 3,
+            *[dma((4, 3))] * 2,
+            pltpu.VMEM((count, HDIM, HDIM), f32),
+            pltpu.VMEM((3, count // 4, HDIM, HDIM), f32),
+            *[dma((2, 3))] * 2,
+            *[pltpu.VMEM((5, lines, HDIM), f32)] * 2,
+            *[dma((5,))] * 2,
+            *row_scratch(half, width),
+        ],
+        compiler_params=pltpu.CompilerParams(
+            collective_id=4, has_side_effects=True, vmem_limit_bytes=56 << 20
+        ),
+        cost_estimate=pl.CostEstimate(
+            flops=24 * totals[0].size * HDIM, bytes_accessed=150 << 20, transcendentals=0
+        ),
+        name="feed_forward_slabs",
+    )(*operands)
+    return factors, [up, down], shared, summed.reshape(base.shape), vector_sum.reshape(vector.shape)
+
+
+def last_slabs(moments, totals, factors, share):
+    rows, columns = totals[0].shape
+    own = jax.ShapeDtypeStruct((rows, columns), bf16)
+    if not fits_planes(columns):
+        factors = [polynomials_over_planes(moments[0], totals[0]), *factors]
+        flops = 12 * totals[0].size * HDIM
+        orthos = [
+            from_blocks(whole_call(apply_kernel, "apply", own, m, v, p, flops=flops))
+            for m, v, p in zip(moments, totals, factors)
+        ]
+        return orthos, from_blocks(totals[0]), shared_by_cores(share)
+    count = columns // HDIM
+    anywhere = pl.BlockSpec(memory_space=pl.ANY)
+    block = jax.ShapeDtypeStruct((4, rows // 4, columns), bf16)
+    dma = pltpu.SemaphoreType.DMA
+    operands = [*moments, *totals, factors, share]
+    *orthos, grads, shared = pl.pallas_call(
+        staged(last_kernel, 8, 8, 5),
+        out_shape=[*[block] * 4, jax.ShapeDtypeStruct((2, *share.shape), share.dtype)],
+        in_specs=[anywhere] * 8,
+        out_specs=[anywhere] * 5,
+        scratch_shapes=[
+            *slots_for(operands),
+            pltpu.VMEM((count, HDIM, HDIM), f32),
+            pltpu.VMEM((3, 4, rows // 4, columns), bf16),
+            *[dma((5, 3))] * 2,
+            dma((1, 5)),
+            *[dma((1,))] * 3,
+            *[dma((4, 3))] * 2,
+            pltpu.VMEM((count, HDIM, HDIM), f32),
+            pltpu.VMEM((3, count // 4, HDIM, HDIM), f32),
+            *[dma((2, 3))] * 2,
+        ],
+        compiler_params=pltpu.CompilerParams(
+            collective_id=5, has_side_effects=True, vmem_limit_bytes=56 << 20
+        ),
+        cost_estimate=pl.CostEstimate(
+            flops=36 * totals[0].size * HDIM, bytes_accessed=100 << 20, transcendentals=0
+        ),
+        name="last_slabs",
+    )(*operands)
+    return orthos, grads, shared
 
 
 def pack(matrices):
@@ -745,7 +929,7 @@
         grid=(count,),
         in_specs=[*[pl.BlockSpec((1, rows, columns), lambda i: (i, 0, 0))] * 2, *specs, *specs],
         out_specs=[spec for spec in specs for _ in range(3)],
-        compiler_params=pltpu.CompilerParams(vmem_limit_bytes=32 << 20),
+        compiler_params=pltpu.CompilerParams(vmem_limit_bytes=56 << 20),
         cost_estimate=pl.CostEstimate(
             flops=4 * grads.size, bytes_accessed=24 * grads.size, transcendentals=0
         ),
@@ -895,18 +1079,18 @@
         [f32],
         3,
     )
-    grad_qkv_low, term_attn = [None, None], [None, None]
+    grad_qkv_low, term_qkv, term_out = [None, None], [None, None], [None, None]
     rows_for = attended_all
     for i in (1, 0):
         grad_context = mm(rows_for, attn_w[i][:, 3 * e :], (1, 0)).astype(bf16)
         grad_qkv_low[i] = attend_backward(qkv[i], grad_context, place)
-        term_attn[i] = jnp.concatenate(
-            [mm(xs, grad_qkv_low[i], (0, 0)), mm(rows_for, context[i], (0, 0))], axis=1
-        )
+        term_qkv[i] = mm(xs, grad_qkv_low[i], (0, 0))
+        term_out[i] = mm(rows_for, context[i], (0, 0))
         if i:
-            term_attn[i] = term_attn[i].astype(bf16)
-            rows_for = after(attended_all, term_attn[i])
-    attn_sum = pair_sum(term_attn)
+            term_qkv[i], term_out[i] = term_qkv[i].astype(bf16), term_out[i].astype(bf16)
+            rows_for = after(attended_all, term_qkv[i], term_out[i])
+    attn_sum = jnp.concatenate([pair_sum(term_qkv), pair_sum(term_out)], axis=1)
+    down_total, up_total = map(scatter_z, (down_sum, up_sum))
     *lows, attn_sum = lax.optimization_barrier((*grad_qkv_low, attn_sum))
     part = sum(mm(lows[i], attn_w[i][:, : 3 * e], (1, 1)) for i in cores).astype(bf16)
 
@@ -941,31 +1125,33 @@
     )
     flat = jnp.concatenate([bqv_all.reshape(-1), bup_all.reshape(-1), rest.reshape(-1)])
 
-    down_total, up_total, attn_total = map(scatter_z, (down_sum, up_sum, attn_sum))
+    attn_total = scatter_z(attn_sum)
     step_scale = matrix_rate * math.sqrt(width / HDIM)
-    (up_blocks, down_blocks), input_rows, flat = gradients_and_orthogonal(
-        "feed_forward_slabs",
-        4,
-        (moments[1], moments[2]),
-        (up_total, down_total),
-        part,
-        grad_first,
-        flat,
-    )
-    attn_total = after(attn_total, input_rows)
-    (attn_blocks,), *_ = gradients_and_orthogonal("attention_slabs", 5, moments[:1], (attn_total,))
-    up_done = finish("up_finish", step_scale, *up_blocks, (moment_up,), (w_up,))
-    down_done = finish("down_finish", step_scale, *down_blocks, (moment_down,), (w_down,))
+    factors, gradient_blocks, layer_out, input_rows, flat = feed_forward_slabs(
+        moments[1:], (up_total, down_total), after(out_rows, attn_sum), part, grad_first, flat
+    )
+    orthos, attn_gradients, input_grad = last_slabs(
+        moments, (attn_total, up_total, down_total), factors, input_rows
+    )
+    gradient_blocks, flat, orthos = lax.optimization_barrier((gradient_blocks, flat, orthos))
+    up_done, down_done = [
+        finish(name, step_scale, *operands)
+        for name, *operands in (
+            ("up_finish", gradient_blocks[0], orthos[1], (moment_up,), (w_up,)),
+            ("down_finish", gradient_blocks[1], orthos[2], (moment_down,), (w_down,)),
+        )
+    ]
     attn_done = finish(
-        "attention_finish", step_scale, *attn_blocks, (moment_qkv, moment_out), (w_qkv, w_out)
+        "attention_finish",
+        step_scale,
+        attn_gradients,
+        orthos[0],
+        (moment_qkv, moment_out),
+        (w_qkv, w_out),
     )
     grads, states, masters = [
         [*attn_done[k], *up_done[k], *down_done[k]] for k in range(3)
     ]
-
-    both = lambda own, other: jnp.stack([jnp.where(t == m, own, other) for m in range(2)])[:, None]
-    layer_out = both(out_rows, swap_core(out_rows))
-    input_grad = both(input_rows, swap_core(input_rows))
 
     cut = bqv_all.size
     cut_two = cut + bup_all.size
@@ -985,8 +1171,8 @@
         for v, s in zip((bias_qv, bias_up, bias_res, norm_gain, norm_shift), vector_states)
     ]
     return (
-        layer_out,
-        input_grad,
+        layer_out[:, None],
+        input_grad[:, None],
         *grads,
         *vector_grads,
         *states,

time: 792 us -> 763 us (0.963)
  local copies, waits for them, and re-layouts: 68.7 us -> 45.5 us
  other arithmetic: 44.3 us -> 30.1 us
  Pallas kernels: 408 us -> 422 us
    unnamed x188 -> x112, local copies, waits for them, and re-layouts: 43.2 us -> 15 us
    pallas_call x3, Pallas kernels: 9.37 us -> 18 us  [finish(): pl.pallas_call(kernel, out_shape=[jax.ShapeDtypeStruct(s.shape, f32) for...]
  transfers between devices with their start and end apart: 20 -> 19, of which waited for: 7 -> 6; matrix products, arithmetic and copies ran while one was open for 24% -> 24% of each run, Pallas kernels for 38% -> 37%
where the time goes in v3:
time: 763 us; the launch traced here: 759 us
  Pallas kernels  422 us (55%)
  matrix products  148 us (19%)
  local copies, waits for them, and re-layouts  45.5 us (6%)
  blocking collectives  44.8 us (6%)
  waiting for transfers between devices  41.7 us (5%)
  other arithmetic  30.1 us (4%)
  between operations  15.5 us (2%)
  starting transfers between devices  10.7 us (1%)
    pallas_call x3, Pallas kernels, exchange(): pl.pallas_call(staged(kernel, len(operands), n_in, 2 + len(out_types)), o...  221 us
    dot_general x24, matrix products, mm(): lax.dot_general(left, right, ((dims[:1], dims[1:]), ((), ())), preferred_...  148 us
    pallas_call x1, Pallas kernels, feed_forward_slabs(): pl.pallas_call(staged(feed_forward_kernel, 8, 8, 6), out_shape=[jax.Shape...  98.2 us
    pallas_call x1, Pallas kernels, last_slabs(): pl.pallas_call(staged(last_kernel, 8, 8, 5), out_shape=[*[block] * 4, jax...  53 us
    all_to_all x2, blocking collectives, over_ctx(): return lax.all_to_all(stack, 'ctx', split_axis=0, concat_axis=0, tiled=True)  44.8 us
    ppermute x4, waiting for transfers between devices, swap_ctx(): return lax.ppermute(value, 'ctx', xor_pairs(4, mask))  23 us
    pallas_call x2, Pallas kernels, attend_backward(): pl.pallas_call(lambda *refs: attend_back_kernel(256, heads, *refs), out_s...  21 us
    pallas_call x3, Pallas kernels, finish(): pl.pallas_call(kernel, out_shape=[jax.ShapeDtypeStruct(s.shape, f32) for...  18 us
  transfers between devices with their start and end apart: 19, of which 6 were waited for; matrix products, arithmetic and copies ran while one was open for 24% of the time, Pallas kernels for 37%

profile of v3, /device:TPU:0, one launch (start us, length us, event | category | flops | bytes accessed | tf_op | source)
XLA Modules:
  0.0 758.7 jit_solution(13825631785571516452)
XLA Ops:
  10.5 19.1 %all_to_all.15 = bf16[4,128,1024]{1,2,0:T(8,128)(2,1)S(1)} all-to-all(bf16[4,128,1024]{1,2,0:T(8,128)(2,1)S(1)} %bitcast.145), channel_id=1, replica_groups=mesh['fsdp'=4,'ctx'=4,'tp'=2] {'ctx'}, dimensions={0} | all-to-all | bytes 2097152 | tf_op jit(solution)/shard_map/all_to_all | solution.py:942
  32.6 2.7 convert_element_type.113
  39.7 14.9 %collective-permute-done = bf16[256,2048]{1,0:T(8,128)(2,1)} collective-permute-done((bf16[256,2048]{1,0:T(8,128)(2,1)S(1)}, bf16[256,2048]{1,0:T(8,128)(2,1)}, u32[]{:S(2)}, u32[]{:S(2)}) %collective-permute-start) | collective-permute-done | bytes 1048608 | tf_op jit(solution)/shard_map/ppermute | solution.py:38
  61.4 5.6 collective-permute-done.2
  71.6 25.7 %all_to_all.16 = bf16[4,128,2048]{1,2,0:T(8,128)(2,1)} all-to-all(bf16[4,128,2048]{1,2,0:T(8,128)(2,1)S(1)} %pad_maximum_fusion.2), channel_id=1, replica_groups=mesh['fsdp'=4,'ctx'=4,'tp'=2] {'ctx'}, dimensions={0} | all-to-all | bytes 4194304 | tf_op jit(solution)/shard_map/all_to_all | solution.py:942
  97.3 3.9 copy.80
  101.2 3.1 fusion.36
  118.6 3.5 pad_maximum_fusion.1
  126.7 2.6 collective-permute-done.5
  129.3 6.6 add_convert_fusion.8.refs_0_.refs_1_.refs_2_
  135.9 5.6 attend_forward.2
  141.6 2.7 fusion.28
  144.4 5.3 add_convert_fusion.7.refs_0_.refs_1_.refs_2_
  149.7 5.5 attend_forward.3
  155.2 4.7 add_convert_fusion.5
  159.9 73.9 %first_rows.1 = (bf16[4,2,128,2048]{3,2,1,0:T(8,128)(2,1)}, f32[2,128,2048]{2,1,0:T(8,128)}, f32[2,128,2048]{2,1,0:T(8,128)}, f32[8,2048]{1,0:T(8,128)}) custom-call(bf16[2,2,2,128,2048]{4,3,2,1,0:T(8,128)(2,1)} %bitcast.136, bf16[2,128,2048]{2,1,0:T(8,128)(2,1)} %bitcast.138, f32[1,2048]{1,0:T(1,128)} %get-tuple-element.271.refs_2_, ...), custom_call_target="tpu_custom_call" | custom-call | flops 31457280 | bytes 136314880 | tf_op jit(solution)/shard_map/first_rows/pallas_call | solution.py:290
  234.0 4.7 all-to-all-start.2
  238.9 11.5 %multiply_convert_fusion.1 = (bf16[1024,1024]{1,0:T(8,128)(2,1)}, f32[1024,1024]{1,0:T(8,128)}) fusion(f32[1024]{0:T(1024)S(1)} %dynamic_slice.28, bf16[1024,2048]{1,0:T(8,128)(2,1)} %bitcast.177, bf16[2048,1024]{1,0:T(8,128)(2,1)} %all-gather.6.cloned.1.call-done), kind=kOutput, calls=%fused_computation.30 | convolution fusion | flops 4305453056 | bytes 14684160 | tf_op jit(solution)/shard_map/dot_general | solution.py:46
  250.5 9.4 %multiply_convert_fusion = (bf16[1024,1024]{1,0:T(8,128)(2,1)}, f32[1024,1024]{1,0:T(8,128)}) fusion(f32[1024]{0:T(1024)S(1)} %slice.237, bf16[1024,2048]{1,0:T(8,128)(2,1)S(1)} %bitcast.178, bf16[2048,1024]{1,0:T(8,128)(2,1)} %collective-permute-done.6), kind=kOutput, calls=%fused_computation.29 | convolution fusion | flops 4305453056 | bytes 14684160 | tf_op jit(solution)/shard_map/dot_general | solution.py:46
  259.8 14.6 %all-gather.8.cloned.1.call-done = bf16[2048,1024]{1,0:T(8,128)(2,1)} async-done(((bf16[512,1024]{1,0:T(8,128)(2,1)}), bf16[2048,1024]{1,0:T(8,128)(2,1)}) %all-gather.8.cloned.1.call-update) | async-done | bytes 4194320 | tf_op jit(solution)/shard_map/all_gather | solution.py:1000
  278.0 7.1 fusion.46
  285.2 6.6 add_convert_fusion.4
  291.8 73.9 %second_rows.1 = (bf16[4,2,128,2048]{3,2,1,0:T(8,128)(2,1)}, bf16[2,128,2048]{2,1,0:T(8,128)(2,1)}, f32[2,128,2048]{2,1,0:T(8,128)}, f32[8,2048]{1,0:T(8,128)}) custom-call(bf16[2,2,2,128,2048]{4,3,2,1,0:T(8,128)(2,1)} %bitcast.143, f32[2,128,2048]{2,1,0:T(8,128)} %get-tuple-element.98.refs_1_, bf16[2,128,2048]{2,1,0:T(8,128)(2,1)} %bitcast.148, ...), custom_call_target="tpu_custom_call" | custom-call | flops 31457280 | bytes 136314880 | tf_op jit(solution)/shard_map/second_rows/pallas_call | solution.py:290
  365.8 7.6 convolution_convert_fusion.1
  373.4 4.8 fusion.47
  378.3 8.0 %fusion.6 = bf16[1024,1024]{1,0:T(8,128)(2,1)} fusion(f32[1024,1024]{1,0:T(8,128)S(1)} %copy-done.46, f32[1024]{0:T(1024)S(1)} %dynamic_slice.28, bf16[1024,2048]{1,0:T(8,128)(2,1)S(1)} %bitcast.184, bf16[2048,1024]{1,0:T(8,128)(2,1)S(1)} %copy-done.42), kind=kOutput, calls=%fused_computation.18 | convolution fusion | flops 4316987392 | bytes 14684160 | tf_op jit(solution)/shard_map/dot_general | solution.py:46
  386.3 5.8 add_convert_fusion.3
  392.2 11.7 %convert_reduce_fusion = (f32[1024]{0:T(1024)S(1)}, bf16[1024,1024]{1,0:T(8,128)(2,1)S(1)}) fusion(f32[1024,1024]{1,0:T(8,128)} %get-tuple-element.287, f32[1024]{0:T(1024)S(1)} %slice.237, bf16[1024,2048]{1,0:T(8,128)(2,1)} %bitcast.182, bf16[2048,1024]{1,0:T(8,128)(2,1)} %copy-done.43), kind=kOutput, calls=%fused_computation.27 | convolution fusion | flops 4319083520 | bytes 14688256 | tf_op jit(solution)/shard_map/dot_general | solution.py:46
  403.9 6.4 convolution_convert_fusion
  410.8 9.2 %fusion.48 = f32[1024,2048]{1,0:T(8,128)} fusion(bf16[1024,1024]{1,0:T(8,128)(2,1)S(1)} %get-tuple-element.250, bf16[2048,1024]{1,0:T(8,128)(2,1)} %collective-permute-done.6), kind=kOutput, calls=%fused_computation.118 | convolution fusion | flops 4294967296 | bytes 14680064 | tf_op jit(solution)/shard_map/dot_general | solution.py:46
  420.0 8.4 %add_convert_fusion.2 = bf16[1024,2048]{1,0:T(8,128)(2,1)} fusion(f32[1024,2048]{1,0:T(8,128)} %fusion.48, bf16[1024,1024]{1,0:T(8,128)(2,1)S(1)} %copy-done.15, bf16[2048,1024]{1,0:T(8,128)(2,1)S(1)} %copy-done.39), kind=kOutput, calls=%fused_computation.3 | convolution fusion | flops 4299161600 | bytes 18874368 | tf_op jit(solution)/shard_map/dot_general | solution.py:46
  428.4 6.4 add_convert_fusion.1
  434.9 73.0 %third_rows.1 = (bf16[4,2,128,2048]{3,2,1,0:T(8,128)(2,1)}, f32[2,128,2048]{2,1,0:T(8,128)}, f32[8,2048]{1,0:T(8,128)}) custom-call(bf16[2,2,2,128,2048]{4,3,2,1,0:T(8,128)(2,1)} %bitcast.142, f32[2,128,2048]{2,1,0:T(8,128)} %get-tuple-element.98.refs_1_, f32[2,128,2048]{2,1,0:T(8,128)} %get-tuple-element.110.refs_2_, ...), custom_call_target="tpu_custom_call" | custom-call | flops 31457280 | bytes 136314880 | tf_op jit(solution)/shard_map/third_rows/pallas_call | solution.py:290
  507.9 3.7 convolution_convert_fusion.5.refs_3_
  511.6 10.6 %attend_backward.2 = bf16[1024,768]{1,0:T(8,128)(2,1)S(1)} custom-call(bf16[1024,768]{1,0:T(8,128)(2,1)S(1)} %add_convert_fusion.7.refs_0_.refs_1_.refs_2_, bf16[1024,768]{1,0:T(8,128)(2,1)S(1)} %add_convert_fusion.7.refs_0_.refs_1_.refs_2_, bf16[1024,768]{1,0:T(8,128)(2,1)S(1)} %add_convert_fusion.7.refs_0_.refs_1_.refs_2_, ...), custom_call_target="tpu_custom_call" | custom-call | flops 2684354560 | bytes 3670016 | tf_op jit(solution)/shard_map/attend_backward/pallas_call | solution.py:426
  522.3 5.0 convolution_convert_fusion.2
  531.8 10.4 %attend_backward.3 = bf16[1024,768]{1,0:T(8,128)(2,1)S(1)} custom-call(bf16[1024,768]{1,0:T(8,128)(2,1)S(1)} %copy-done.3, bf16[1024,768]{1,0:T(8,128)(2,1)S(1)} %copy-done.3, bf16[1024,768]{1,0:T(8,128)(2,1)S(1)} %copy-done.3, bf16[1024,256]{1,0:T(8,128)(2,1)S(1)} %convolution_convert_fusion.4.refs_3_, s32[1024,1]{1,0:T(8,128)S(1)} %bitcast.130, ...), custom_call_target="tpu_custom_call" | custom-call | flops 2684354560 | bytes 3670016 | tf_op jit(solution)/shard_map/attend_backward/pallas_call | solution.py:426
  543.6 5.2 add_convert_fusion.6
  548.9 2.6 pad_maximum_fusion
  551.5 3.7 fusion.35
  560.8 5.3 fusion.17
  566.1 7.4 add_convert_fusion
  573.6 98.2 %feed_forward_slabs.1 = (f32[16,128,128]{2,1,0:T(8,128)}, bf16[4,128,1024]{2,1,0:T(8,128)(2,1)}, bf16[4,128,1024]{2,1,0:T(8,128)(2,1)}, bf16[2,256,2048]{2,1,0:T...) custom-call(bf16[512,1024]{1,0:T(8,128)(2,1)} %get-tuple-element.253.refs_0_.refs_1_, ...), custom_call_target="tpu_custom_call" | custom-call | flops 1610612736 | bytes 157286400 | tf_op jit(solution)/shard_map/feed_forward_slabs/pallas_call | solution.py:803
  671.9 53.0 %last_slabs.1 = (bf16[4,128,1024]{2,1,0:T(8,128)(2,1)}, bf16[4,128,1024]{2,1,0:T(8,128)(2,1)}, bf16[4,128,1024]{2,1,0:T(8,128)(2,1)}, bf16[4,128,1024]{2,1,0:T(8,128)(2,1)}, f32[2,256,2048]{2,1,0:T(8,128)}) custom-call(bf16[512,1024]{1,0:T(8,128)(2,1)} %get-tuple-element.251.refs_0_, bf16[512,1024]{1,0:T(8,128)(2,1)} %get-tuple-element.253.refs_0_.refs_1_, ...), custom_call_target="tpu_custom_call" | custom-call | flops 2415919104 | bytes 104857600 | tf_op jit(solution)/shard_map/last_slabs/pallas_call | solution.py:856
  725.1 5.9 down_finish.1
  731.0 5.8 up_finish.1
  736.9 6.3 attention_finish.1
  746.4 3.3 copy.110
  (226 shorter events, 62.1 us)
Async XLA Ops:
  7.2 23.8 %copy-start = (bf16[2,1,256,2048]{3,2,1,0:T(8,128)(2,1)S(1)}, bf16[2,1,256,2048]{3,2,1,0:T(8,128)(2,1)}, u32[]{:S(2)}) copy-start(bf16[2,1,256,2048]{3,2,1,0:T(8,128)(2,1)} %param.21) | copy-start | bytes 6291460
  7.2 114.9 %all-gather.4.cloned.1.call-start = ((), (), s32[]{:S(2)}) async-start(), calls=%async_computation.6 | async-start | bytes 5242880 | tf_op jit(solution)/shard_map/all_gather | solution.py:1000
  30.9 203.0 %all-gather.6.cloned.1.call-start = ((), (), s32[]{:S(2)}) async-start(), calls=%async_computation.7 | async-start | bytes 5242880 | tf_op jit(solution)/shard_map/all_gather | solution.py:1000
  31.1 23.5 %collective-permute-start = (bf16[256,2048]{1,0:T(8,128)(2,1)S(1)}, bf16[256,2048]{1,0:T(8,128)(2,1)}, u32[]{:S(2)}, u32[]{:S(2)}) collective-permute-start(bf16[256,2048]{1,0:T(8,128)(2,1)S(1)} %fusion.89), channel_id=1, source_target_pairs={{0,2},{2,0},{4,6},{6,4},{1,3},{3,1},{5,7},{7,5},{8,10},{10,8},{12,... | collective-permute-start | bytes 3145736 | tf_op jit(solution)/shard_map/ppermute | solution.py:38
  32.1 25.1 %collective-permute-start.1 = (bf16[256,2048]{1,0:T(8,128)(2,1)S(1)}, bf16[256,2048]{1,0:T(8,128)(2,1)}, u32[]{:S(2)}, u32[]{:S(2)}) collective-permute-start(bf16[256,2048]{1,0:T(8,128)(2,1)S(1)} %fusion.89), channel_id=1, source_target_pairs={{0,4},{2,6},{4,0},{6,2},{1,5},{3,7},{5,1},{7,3},{8,12},{10,14},{12... | collective-permute-start | bytes 3145736 | tf_op jit(solution)/shard_map/ppermute | solution.py:38
  55.7 11.3 %collective-permute-start.2 = (bf16[128,2048]{1,0:T(8,128)(2,1)S(1)}, bf16[128,2048]{1,0:T(8,128)(2,1)S(1)}, u32[]{:S(2)}, u32[]{:S(2)}) collective-permute-start(bf16[128,2048]{1,0:T(8,128)(2,1)S(1)} %slice.227), channel_id=1, source_target_pairs={{0,4},{2,6},{4,0},{6,2},{1,5},{3,7},{5,1},{7,3},{8,12},{10,14},{12... | collective-permute-start | bytes 1572872 | tf_op jit(solution)/shard_map/ppermute | solution.py:38
  58.2 11.3 %collective-permute-start.3 = (bf16[128,2048]{1,0:T(8,128)(2,1)S(1)}, bf16[128,2048]{1,0:T(8,128)(2,1)S(1)}, u32[]{:S(2)}, u32[]{:S(2)}) collective-permute-start(bf16[128,2048]{1,0:T(8,128)(2,1)S(1)} %slice.228), channel_id=1, source_target_pairs={{0,2},{2,0},{4,6},{6,4},{1,3},{3,1},{5,7},{7,5},{8,10},{10,8},{12,... | collective-permute-start | bytes 1572872 | tf_op jit(solution)/shard_map/ppermute | solution.py:38
  101.2 8.0 %copy-start.14 = (f32[1024,128]{1,0:T(8,128)S(1)}, f32[1024,128]{1,0:T(8,128)}, u32[]{:S(2)}) copy-start(f32[1024,128]{1,0:T(8,128)} %refs_1_.3) | copy-start | bytes 1572868
  104.3 170.1 %all-gather.8.cloned.1.call-start = ((), (), s32[]{:S(2)}) async-start(), calls=%async_computation.8 | async-start | bytes 5242880 | tf_op jit(solution)/shard_map/all_gather | solution.py:1000
  118.6 7.2 copy-start.26
  118.6 7.2 copy-start.28
  122.1 22.2 %collective-permute-start.4 = (bf16[2048,1024]{1,0:T(8,128)(2,1)}, bf16[2048,1024]{1,0:T(8,128)(2,1)}, u32[]{:S(2)}, u32[]{:S(2)}) collective-permute-start(bf16[2048,1024]{1,0:T(8,128)(2,1)} %all-gather.4.cloned.1.call-done), channel_id=1, source_target_pairs={{0,1},{1,0},{2,3},{3,2},{4,5},{5,4},{6,7},{7,6},{8,9},{9,8},{10,11... | collective-permute-start | bytes 12582920 | tf_op jit(solution)/shard_map/ppermute | solution.py:34
  122.9 6.4 collective-permute-start.5
  135.9 8.4 %copy-start.2 = (bf16[1024,768]{1,0:T(8,128)(2,1)}, bf16[1024,768]{1,0:T(8,128)(2,1)S(1)}, u32[]{:S(2)}) copy-start(bf16[1024,768]{1,0:T(8,128)(2,1)S(1)} %add_convert_fusion.8.refs_0_.refs_1_.refs_2_) | copy-start | bytes 4718596
  233.9 16.6 %collective-permute-start.6 = (bf16[2048,1024]{1,0:T(8,128)(2,1)}, bf16[2048,1024]{1,0:T(8,128)(2,1)}, u32[]{:S(2)}, u32[]{:S(2)}) collective-permute-start(bf16[2048,1024]{1,0:T(8,128)(2,1)} %all-gather.6.cloned.1.call-done), channel_id=1, source_target_pairs={{0,1},{1,0},{2,3},{3,2},{4,5},{5,4},{6,7},{7,6},{8,9},{9,8},{10,11... | collective-permute-start | bytes 12582920 | tf_op jit(solution)/shard_map/ppermute | solution.py:34
  234.0 41.8 %all-to-all-start.2 = ((bf16[4,128,3072]{2,1,0:T(8,128)(2,1)}), bf16[4,128,3072]{2,1,0:T(8,128)(2,1)}, u32[]{:S(2)}, u32[]{:S(2)}) async-start(bf16[4,128,3072]{2,1,0:T(8,128)(2,1)} %pad_maximum_fusion.1), calls=%async_computation.2 | async-start | bytes 6291456 | tf_op jit(solution)/shard_map/all_to_all | solution.py:942
  238.6 334.9 %reduce-scatter.6.cloned.1.call-start = ((), (), s32[]{:S(2)}) async-start(), calls=%async_computation.10 | async-start | bytes 5242880 | tf_op jit(solution)/shard_map/reduce_scatter | solution.py:1056
  238.9 11.6 %copy-start.40 = (bf16[4,2,128,2048]{3,2,1,0:T(8,128)(2,1)S(1)}, bf16[4,2,128,2048]{3,2,1,0:T(8,128)(2,1)}, u32[]{:S(2)}) copy-start(bf16[4,2,128,2048]{3,2,1,0:T(8,128)(2,1)} %get-tuple-element.94) | copy-start | bytes 12582916
  275.7 9.5 %collective-permute-start.7 = (bf16[2048,1024]{1,0:T(8,128)(2,1)}, bf16[2048,1024]{1,0:T(8,128)(2,1)S(1)}, u32[]{:S(2)}, u32[]{:S(2)}) collective-permute-start(bf16[2048,1024]{1,0:T(8,128)(2,1)} %all-gather.8.cloned.1.call-done), channel_id=1, source_target_pairs={{0,1},{1,0},{2,3},{3,2},{4,5},{5,4},{6,7},{7,6},{8,9},{9,8},{10,11... | collective-permute-start | bytes 12582920 | tf_op jit(solution)/shard_map/ppermute | solution.py:34
  278.0 7.2 copy-start.48
  365.7 7.6 %copy-start.44 = (bf16[4,2,128,2048]{3,2,1,0:T(8,128)(2,1)S(1)}, bf16[4,2,128,2048]{3,2,1,0:T(8,128)(2,1)}, u32[]{:S(2)}) copy-start(bf16[4,2,128,2048]{3,2,1,0:T(8,128)(2,1)} %get-tuple-element.99) | copy-start | bytes 12582916
  365.8 7.6 %copy-start.47 = (bf16[1024,1024]{1,0:T(8,128)(2,1)S(1)}, bf16[1024,1024]{1,0:T(8,128)(2,1)}, u32[]{:S(2)}) copy-start(bf16[1024,1024]{1,0:T(8,128)(2,1)} %get-tuple-element.284) | copy-start | bytes 6291460
  378.2 8.1 %collective-permute-start.8 = (bf16[2048,1024]{1,0:T(8,128)(2,1)S(1)}, bf16[2048,1024]{1,0:T(8,128)(2,1)}, u32[]{:S(2)}, u32[]{:S(2)}) collective-permute-start(bf16[2048,1024]{1,0:T(8,128)(2,1)S(1)} %convolution_convert_fusion.1), channel_id=1, source_target_pairs={{0,1},{1,0},{2,3},{3,2},{4,5},{5,4},{6,7},{7,6},{8,9},{9,8},{10,11... | collective-permute-start | bytes 12582920 | tf_op jit(solution)/shard_map/ppermute | solution.py:34
  392.2 181.4 %reduce-scatter.4.cloned.1.call-start = ((), (), s32[]{:S(2)}) async-start(), calls=%async_computation.9 | async-start | bytes 5242880 | tf_op jit(solution)/shard_map/reduce_scatter | solution.py:1056
  392.2 11.7 %copy-start.41 = (bf16[4,2,128,2048]{3,2,1,0:T(8,128)(2,1)S(1)}, bf16[4,2,128,2048]{3,2,1,0:T(8,128)(2,1)}, u32[]{:S(2)}) copy-start(bf16[4,2,128,2048]{3,2,1,0:T(8,128)(2,1)} %get-tuple-element.94) | copy-start | bytes 12582916
  410.4 9.7 %copy-start.15 = (bf16[1024,1024]{1,0:T(8,128)(2,1)S(1)}, bf16[1024,1024]{1,0:T(8,128)(2,1)}, u32[]{:S(2)}) copy-start(bf16[1024,1024]{1,0:T(8,128)(2,1)} %fusion.6) | copy-start | bytes 6291460
  410.4 9.7 %copy-start.39 = (bf16[2048,1024]{1,0:T(8,128)(2,1)S(1)}, bf16[2048,1024]{1,0:T(8,128)(2,1)}, u32[]{:S(2)}) copy-start(bf16[2048,1024]{1,0:T(8,128)(2,1)} %all-gather.6.cloned.1.call-done) | copy-start | bytes 12582916
  410.4 18.1 %collective-permute-start.9 = (bf16[2048,1024]{1,0:T(8,128)(2,1)}, bf16[2048,1024]{1,0:T(8,128)(2,1)S(1)}, u32[]{:S(2)}, u32[]{:S(2)}) collective-permute-start(bf16[2048,1024]{1,0:T(8,128)(2,1)} %convolution_convert_fusion), channel_id=1, source_target_pairs={{0,1},{1,0},{2,3},{3,2},{4,5},{5,4},{6,7},{7,6},{8,9},{9,8},{10,11... | collective-permute-start | bytes 12582920 | tf_op jit(solution)/shard_map/ppermute | solution.py:34
  434.8 237.0 %reduce-scatter.8.cloned.1.call-start = ((), (), s32[]{:S(2)}) async-start(), calls=%async_computation.11 | async-start | bytes 5242880 | tf_op jit(solution)/shard_map/reduce_scatter | solution.py:1056
  511.6 10.6 %copy-start.18 = (bf16[1024,2048]{1,0:T(8,128)(2,1)S(1)}, bf16[1024,2048]{1,0:T(8,128)(2,1)}, u32[]{:S(2)}) copy-start(bf16[1024,2048]{1,0:T(8,128)(2,1)} %copy-done.16) | copy-start | bytes 12582916
  527.3 16.3 %collective-permute-start.10 = (bf16[2048,768]{1,0:T(8,128)(2,1)}, bf16[2048,768]{1,0:T(8,128)(2,1)}, u32[]{:S(2)}, u32[]{:S(2)}) collective-permute-start(bf16[2048,768]{1,0:T(8,128)(2,1)} %convolution_convert_fusion.2), channel_id=1, source_target_pairs={{0,1},{1,0},{2,3},{3,2},{4,5},{5,4},{6,7},{7,6},{8,9},{9,8},{10,11... | collective-permute-start | bytes 9437192 | tf_op jit(solution)/shard_map/ppermute | solution.py:34
  528.7 13.5 %collective-permute-start.11 = (bf16[2048,256]{1,0:T(8,128)(2,1)S(1)}, bf16[2048,256]{1,0:T(8,128)(2,1)S(1)}, u32[]{:S(2)}, u32[]{:S(2)}) collective-permute-start(bf16[2048,256]{1,0:T(8,128)(2,1)S(1)} %convolution_convert_fusion.3), channel_id=1, source_target_pairs={{0,1},{1,0},{2,3},{3,2},{4,5},{5,4},{6,7},{7,6},{8,9},{9,8},{10,11... | collective-permute-start | bytes 3145736 | tf_op jit(solution)/shard_map/ppermute | solution.py:34
  531.7 10.4 %copy-start.5 = (bf16[1024,256]{1,0:T(8,128)(2,1)S(1)}, bf16[1024,256]{1,0:T(8,128)(2,1)}, u32[]{:S(2)}) copy-start(bf16[1024,256]{1,0:T(8,128)(2,1)} %copy-done.4) | copy-start | bytes 1572868
  551.5 7.1 copy-start.9
  671.9 53.0 %copy-start.19 = (f32[192,128]{1,0:T(8,128)S(1)}, f32[192,128]{1,0:T(8,128)}, u32[]{:S(2)}) copy-start(f32[192,128]{1,0:T(8,128)} %get-tuple-element.129) | copy-start | bytes 294916
  725.0 18.2 %copy-start.22 = (f32[1,4096]{1,0:T(1,128)}, f32[1,4096]{1,0:T(1,128)S(1)}, u32[]{:S(2)}) copy-start(f32[1,4096]{1,0:T(1,128)S(1)} %constant_dynamic-slice_fusion.1) | copy-start | bytes 49156
  725.0 18.8 %copy-start.23 = (f32[2,2048]{1,0:T(2,128)}, f32[2,2048]{1,0:T(2,128)S(1)}, u32[]{:S(2)}) copy-start(f32[2,2048]{1,0:T(2,128)S(1)} %slice.220) | copy-start | bytes 49156
  725.0 19.4 %copy-start.24 = (f32[2,2048]{1,0:T(2,128)}, f32[2,2048]{1,0:T(2,128)S(1)}, u32[]{:S(2)}) copy-start(f32[2,2048]{1,0:T(2,128)S(1)} %slice.222) | copy-start | bytes 49156
  725.1 20.0 %copy-start.25 = (f32[2,2048]{1,0:T(2,128)}, f32[2,2048]{1,0:T(2,128)S(1)}, u32[]{:S(2)}) copy-start(f32[2,2048]{1,0:T(2,128)S(1)} %slice.224) | copy-start | bytes 49156
  736.8 7.0 copy-start.21
  736.8 7.0 copy-start.34
  736.8 7.7 %copy-start.27 = (f32[2,2048]{1,0:T(2,128)S(1)}, f32[2,2048]{1,0:T(2,128)}, u32[]{:S(2)}) copy-start(f32[2,2048]{1,0:T(2,128)} %param.31) | copy-start | bytes 49156
  736.8 7.6 %copy-start.35 = (f32[2,2048]{1,0:T(2,128)S(1)}, f32[2,2048]{1,0:T(2,128)}, u32[]{:S(2)}) copy-start(f32[2,2048]{1,0:T(2,128)} %param.40) | copy-start | bytes 49156
  736.8 8.3 %copy-start.29 = (f32[2,2048]{1,0:T(2,128)S(1)}, f32[2,2048]{1,0:T(2,128)}, u32[]{:S(2)}) copy-start(f32[2,2048]{1,0:T(2,128)} %param.32) | copy-start | bytes 49156
  736.9 8.3 %copy-start.36 = (f32[2,2048]{1,0:T(2,128)S(1)}, f32[2,2048]{1,0:T(2,128)}, u32[]{:S(2)}) copy-start(f32[2,2048]{1,0:T(2,128)} %param.41) | copy-start | bytes 49156
  736.9 8.9 %copy-start.32 = (f32[2,1024]{1,0:T(2,128)S(1)}, f32[2,1024]{1,0:T(2,128)}, u32[]{:S(2)}) copy-start(f32[2,1024]{1,0:T(2,128)} %param.28) | copy-start | bytes 24580
  736.9 8.9 %copy-start.37 = (f32[2,1024]{1,0:T(2,128)S(1)}, f32[2,1024]{1,0:T(2,128)}, u32[]{:S(2)}) copy-start(f32[2,1024]{1,0:T(2,128)} %param.37) | copy-start | bytes 24580
  736.9 12.8 %copy-start.13 = (f32[2,256,2048]{2,1,0:T(8,128)S(1)}, f32[2,256,2048]{2,1,0:T(8,128)}, u32[]{:S(2)}) copy-start(f32[2,256,2048]{2,1,0:T(8,128)} %get-tuple-element.125) | copy-start | bytes 12582916
  (20 other events, 93.9 us)
Sparse Core Ops, SparseCore 0:
  31.0 80.4 all-gather.3
  113.7 79.2 all-gather.5
  195.2 79.2 all-gather.7
  392.3 77.0 reduce-scatter.5
  471.7 77.2 reduce-scatter.3
  551.6 101.2 reduce-scatter.7

commit v4 on v3

--- a/solution.py
+++ b/solution.py
@@ -514,6 +514,23 @@
         out_ref[n] = total
 
 
+def fold(symmetric):
+    half = symmetric.shape[0] // 2
+    last = symmetric[half:, half:]
+    sides = jnp.concatenate([last[: half // 2], last[half // 2 :]], axis=1)
+    return jnp.concatenate([symmetric[:half], sides], axis=0)
+
+
+def unfold(folded):
+    half = folded.shape[1] // 2
+    top, sides = folded[:half], folded[half:]
+    last = jnp.concatenate([sides[:, :half], sides[:, half:]], axis=0)
+    return jnp.concatenate([top, jnp.concatenate([top[:, half:].T, last], axis=1)], axis=0)
+
+
+FOLDED = 3 * HDIM // 4
+
+
 def summed_polynomials(moments, totals, grams, pieces, send, receive, keep, between):
     each_group = totals[0].shape[1] // HDIM
     count = grams.shape[0]
@@ -527,7 +544,7 @@
         first = b * size
         for n in range(first, first + size):
             g = n // each_group
-            grams[n] = gram_of(moments[g], totals[g], n % each_group)
+            grams[n] = fold(gram_of(moments[g], totals[g], n % each_group))
         copies.append([])
         for i in (1, 2, 3):
             one = remote(
@@ -546,8 +563,8 @@
         for i in (1, 2, 3):
             copies[b][i - 1].wait()
             sums = [s + pieces[i - 1, b * each + n] for n, s in enumerate(sums)]
-        for n, value in enumerate(polynomial(sums)):
-            keep(b, n, value)
+        for n, value in enumerate(polynomial([unfold(v) for v in sums])):
+            keep(b, n, fold(value))
         yield b
 
 
@@ -626,11 +643,12 @@
 
 
 def feed_forward_kernel(given, ready, *refs):
-    moments, totals, (part, base, vector), refs = refs[:2], refs[2:4], refs[4:7], refs[7:]
-    share, refs = refs[0], refs[1:]
+    moments, totals, (base, vector, share), refs = refs[:2], refs[2:4], refs[4:7], refs[7:]
+    grads_low, weights, refs = refs[:2], refs[2:4], refs[4:]
     (out, *grads), (shared, summed, vector_out), refs = refs[:3], refs[3:6], refs[6:]
     factors, send_c, receive_c, local, send_t, receive_t, local_t, send_f, receive_f = refs[:9]
-    gram_refs, (sent_v, got_v, send_v, receive_v), row_refs = refs[9:13], refs[13:17], refs[17:]
+    gram_refs, (sent_v, got_v, send_v, receive_v) = refs[9:13], refs[13:17]
+    part, row_refs = refs[17], refs[18:]
     c, f, t = (lax.axis_index(axis) for axis in ("ctx", "fsdp", "tp"))
     partners = [
         ("tp", 1 - t),
@@ -656,8 +674,21 @@
             vector_out[...] = sent_v[k] + got_v[k]
 
     sum_rows = RowSums(part, *row_refs)
-    sum_rows.first(given[4])
-    ready(0, 8)
+    half, width = part.shape[3:]
+    depth = grads_low[0].shape[1]
+    block = width // 4
+
+    def make_part(k, carry):
+        rows = pl.ds(pl.multiple_of(k * 2 * half, 2 * half), 2 * half)
+        for n in range(4):
+            column = pl.ds(n * block, block)
+            value = sum(mm(grads_low[i][rows, :], weights[i][column, :depth], (1, 1)) for i in range(2))
+            value = value.astype(bf16)
+            part[k // 2, k % 2, 0, :, column] = value[:half]
+            part[k // 2, k % 2, 1, :, column] = value[half:]
+        return carry
+
+    ready(0, 7)
     started = rows_to_owners(totals, grads, send_c, receive_c, local)
     started += share_core(share, shared, send_t, receive_t, local_t)
     sent_v[0] = vector[...]
@@ -670,12 +701,16 @@
         factors[b * size + f * each + n] = value
 
     def between():
+        ready(7, 11)
+        lax.fori_loop(0, 4, make_part, 0)
+        sum_rows.first(part)
         vector_next(0)
-        sum_rows.second()
-        vector_next(1)
 
     for b in summed_polynomials(moments, totals, *gram_refs, keep, between):
         chains[b].start(0)
+        if b == 0:
+            vector_next(1)
+            sum_rows.second()
     vector_next(2)
     for j in range(sum_rows.pieces):
         span, total = sum_rows.third(j)
@@ -714,6 +749,7 @@
     started += share_core(share, shared, send_t, receive_t, local_t)
 
     def send_ortho(g, first, size, kind, factor):
+        made = {n: unfold(factor(n)) for n in range(first, first + size)}
         wide = pl.ds(first * HDIM, size * HDIM)
         for i in (3, 1, 2, 0):
             side = (c + i) % 4
@@ -723,7 +759,7 @@
                 state = decay_rate * moments[g][span, column].astype(f32)
                 state = state + totals[g][span, column].astype(f32)
                 stage[g, i, :, column] = jnp.dot(
-                    state, factor(n), precision=highest, preferred_element_type=f32
+                    state, made[n], precision=highest, preferred_element_type=f32
                 ).astype(bf16)
             source, target = stage.at[g, i, :, wide], orthos[g].at[c, :, wide]
             if i:
@@ -778,12 +814,14 @@
     return jnp.stack([jnp.where(t == m, share, other) for m in range(2)])
 
 
-def feed_forward_slabs(moments, totals, share, part, base, vector):
+def feed_forward_slabs(moments, totals, share, grads_low, weights, base, vector):
     rows, columns = totals[0].shape
     if not fits_planes(columns):
         factors = [polynomials_over_planes(m, v) for m, v in zip(moments, totals)]
         summed = lax.psum(vector, ("fsdp", "ctx", "tp"))
         blocks = [from_blocks(v) for v in totals]
+        depth = grads_low[0].shape[1]
+        part = sum(mm(g, w[:, :depth], (1, 1)) for g, w in zip(grads_low, weights)).astype(bf16)
         return factors, blocks, shared_by_cores(share), base + collect(part), summed
     count = 2 * columns // HDIM
     vmem = pl.BlockSpec(memory_space=pltpu.VMEM)
@@ -795,35 +833,37 @@
     operands = [
         *moments,
         *totals,
-        part.reshape(2, 2, 2, half, width),
         base.reshape(2, half, width),
         vector.reshape(lines, HDIM),
         share,
+        *grads_low,
+        *weights,
     ]
     factors, up, down, shared, summed, vector_sum = pl.pallas_call(
-        staged(feed_forward_kernel, 8, 8, 6),
+        staged(feed_forward_kernel, 11, 11, 6),
         out_shape=[
-            jax.ShapeDtypeStruct((count, HDIM, HDIM), f32),
+            jax.ShapeDtypeStruct((count, FOLDED, HDIM), f32),
             block,
             block,
             jax.ShapeDtypeStruct((2, *share.shape), share.dtype),
             jax.ShapeDtypeStruct((2, half, width), f32),
             jax.ShapeDtypeStruct((lines, HDIM), f32),
         ],
-        in_specs=[anywhere] * 8,
+        in_specs=[anywhere] * 11,
         out_specs=[vmem, anywhere, anywhere, anywhere, vmem, vmem],
         scratch_shapes=[
             *slots_for(operands),
-            pltpu.VMEM((count, HDIM, HDIM), f32),
+            pltpu.VMEM((count, FOLDED, HDIM), f32),
             *[dma((2, 3))] * 2,
             dma((1, 2)),
             *[dma((1,))] * 3,
             *[dma((4, 3))] * 2,
-            pltpu.VMEM((count, HDIM, HDIM), f32),
-            pltpu.VMEM((3, count // 4, HDIM, HDIM), f32),
+            pltpu.VMEM((count, FOLDED, HDIM), f32),
+            pltpu.VMEM((3, count // 4, FOLDED, HDIM), f32),
             *[dma((2, 3))] * 2,
             *[pltpu.VMEM((5, lines, HDIM), f32)] * 2,
             *[dma((5,))] * 2,
+            pltpu.VMEM((2, 2, 2, half, width), bf16),
             *row_scratch(half, width),
         ],
         compiler_params=pltpu.CompilerParams(
@@ -860,14 +900,14 @@
         out_specs=[anywhere] * 5,
         scratch_shapes=[
             *slots_for(operands),
-            pltpu.VMEM((count, HDIM, HDIM), f32),
+            pltpu.VMEM((count, FOLDED, HDIM), f32),
             pltpu.VMEM((3, 4, rows // 4, columns), bf16),
             *[dma((5, 3))] * 2,
             dma((1, 5)),
             *[dma((1,))] * 3,
             *[dma((4, 3))] * 2,
-            pltpu.VMEM((count, HDIM, HDIM), f32),
-            pltpu.VMEM((3, count // 4, HDIM, HDIM), f32),
+            pltpu.VMEM((count, FOLDED, HDIM), f32),
+            pltpu.VMEM((3, count // 4, FOLDED, HDIM), f32),
             *[dma((2, 3))] * 2,
         ],
         compiler_params=pltpu.CompilerParams(
@@ -881,16 +921,41 @@
     return orthos, grads, shared
 
 
-def pack(matrices):
-    qkv, out, up, down = matrices
+def pack_attention_kernel(qkv_ref, out_ref, stack_ref):
+    wide = qkv_ref.shape[2]
+    for which in range(3):
+        stack_ref[0, :, which * wide : (which + 1) * wide] = qkv_ref[which].astype(bf16)
+    stack_ref[0, :, 3 * wide :] = out_ref[...].T.astype(bf16)
+
+
+def pack_attention(qkv, out):
+    count = lax.axis_size("ctx")
+    _, rows, columns = qkv.shape
+    wide = columns // count
+    return pl.pallas_call(
+        pack_attention_kernel,
+        out_shape=jax.ShapeDtypeStruct((count, rows, 4 * wide), bf16),
+        grid=(count,),
+        in_specs=[
+            pl.BlockSpec((3, rows, wide), lambda i: (0, 0, i)),
+            pl.BlockSpec((wide, rows), lambda i: (i, 0)),
+        ],
+        out_specs=pl.BlockSpec((1, rows, 4 * wide), lambda i: (i, 0, 0)),
+        compiler_params=pltpu.CompilerParams(vmem_limit_bytes=56 << 20),
+        cost_estimate=pl.CostEstimate(
+            flops=qkv.size, bytes_accessed=8 * qkv.size, transcendentals=0
+        ),
+        name="pack_attention",
+    )(qkv, out)
+
+
+def pack_feed_forward(up, down):
     count = lax.axis_size("ctx")
     rows = up.shape[0]
     low = lambda v: v.astype(bf16)
-    four = jnp.concatenate([low(qkv), low(out).T[None]], axis=0)
-    attn = four.reshape(4, rows, count, -1).transpose(2, 1, 0, 3).reshape(count, rows, -1)
     up_cut = low(up).reshape(rows, count, -1).transpose(1, 0, 2)
     down_cut = low(down).T.reshape(rows, count, -1).transpose(1, 0, 2)
-    return attn, up_cut, down_cut
+    return up_cut, down_cut
 
 
 def finish(name, scale, grads, orthos, moments, weights):
@@ -995,14 +1060,20 @@
     place = jnp.take(place, order, axis=0).reshape(length)
 
     after = lambda value, *others: lax.optimization_barrier((value, *others))[0]
-    attn_stack, up_stack, down_stack = pack((w_qkv, w_out, w_up, w_down))
-    attn_block = to_blocks(attn_stack)
+    attn_block = to_blocks(pack_attention(w_qkv, w_out))
+    up_late, down_late, *moments_late, _ = lax.optimization_barrier(
+        (w_up, w_down, moment_qkv, moment_out, moment_up, moment_down, attn_block)
+    )
+    up_stack, down_stack = pack_feed_forward(up_late, down_late)
     gather_z = lambda v: lax.all_gather(v, "fsdp", axis=0, tiled=True)
-    xs = jnp.concatenate(spread(after(row_low, attn_block)), axis=0)
+    row_first, upper, _ = lax.optimization_barrier((row_low, upper, attn_block))
+    xs = jnp.concatenate(spread(row_first), axis=0)
     both_block = to_blocks(after(jnp.concatenate([up_stack, down_stack], axis=2), xs))
     up_block, down_block = both_block[:, :u], both_block[:, u:]
     attn_g, up_g, down_g = map(gather_z, (attn_block, up_block, down_block))
-    moment_stack = jnp.concatenate(pack((moment_qkv, moment_out, moment_up, moment_down)), axis=2)
+    moment_stack = jnp.concatenate(
+        [pack_attention(*moments_late[:2]), *pack_feed_forward(*moments_late[2:])], axis=2
+    )
     moment_stack = after(moment_stack, both_block)
     attn_g = after(attn_g, moment_stack)
     attn_w = (attn_g, swap_core(attn_g))
@@ -1092,7 +1163,6 @@
     attn_sum = jnp.concatenate([pair_sum(term_qkv), pair_sum(term_out)], axis=1)
     down_total, up_total = map(scatter_z, (down_sum, up_sum))
     *lows, attn_sum = lax.optimization_barrier((*grad_qkv_low, attn_sum))
-    part = sum(mm(lows[i], attn_w[i][:, : 3 * e], (1, 1)) for i in cores).astype(bf16)
 
     qv_sums = []
     for i in cores:
@@ -1128,7 +1198,7 @@
     attn_total = scatter_z(attn_sum)
     step_scale = matrix_rate * math.sqrt(width / HDIM)
     factors, gradient_blocks, layer_out, input_rows, flat = feed_forward_slabs(
-        moments[1:], (up_total, down_total), after(out_rows, attn_sum), part, grad_first, flat
+        moments[1:], (up_total, down_total), after(out_rows, attn_sum), lows, attn_w, grad_first, flat
     )
     orthos, attn_gradients, input_grad = last_slabs(
         moments, (attn_total, up_total, down_total), factors, input_rows

time: 763 us -> 755 us (0.990)
  Pallas kernels: 422 us -> 442 us
  matrix products: 148 us -> 137 us
  other arithmetic: 30.1 us -> 21.6 us
    all_to_all x1, waiting for transfers between devices: 1.25 us -> 12.9 us  [over_ctx(): return lax.all_to_all(stack, 'ctx', split_axis=0, concat_axis=0, tiled=True)]
    all_gather x3, waiting for transfers between devices: 14.7 us -> 3.21 us  [body(): gather_z = lambda v: lax.all_gather(v, 'fsdp', axis=0, tiled=True)]
    dot_general x24 -> x22, matrix products: 148 us -> 137 us  [mm(): lax.dot_general(left, right, ((dims[:1], dims[1:]), ((), ())), preferred_...]
    pallas_call x2, Pallas kernels: 11.1 us -> 22.5 us  [attend_forward(): pl.pallas_call(lambda *refs: attend_kernel(256, *refs), out_shape=jax.Sha...]
    pallas_call x1 -> x3, Pallas kernels: 98.2 us -> 107 us  [the longest x1 99.5 us: feed_forward_slabs(): pl.pallas_call(staged(feed_forward_kernel, 11, 11, 6), out_shape=[jax.Sha...]
  transfers between devices with their start and end apart: 19 -> 19, of which waited for: 6 -> 7; matrix products, arithmetic and copies ran while one was open for 24% -> 21% of each run, Pallas kernels for 37% -> 39%
where the time goes in v4:
time: 755 us; the launch traced here: 757 us
  Pallas kernels  442 us (59%)
  matrix products  137 us (18%)
  blocking collectives  46.3 us (6%)
  waiting for transfers between devices  45.6 us (6%)
  local copies, waits for them, and re-layouts  38.9 us (5%)
  other arithmetic  21.6 us (3%)
  between operations  15.4 us (2%)
  starting transfers between devices  9.72 us (1%)
    pallas_call x3, Pallas kernels, exchange(): pl.pallas_call(staged(kernel, len(operands), n_in, 2 + len(out_types)), o...  220 us
    dot_general x22, matrix products, mm(): lax.dot_general(left, right, ((dims[:1], dims[1:]), ((), ())), preferred_...  137 us
    pallas_call x1, Pallas kernels, feed_forward_slabs(): pl.pallas_call(staged(feed_forward_kernel, 11, 11, 6), out_shape=[jax.Sha...  99.5 us
    pallas_call x1, Pallas kernels, last_slabs(): pl.pallas_call(staged(last_kernel, 8, 8, 5), out_shape=[*[block] * 4, jax...  53 us
    all_to_all x2, blocking collectives, over_ctx(): return lax.all_to_all(stack, 'ctx', split_axis=0, concat_axis=0, tiled=True)  46.3 us
    ppermute x4, waiting for transfers between devices, swap_ctx(): return lax.ppermute(value, 'ctx', xor_pairs(4, mask))  26.5 us
    pallas_call x2, Pallas kernels, attend_forward(): pl.pallas_call(lambda *refs: attend_kernel(256, *refs), out_shape=jax.Sha...  22.5 us
    pallas_call x2, Pallas kernels, attend_backward(): pl.pallas_call(lambda *refs: attend_back_kernel(256, heads, *refs), out_s...  21 us
  transfers between devices with their start and end apart: 19, of which 7 were waited for; matrix products, arithmetic and copies ran while one was open for 21% of the time, Pallas kernels for 39%

profile of v4, /device:TPU:0, one launch (start us, length us, event | category | flops | bytes accessed | tf_op | source)
XLA Modules:
  0.0 756.5 jit_solution(16087532959489710348)
XLA Ops:
  7.3 3.9 pack_attention.2
  11.1 20.0 %all_to_all.15 = bf16[4,128,1024]{2,1,0:T(8,128)(2,1)} all-to-all(bf16[4,128,1024]{2,1,0:T(8,128)(2,1)} %pack_attention.2), channel_id=1, replica_groups=mesh['fsdp'=4,'ctx'=4,'tp'=2] {'ctx'}, dimensions={0} | all-to-all | bytes 2097152 | tf_op jit(solution)/shard_map/all_to_all | solution.py:1007
  40.4 17.5 %collective-permute-done = bf16[256,2048]{1,0:T(8,128)(2,1)} collective-permute-done((bf16[256,2048]{1,0:T(8,128)(2,1)S(1)}, bf16[256,2048]{1,0:T(8,128)(2,1)}, u32[]{:S(2)}, u32[]{:S(2)}) %collective-permute-start) | collective-permute-done | bytes 1048608 | tf_op jit(solution)/shard_map/ppermute | solution.py:38
  64.5 6.4 collective-permute-done.2
  75.6 26.3 %all_to_all.16 = bf16[4,128,2048]{1,2,0:T(8,128)(2,1)} all-to-all(bf16[4,128,2048]{1,2,0:T(8,128)(2,1)S(1)} %pad_maximum_fusion.2), channel_id=1, replica_groups=mesh['fsdp'=4,'ctx'=4,'tp'=2] {'ctx'}, dimensions={0} | all-to-all | bytes 4194304 | tf_op jit(solution)/shard_map/all_to_all | solution.py:1007
  101.9 3.9 copy.70
  105.8 3.0 fusion.33
  109.3 3.7 pack_attention.3
  119.2 3.6 pad_maximum_fusion.1
  127.3 2.6 collective-permute-done.5
  130.0 6.6 add_convert_fusion.7.refs_0_.refs_1_.refs_2_
  136.6 5.5 attend_forward.2
  142.1 2.7 fusion.25
  144.9 5.3 add_convert_fusion.6.refs_0_.refs_1_.refs_2_
  150.2 17.1 %attend_forward.3 = bf16[1024,256]{1,0:T(8,128)(2,1)S(1)} custom-call(bf16[1024,768]{1,0:T(8,128)(2,1)S(1)} %add_convert_fusion.6.refs_0_.refs_1_.refs_2_, bf16[1024,768]{1,0:T(8,128)(2,1)S(1)} %add_convert_fusion.6.refs_0_.refs_1_.refs_2_, bf16[1024,768]{1,0:T(8,128)(2,1)S(1)} %add_convert_fusion.6.refs_0_.refs_1_.refs_2_, s32[1024,1]{1,0:T(8,128)S(1)} %bitcast.110, ...), custom_call_target="tpu_custom_call" | custom-call | flops 1073741824 | bytes 2097152 | tf_op jit(solution)/shard_map/attend_forward/pallas_call | solution.py:372
  167.3 4.7 add_convert_fusion.4
  172.0 73.9 %first_rows.1 = (bf16[4,2,128,2048]{3,2,1,0:T(8,128)(2,1)}, f32[2,128,2048]{2,1,0:T(8,128)}, f32[2,128,2048]{2,1,0:T(8,128)}, f32[8,2048]{1,0:T(8,128)}) custom-call(bf16[2,2,2,128,2048]{4,3,2,1,0:T(8,128)(2,1)} %bitcast.118, bf16[2,128,2048]{2,1,0:T(8,128)(2,1)} %bitcast.120, f32[1,2048]{1,0:T(1,128)} %get-tuple-element.285.refs_2_, ...), custom_call_target="tpu_custom_call" | custom-call | flops 31457280 | bytes 136314880 | tf_op jit(solution)/shard_map/first_rows/pallas_call | solution.py:290
  246.1 4.7 all-to-all-start.2
  250.8 11.5 %multiply_convert_fusion.1 = (bf16[1024,1024]{1,0:T(8,128)(2,1)}, f32[1024,1024]{1,0:T(8,128)}) fusion(f32[1024]{0:T(1024)S(1)} %dynamic_slice.29, bf16[1024,2048]{1,0:T(8,128)(2,1)} %bitcast.154, bf16[2048,1024]{1,0:T(8,128)(2,1)} %all-gather.6.cloned.1.call-done), kind=kOutput, calls=%fused_computation.29 | convolution fusion | flops 4305453056 | bytes 14684160 | tf_op jit(solution)/shard_map/dot_general | solution.py:46
  262.3 9.4 %multiply_convert_fusion = (bf16[1024,1024]{1,0:T(8,128)(2,1)}, f32[1024,1024]{1,0:T(8,128)}) fusion(f32[1024]{0:T(1024)S(1)} %slice.235, bf16[1024,2048]{1,0:T(8,128)(2,1)S(1)} %bitcast.155, bf16[2048,1024]{1,0:T(8,128)(2,1)} %collective-permute-done.6), kind=kOutput, calls=%fused_computation.28 | convolution fusion | flops 4305453056 | bytes 14684160 | tf_op jit(solution)/shard_map/dot_general | solution.py:46
  271.7 3.2 all-gather.8.cloned.1.call-done
  274.9 12.9 %all-to-all-done.2 = bf16[4,128,3072]{2,1,0:T(8,128)(2,1)} async-done(((bf16[4,128,3072]{2,1,0:T(8,128)(2,1)}), bf16[4,128,3072]{2,1,0:T(8,128)(2,1)}, u32[]{:S(2)}, u32[]{:S(2)}) %all-to-all-start.2) | async-done | bytes 3145760 | tf_op jit(solution)/shard_map/all_to_all | solution.py:1007
  287.8 7.1 fusion.43
  295.2 6.6 add_convert_fusion.3
  301.8 73.6 %second_rows.1 = (bf16[4,2,128,2048]{3,2,1,0:T(8,128)(2,1)}, bf16[2,128,2048]{2,1,0:T(8,128)(2,1)}, f32[2,128,2048]{2,1,0:T(8,128)}, f32[8,2048]{1,0:T(8,128)}) custom-call(bf16[2,2,2,128,2048]{4,3,2,1,0:T(8,128)(2,1)} %bitcast.125, f32[2,128,2048]{2,1,0:T(8,128)} %get-tuple-element.111.refs_1_, bf16[2,128,2048]{2,1,0:T(8,128)(2,1)} %bitcast.129, ...), custom_call_target="tpu_custom_call" | custom-call | flops 31457280 | bytes 136314880 | tf_op jit(solution)/shard_map/second_rows/pallas_call | solution.py:290
  375.4 7.6 %convolution_convert_fusion.1 = bf16[2048,1024]{1,0:T(8,128)(2,1)S(1)} fusion(bf16[1024,2048]{1,0:T(8,128)(2,1)} %bitcast.158, bf16[1024,1024]{1,0:T(8,128)(2,1)} %get-tuple-element.300), kind=kOutput, calls=%fused_computation.31 | convolution fusion | flops 4297064448 | bytes 10485760 | tf_op jit(solution)/shard_map/dot_general | solution.py:46
  383.0 4.8 fusion.44
  388.0 8.0 %fusion.6 = bf16[1024,1024]{1,0:T(8,128)(2,1)} fusion(f32[1024,1024]{1,0:T(8,128)S(1)} %copy-done.46, f32[1024]{0:T(1024)S(1)} %dynamic_slice.29, bf16[1024,2048]{1,0:T(8,128)(2,1)S(1)} %bitcast.161, bf16[2048,1024]{1,0:T(8,128)(2,1)S(1)} %copy-done.42), kind=kOutput, calls=%fused_computation.17 | convolution fusion | flops 4316987392 | bytes 14684160 | tf_op jit(solution)/shard_map/dot_general | solution.py:46
  396.0 5.8 add_convert_fusion.2
  401.9 11.7 %convert_reduce_fusion = (f32[1024]{0:T(1024)S(1)}, bf16[1024,1024]{1,0:T(8,128)(2,1)S(1)}) fusion(f32[1024,1024]{1,0:T(8,128)} %get-tuple-element.301, f32[1024]{0:T(1024)S(1)} %slice.235, bf16[1024,2048]{1,0:T(8,128)(2,1)} %bitcast.159, bf16[2048,1024]{1,0:T(8,128)(2,1)} %copy-done.43), kind=kOutput, calls=%fused_computation.26 | convolution fusion | flops 4319083520 | bytes 14688256 | tf_op jit(solution)/shard_map/dot_general | solution.py:46
  413.6 6.4 convolution_convert_fusion
  420.5 9.2 %fusion.45 = f32[1024,2048]{1,0:T(8,128)} fusion(bf16[1024,1024]{1,0:T(8,128)(2,1)S(1)} %get-tuple-element.264, bf16[2048,1024]{1,0:T(8,128)(2,1)} %collective-permute-done.6), kind=kOutput, calls=%fused_computation.111 | convolution fusion | flops 4294967296 | bytes 14680064 | tf_op jit(solution)/shard_map/dot_general | solution.py:46
  429.7 8.4 %add_convert_fusion.1 = bf16[1024,2048]{1,0:T(8,128)(2,1)} fusion(f32[1024,2048]{1,0:T(8,128)} %fusion.45, bf16[1024,1024]{1,0:T(8,128)(2,1)S(1)} %copy-done.14, bf16[2048,1024]{1,0:T(8,128)(2,1)S(1)} %copy-done.39), kind=kOutput, calls=%fused_computation.2 | convolution fusion | flops 4299161600 | bytes 18874368 | tf_op jit(solution)/shard_map/dot_general | solution.py:46
  438.1 6.4 add_convert_fusion
  444.6 73.0 %third_rows.1 = (bf16[4,2,128,2048]{3,2,1,0:T(8,128)(2,1)}, f32[2,128,2048]{2,1,0:T(8,128)}, f32[8,2048]{1,0:T(8,128)}) custom-call(bf16[2,2,2,128,2048]{4,3,2,1,0:T(8,128)(2,1)} %bitcast.124, f32[2,128,2048]{2,1,0:T(8,128)} %get-tuple-element.111.refs_1_, f32[2,128,2048]{2,1,0:T(8,128)} %get-tuple-element.124.refs_2_, ...), custom_call_target="tpu_custom_call" | custom-call | flops 31457280 | bytes 136314880 | tf_op jit(solution)/shard_map/third_rows/pallas_call | solution.py:290
  517.6 3.8 convolution_convert_fusion.5.refs_3_
  521.5 10.6 %attend_backward.2.refs_8_ = bf16[1024,768]{1,0:T(8,128)(2,1)S(1)} custom-call(bf16[1024,768]{1,0:T(8,128)(2,1)S(1)} %add_convert_fusion.6.refs_0_.refs_1_.refs_2_, bf16[1024,768]{1,0:T(8,128)(2,1)S(1)} %add_convert_fusion.6.refs_0_.refs_1_.refs_2_, bf16[1024,768]{1,0:T(8,128)(2,1)S(1)} %add_convert_fusion.6.refs_0_.refs_1_.refs_2_, ...), custom_call_target="tpu_custom_call" | custom-call | flops 2684354560 | bytes 3670016 | tf_op jit(solution)/shard_map/attend_backward/pallas_call | solution.py:426
  532.1 5.0 convolution_convert_fusion.2
  542.5 10.4 %attend_backward.3.refs_7_ = bf16[1024,768]{1,0:T(8,128)(2,1)S(1)} custom-call(bf16[1024,768]{1,0:T(8,128)(2,1)S(1)} %copy-done.3, bf16[1024,768]{1,0:T(8,128)(2,1)S(1)} %copy-done.3, bf16[1024,768]{1,0:T(8,128)(2,1)S(1)} %copy-done.3, bf16[1024,256]{1,0:T(8,128)(2,1)S(1)} %convolution_convert_fusion.4.refs_3_, s32[1024,1]{1,0:T(8,128)S(1)} %bitcast.112, ...), custom_call_target="tpu_custom_call" | custom-call | flops 2684354560 | bytes 3670016 | tf_op jit(solution)/shard_map/attend_backward/pallas_call | solution.py:426
  554.3 5.5 add_convert_fusion.5
  559.8 2.6 pad_maximum_fusion
  562.5 3.7 fusion.32
  570.1 99.5 %feed_forward_slabs.1 = (f32[16,96,128]{2,1,0:T(8,128)}, bf16[4,128,1024]{2,1,0:T(8,128)(2,1)}, bf16[4,128,1024]{2,1,0:T(8,128)(2,1)}, bf16[2,256,2048]{2,1,0:T(...) custom-call(bf16[512,1024]{1,0:T(8,128)(2,1)} %get-tuple-element.267.refs_0_.refs_1_, ...), custom_call_target="tpu_custom_call" | custom-call | flops 1610612736 | bytes 157286400 | tf_op jit(solution)/shard_map/feed_forward_slabs/pallas_call | solution.py:842
  669.7 53.0 %last_slabs.1 = (bf16[4,128,1024]{2,1,0:T(8,128)(2,1)}, bf16[4,128,1024]{2,1,0:T(8,128)(2,1)}, bf16[4,128,1024]{2,1,0:T(8,128)(2,1)}, bf16[4,128,1024]{2,1,0:T(8,128)(2,1)}, f32[2,256,2048]{2,1,0:T(8,128)}) custom-call(bf16[512,1024]{1,0:T(8,128)(2,1)} %get-tuple-element.265.refs_0_, bf16[512,1024]{1,0:T(8,128)(2,1)} %get-tuple-element.267.refs_0_.refs_1_, ...), custom_call_target="tpu_custom_call" | custom-call | flops 2415919104 | bytes 104857600 | tf_op jit(solution)/shard_map/last_slabs/pallas_call | solution.py:896
  722.9 5.9 down_finish.1
  728.8 5.8 up_finish.1
  734.7 6.3 attention_finish.1
  744.2 3.3 copy.97
  (214 shorter events, 48.7 us)
Async XLA Ops:
  7.2 26.5 %copy-start = (bf16[2,1,256,2048]{3,2,1,0:T(8,128)(2,1)S(1)}, bf16[2,1,256,2048]{3,2,1,0:T(8,128)(2,1)}, u32[]{:S(2)}) copy-start(bf16[2,1,256,2048]{3,2,1,0:T(8,128)(2,1)} %param.21) | copy-start | bytes 6291460
  7.2 115.6 %all-gather.4.cloned.1.call-start = ((), (), s32[]{:S(2)}) async-start(), calls=%async_computation.6 | async-start | bytes 5242880 | tf_op jit(solution)/shard_map/all_gather | solution.py:1068
  31.1 214.8 %all-gather.6.cloned.1.call-start = ((), (), s32[]{:S(2)}) async-start(), calls=%async_computation.7 | async-start | bytes 5242880 | tf_op jit(solution)/shard_map/all_gather | solution.py:1068
  33.8 24.2 %collective-permute-start = (bf16[256,2048]{1,0:T(8,128)(2,1)S(1)}, bf16[256,2048]{1,0:T(8,128)(2,1)}, u32[]{:S(2)}, u32[]{:S(2)}) collective-permute-start(bf16[256,2048]{1,0:T(8,128)(2,1)S(1)} %fusion.84), channel_id=1, source_target_pairs={{0,2},{2,0},{4,6},{6,4},{1,3},{3,1},{5,7},{7,5},{8,10},{10,8},{12,... | collective-permute-start | bytes 3145736 | tf_op jit(solution)/shard_map/ppermute | solution.py:38
  34.8 25.7 %collective-permute-start.1 = (bf16[256,2048]{1,0:T(8,128)(2,1)S(1)}, bf16[256,2048]{1,0:T(8,128)(2,1)}, u32[]{:S(2)}, u32[]{:S(2)}) collective-permute-start(bf16[256,2048]{1,0:T(8,128)(2,1)S(1)} %fusion.84), channel_id=1, source_target_pairs={{0,4},{2,6},{4,0},{6,2},{1,5},{3,7},{5,1},{7,3},{8,12},{10,14},{12... | collective-permute-start | bytes 3145736 | tf_op jit(solution)/shard_map/ppermute | solution.py:38
  59.0 11.9 %collective-permute-start.2 = (bf16[128,2048]{1,0:T(8,128)(2,1)S(1)}, bf16[128,2048]{1,0:T(8,128)(2,1)S(1)}, u32[]{:S(2)}, u32[]{:S(2)}) collective-permute-start(bf16[128,2048]{1,0:T(8,128)(2,1)S(1)} %slice.225), channel_id=1, source_target_pairs={{0,4},{2,6},{4,0},{6,2},{1,5},{3,7},{5,1},{7,3},{8,12},{10,14},{12... | collective-permute-start | bytes 1572872 | tf_op jit(solution)/shard_map/ppermute | solution.py:38
  61.6 12.0 %collective-permute-start.3 = (bf16[128,2048]{1,0:T(8,128)(2,1)S(1)}, bf16[128,2048]{1,0:T(8,128)(2,1)S(1)}, u32[]{:S(2)}, u32[]{:S(2)}) collective-permute-start(bf16[128,2048]{1,0:T(8,128)(2,1)S(1)} %slice.226), channel_id=1, source_target_pairs={{0,2},{2,0},{4,6},{6,4},{1,3},{3,1},{5,7},{7,5},{8,10},{10,8},{12,... | collective-permute-start | bytes 1572872 | tf_op jit(solution)/shard_map/ppermute | solution.py:38
  108.9 166.0 %all-gather.8.cloned.1.call-start = ((), (), s32[]{:S(2)}) async-start(), calls=%async_computation.8 | async-start | bytes 5242880 | tf_op jit(solution)/shard_map/all_gather | solution.py:1068
  119.2 7.2 copy-start.26
  119.2 7.2 copy-start.28
  122.8 22.1 %collective-permute-start.4 = (bf16[2048,1024]{1,0:T(8,128)(2,1)}, bf16[2048,1024]{1,0:T(8,128)(2,1)}, u32[]{:S(2)}, u32[]{:S(2)}) collective-permute-start(bf16[2048,1024]{1,0:T(8,128)(2,1)} %all-gather.4.cloned.1.call-done.refs_9_), channel_id=1, source_target_pairs={{0,1},{1,0},{2,3},{3,2},{4,5},{5,4},{6,7},{7,6},{8,9},{9,8},{10,11... | collective-permute-start | bytes 12582920 | tf_op jit(solution)/shard_map/ppermute | solution.py:34
  123.5 6.4 collective-permute-start.5
  127.3 22.9 %copy-start.6 = (s32[1,1024]{0,1:T(8,128)}, s32[1,1024]{0,1:T(8,128)S(1)}, u32[]{:S(2)}) copy-start(s32[1,1024]{0,1:T(8,128)S(1)} %copy.82) | copy-start | bytes 12292
  136.6 8.2 %copy-start.2 = (bf16[1024,768]{1,0:T(8,128)(2,1)}, bf16[1024,768]{1,0:T(8,128)(2,1)S(1)}, u32[]{:S(2)}) copy-start(bf16[1024,768]{1,0:T(8,128)(2,1)S(1)} %add_convert_fusion.7.refs_0_.refs_1_.refs_2_) | copy-start | bytes 4718596
  246.0 16.4 %collective-permute-start.6 = (bf16[2048,1024]{1,0:T(8,128)(2,1)}, bf16[2048,1024]{1,0:T(8,128)(2,1)}, u32[]{:S(2)}, u32[]{:S(2)}) collective-permute-start(bf16[2048,1024]{1,0:T(8,128)(2,1)} %all-gather.6.cloned.1.call-done), channel_id=1, source_target_pairs={{0,1},{1,0},{2,3},{3,2},{4,5},{5,4},{6,7},{7,6},{8,9},{9,8},{10,11... | collective-permute-start | bytes 12582920 | tf_op jit(solution)/shard_map/ppermute | solution.py:34
  246.1 41.8 %all-to-all-start.2 = ((bf16[4,128,3072]{2,1,0:T(8,128)(2,1)}), bf16[4,128,3072]{2,1,0:T(8,128)(2,1)}, u32[]{:S(2)}, u32[]{:S(2)}) async-start(bf16[4,128,3072]{2,1,0:T(8,128)(2,1)} %pad_maximum_fusion.1), calls=%async_computation.2 | async-start | bytes 6291456 | tf_op jit(solution)/shard_map/all_to_all | solution.py:1007
  250.7 319.4 %reduce-scatter.6.cloned.1.call-start = ((), (), s32[]{:S(2)}) async-start(), calls=%async_computation.10 | async-start | bytes 5242880 | tf_op jit(solution)/shard_map/reduce_scatter | solution.py:1127
  250.8 11.6 %copy-start.40 = (bf16[4,2,128,2048]{3,2,1,0:T(8,128)(2,1)S(1)}, bf16[4,2,128,2048]{3,2,1,0:T(8,128)(2,1)}, u32[]{:S(2)}) copy-start(bf16[4,2,128,2048]{3,2,1,0:T(8,128)(2,1)} %get-tuple-element.107) | copy-start | bytes 12582916
  287.8 7.4 copy-start.48
  287.8 7.4 collective-permute-start.7
  375.4 7.6 %copy-start.44 = (bf16[4,2,128,2048]{3,2,1,0:T(8,128)(2,1)S(1)}, bf16[4,2,128,2048]{3,2,1,0:T(8,128)(2,1)}, u32[]{:S(2)}) copy-start(bf16[4,2,128,2048]{3,2,1,0:T(8,128)(2,1)} %get-tuple-element.113) | copy-start | bytes 12582916
  375.4 7.6 %copy-start.47 = (bf16[1024,1024]{1,0:T(8,128)(2,1)S(1)}, bf16[1024,1024]{1,0:T(8,128)(2,1)}, u32[]{:S(2)}) copy-start(bf16[1024,1024]{1,0:T(8,128)(2,1)} %get-tuple-element.298) | copy-start | bytes 6291460
  387.9 8.1 %collective-permute-start.8 = (bf16[2048,1024]{1,0:T(8,128)(2,1)S(1)}, bf16[2048,1024]{1,0:T(8,128)(2,1)}, u32[]{:S(2)}, u32[]{:S(2)}) collective-permute-start(bf16[2048,1024]{1,0:T(8,128)(2,1)S(1)} %convolution_convert_fusion.1), channel_id=1, source_target_pairs={{0,1},{1,0},{2,3},{3,2},{4,5},{5,4},{6,7},{7,6},{8,9},{9,8},{10,11... | collective-permute-start | bytes 12582920 | tf_op jit(solution)/shard_map/ppermute | solution.py:34
  401.8 168.3 %reduce-scatter.4.cloned.1.call-start = ((), (), s32[]{:S(2)}) async-start(), calls=%async_computation.9 | async-start | bytes 5242880 | tf_op jit(solution)/shard_map/reduce_scatter | solution.py:1127
  401.9 11.7 %copy-start.41 = (bf16[4,2,128,2048]{3,2,1,0:T(8,128)(2,1)S(1)}, bf16[4,2,128,2048]{3,2,1,0:T(8,128)(2,1)}, u32[]{:S(2)}) copy-start(bf16[4,2,128,2048]{3,2,1,0:T(8,128)(2,1)} %get-tuple-element.107) | copy-start | bytes 12582916
  420.0 9.7 %copy-start.14 = (bf16[1024,1024]{1,0:T(8,128)(2,1)S(1)}, bf16[1024,1024]{1,0:T(8,128)(2,1)}, u32[]{:S(2)}) copy-start(bf16[1024,1024]{1,0:T(8,128)(2,1)} %fusion.6) | copy-start | bytes 6291460
  420.0 9.7 %copy-start.39 = (bf16[2048,1024]{1,0:T(8,128)(2,1)S(1)}, bf16[2048,1024]{1,0:T(8,128)(2,1)}, u32[]{:S(2)}) copy-start(bf16[2048,1024]{1,0:T(8,128)(2,1)} %all-gather.6.cloned.1.call-done) | copy-start | bytes 12582916
  420.0 18.1 %collective-permute-start.9 = (bf16[2048,1024]{1,0:T(8,128)(2,1)}, bf16[2048,1024]{1,0:T(8,128)(2,1)S(1)}, u32[]{:S(2)}, u32[]{:S(2)}) collective-permute-start(bf16[2048,1024]{1,0:T(8,128)(2,1)} %convolution_convert_fusion), channel_id=1, source_target_pairs={{0,1},{1,0},{2,3},{3,2},{4,5},{5,4},{6,7},{7,6},{8,9},{9,8},{10,11... | collective-permute-start | bytes 12582920 | tf_op jit(solution)/shard_map/ppermute | solution.py:34
  444.5 225.1 %reduce-scatter.8.cloned.1.call-start = ((), (), s32[]{:S(2)}) async-start(), calls=%async_computation.11 | async-start | bytes 5242880 | tf_op jit(solution)/shard_map/reduce_scatter | solution.py:1127
  521.4 10.7 %copy-start.18 = (bf16[1024,2048]{1,0:T(8,128)(2,1)S(1)}, bf16[1024,2048]{1,0:T(8,128)(2,1)}, u32[]{:S(2)}) copy-start(bf16[1024,2048]{1,0:T(8,128)(2,1)} %copy-done.16) | copy-start | bytes 12582916
  532.1 35.9 %copy-start.4 = (bf16[1024,768]{1,0:T(8,128)(2,1)}, bf16[1024,768]{1,0:T(8,128)(2,1)S(1)}, u32[]{:S(2)}) copy-start(bf16[1024,768]{1,0:T(8,128)(2,1)S(1)} %attend_backward.2.refs_8_) | copy-start | bytes 4718596
  537.1 17.2 %collective-permute-start.10 = (bf16[2048,768]{1,0:T(8,128)(2,1)}, bf16[2048,768]{1,0:T(8,128)(2,1)}, u32[]{:S(2)}, u32[]{:S(2)}) collective-permute-start(bf16[2048,768]{1,0:T(8,128)(2,1)} %convolution_convert_fusion.2), channel_id=1, source_target_pairs={{0,1},{1,0},{2,3},{3,2},{4,5},{5,4},{6,7},{7,6},{8,9},{9,8},{10,11... | collective-permute-start | bytes 9437192 | tf_op jit(solution)/shard_map/ppermute | solution.py:34
  539.5 13.4 %collective-permute-start.11 = (bf16[2048,256]{1,0:T(8,128)(2,1)}, bf16[2048,256]{1,0:T(8,128)(2,1)S(1)}, u32[]{:S(2)}, u32[]{:S(2)}) collective-permute-start(bf16[2048,256]{1,0:T(8,128)(2,1)} %convolution_convert_fusion.3), channel_id=1, source_target_pairs={{0,1},{1,0},{2,3},{3,2},{4,5},{5,4},{6,7},{7,6},{8,9},{9,8},{10,11... | collective-permute-start | bytes 3145736 | tf_op jit(solution)/shard_map/ppermute | solution.py:34
  542.5 10.4 %copy-start.9 = (bf16[1024,256]{1,0:T(8,128)(2,1)S(1)}, bf16[1024,256]{1,0:T(8,128)(2,1)}, u32[]{:S(2)}) copy-start(bf16[1024,256]{1,0:T(8,128)(2,1)} %copy-done.8) | copy-start | bytes 1572868
  552.9 14.8 %copy-start.5 = (bf16[1024,768]{1,0:T(8,128)(2,1)}, bf16[1024,768]{1,0:T(8,128)(2,1)S(1)}, u32[]{:S(2)}) copy-start(bf16[1024,768]{1,0:T(8,128)(2,1)S(1)} %attend_backward.3.refs_7_) | copy-start | bytes 4718596
  669.6 53.1 %copy-start.19 = (f32[192,128]{1,0:T(8,128)S(1)}, f32[192,128]{1,0:T(8,128)}, u32[]{:S(2)}) copy-start(f32[192,128]{1,0:T(8,128)} %get-tuple-element.143) | copy-start | bytes 294916
  722.8 18.2 %copy-start.22 = (f32[1,4096]{1,0:T(1,128)}, f32[1,4096]{1,0:T(1,128)S(1)}, u32[]{:S(2)}) copy-start(f32[1,4096]{1,0:T(1,128)S(1)} %constant_dynamic-slice_fusion.1) | copy-start | bytes 49156
  722.8 18.8 %copy-start.23 = (f32[2,2048]{1,0:T(2,128)}, f32[2,2048]{1,0:T(2,128)S(1)}, u32[]{:S(2)}) copy-start(f32[2,2048]{1,0:T(2,128)S(1)} %slice.218) | copy-start | bytes 49156
  722.9 19.4 %copy-start.24 = (f32[2,2048]{1,0:T(2,128)}, f32[2,2048]{1,0:T(2,128)S(1)}, u32[]{:S(2)}) copy-start(f32[2,2048]{1,0:T(2,128)S(1)} %slice.220) | copy-start | bytes 49156
  722.9 20.0 %copy-start.25 = (f32[2,2048]{1,0:T(2,128)}, f32[2,2048]{1,0:T(2,128)S(1)}, u32[]{:S(2)}) copy-start(f32[2,2048]{1,0:T(2,128)S(1)} %slice.222) | copy-start | bytes 49156
  734.6 7.0 copy-start.21
  734.6 7.7 %copy-start.27 = (f32[2,2048]{1,0:T(2,128)S(1)}, f32[2,2048]{1,0:T(2,128)}, u32[]{:S(2)}) copy-start(f32[2,2048]{1,0:T(2,128)} %param.31) | copy-start | bytes 49156
  734.6 7.6 %copy-start.35 = (f32[2,2048]{1,0:T(2,128)S(1)}, f32[2,2048]{1,0:T(2,128)}, u32[]{:S(2)}) copy-start(f32[2,2048]{1,0:T(2,128)} %param.40) | copy-start | bytes 49156
  734.7 8.3 %copy-start.29 = (f32[2,2048]{1,0:T(2,128)S(1)}, f32[2,2048]{1,0:T(2,128)}, u32[]{:S(2)}) copy-start(f32[2,2048]{1,0:T(2,128)} %param.32) | copy-start | bytes 49156
  734.7 8.3 %copy-start.36 = (f32[2,2048]{1,0:T(2,128)S(1)}, f32[2,2048]{1,0:T(2,128)}, u32[]{:S(2)}) copy-start(f32[2,2048]{1,0:T(2,128)} %param.41) | copy-start | bytes 49156
  734.7 8.9 %copy-start.32 = (f32[2,1024]{1,0:T(2,128)S(1)}, f32[2,1024]{1,0:T(2,128)}, u32[]{:S(2)}) copy-start(f32[2,1024]{1,0:T(2,128)} %param.28) | copy-start | bytes 24580
  734.7 8.9 %copy-start.37 = (f32[2,1024]{1,0:T(2,128)S(1)}, f32[2,1024]{1,0:T(2,128)}, u32[]{:S(2)}) copy-start(f32[2,1024]{1,0:T(2,128)} %param.37) | copy-start | bytes 24580
  734.7 12.8 %copy-start.13 = (f32[2,256,2048]{2,1,0:T(8,128)S(1)}, f32[2,256,2048]{2,1,0:T(8,128)}, u32[]{:S(2)}) copy-start(f32[2,256,2048]{2,1,0:T(8,128)} %get-tuple-element.139) | copy-start | bytes 12582916
  (20 other events, 96.8 us)
Sparse Core Ops, SparseCore 0:
  31.3 80.6 all-gather.3
  114.1 79.2 all-gather.5
  195.6 79.2 all-gather.7
  401.9 76.2 reduce-scatter.5
  480.5 77.2 reduce-scatter.3
  562.6 104.6 reduce-scatter.7

commit v5 on v4

--- a/solution.py
+++ b/solution.py
@@ -949,6 +949,54 @@
     )(qkv, out)
 
 
+def attention_block_kernel(given, ready, qkv_ref, out_ref, block_ref, stage, send, receive, local):
+    wide = stage.shape[2] // 4
+    c = lax.axis_index("ctx")
+    greet([("ctx", (c + i) % 4) for i in (1, 2, 3)])
+    ready(0, 2)
+    copies = []
+    for i in (3, 1, 2, 0):
+        side = (c + i) % 4
+        span = pl.ds(pl.multiple_of(side * wide, wide), wide)
+        for which in range(3):
+            stage[i, :, which * wide : (which + 1) * wide] = qkv_ref[which, :, span].astype(bf16)
+        stage[i, :, 3 * wide :] = out_ref[span, :].T.astype(bf16)
+        if i:
+            sems = send.at[i - 1], receive.at[i - 1]
+            copies.append(remote(stage.at[i], block_ref.at[c], *sems, "ctx", side))
+        else:
+            copies.append(pltpu.make_async_copy(stage.at[i], block_ref.at[c], local.at[0]))
+        copies[-1].start()
+    for one in copies:
+        one.wait()
+
+
+def attention_block(qkv, out):
+    _, rows, columns = qkv.shape
+    if lax.axis_size("ctx") != 4 or columns % 512 or rows % 16:
+        return to_blocks(pack_attention(qkv, out))
+    shape = (4, rows, columns)
+    anywhere = pl.BlockSpec(memory_space=pl.ANY)
+    block = pl.pallas_call(
+        staged(attention_block_kernel, 2, 2, 1),
+        out_shape=jax.ShapeDtypeStruct(shape, bf16),
+        in_specs=[anywhere] * 2,
+        out_specs=anywhere,
+        scratch_shapes=[
+            *slots_for([qkv, out]),
+            pltpu.VMEM(shape, bf16),
+            *[pltpu.SemaphoreType.DMA((3,))] * 2,
+            pltpu.SemaphoreType.DMA((1,)),
+        ],
+        compiler_params=pltpu.CompilerParams(
+            collective_id=6, has_side_effects=True, vmem_limit_bytes=56 << 20
+        ),
+        cost_estimate=pl.CostEstimate(flops=qkv.size, bytes_accessed=30 << 20, transcendentals=0),
+        name="attention_block",
+    )(qkv, out)
+    return block.reshape(4 * rows, columns)
+
+
 def pack_feed_forward(up, down):
     count = lax.axis_size("ctx")
     rows = up.shape[0]
@@ -1060,7 +1108,7 @@
     place = jnp.take(place, order, axis=0).reshape(length)
 
     after = lambda value, *others: lax.optimization_barrier((value, *others))[0]
-    attn_block = to_blocks(pack_attention(w_qkv, w_out))
+    attn_block = attention_block(w_qkv, w_out)
     up_late, down_late, *moments_late, _ = lax.optimization_barrier(
         (w_up, w_down, moment_qkv, moment_out, moment_up, moment_down, attn_block)
     )
@@ -1071,9 +1119,8 @@
     both_block = to_blocks(after(jnp.concatenate([up_stack, down_stack], axis=2), xs))
     up_block, down_block = both_block[:, :u], both_block[:, u:]
     attn_g, up_g, down_g = map(gather_z, (attn_block, up_block, down_block))
-    moment_stack = jnp.concatenate(
-        [pack_attention(*moments_late[:2]), *pack_feed_forward(*moments_late[2:])], axis=2
-    )
+    attn_moments = to_blocks(after(pack_attention(*moments_late[:2]), both_block))
+    moment_stack = jnp.concatenate(pack_feed_forward(*moments_late[2:]), axis=2)
     moment_stack = after(moment_stack, both_block)
     attn_g = after(attn_g, moment_stack)
     attn_w = (attn_g, swap_core(attn_g))
@@ -1091,6 +1138,7 @@
     context = [attend_forward(qkv[i], place) for i in cores]
     part = sum(mm(context[i], attn_w[i][:, 3 * e :], (1, 1)) for i in cores).astype(bf16)
     row = lambda matrix, index: matrix[index : index + 1]
+    part = after(part, attn_moments)
     first_all, (first_unit, first_inverse), _ = exchange(
         "first_rows",
         1,
@@ -1102,7 +1150,7 @@
         0,
     )
     moment_block = to_blocks(after(moment_stack, first_all))
-    moments = [moment_block[:, : 4 * e], moment_block[:, 4 * e : 4 * e + u], moment_block[:, 4 * e + u :]]
+    moments = [attn_moments, moment_block[:, :u], moment_block[:, u:]]
     up_g = after(up_g, first_all)
     up_w = (up_g, swap_core(up_g))
     pre_act = [mm(first_all, up_w[i], (1, 0)) + small_pair[i][2 * e :] for i in cores]

time: 755 us -> 742 us (0.983)
  blocking collectives: 46.3 us -> 27.7 us
    all_to_all x2 -> x1, blocking collectives: 46.3 us -> 27.7 us  [over_ctx(): return lax.all_to_all(stack, 'ctx', split_axis=0, concat_axis=0, tiled=True)]
    pallas_call x0 -> x1, Pallas kernels: none -> 17.8 us  [attention_block(): pl.pallas_call(staged(attention_block_kernel, 2, 2, 1), out_shape=jax.Sha...]
    all_to_all x1 -> x2, waiting for transfers between devices: 12.9 us -> 0.01 us  [over_ctx(): return lax.all_to_all(stack, 'ctx', split_axis=0, concat_axis=0, tiled=True)]
    pallas_call x2, Pallas kernels: 22.5 us -> 11.3 us  [attend_forward(): pl.pallas_call(lambda *refs: attend_kernel(256, *refs), out_shape=jax.Sha...]
    all_gather x3, waiting for transfers between devices: 3.21 us -> 12.4 us  [body(): gather_z = lambda v: lax.all_gather(v, 'fsdp', axis=0, tiled=True)]
  transfers between devices with their start and end apart: 19 -> 20, of which waited for: 7 -> 5; matrix products, arithmetic and copies ran while one was open for 21% -> 22% of each run, Pallas kernels for 39% -> 38%
where the time goes in v5:
time: 742 us; the launch traced here: 737 us
  Pallas kernels  445 us (60%)
  matrix products  138 us (19%)
  waiting for transfers between devices  38.6 us (5%)
  local copies, waits for them, and re-layouts  36.9 us (5%)
  blocking collectives  27.7 us (4%)
  other arithmetic  21.8 us (3%)
  between operations  15.5 us (2%)
  starting transfers between devices  13.4 us (2%)
    pallas_call x3, Pallas kernels, exchange(): pl.pallas_call(staged(kernel, len(operands), n_in, 2 + len(out_types)), o...  223 us
    dot_general x22, matrix products, mm(): lax.dot_general(left, right, ((dims[:1], dims[1:]), ((), ())), preferred_...  138 us
    pallas_call x1, Pallas kernels, feed_forward_slabs(): pl.pallas_call(staged(feed_forward_kernel, 11, 11, 6), out_shape=[jax.Sha...  97.7 us
    pallas_call x1, Pallas kernels, last_slabs(): pl.pallas_call(staged(last_kernel, 8, 8, 5), out_shape=[*[block] * 4, jax...  53 us
    all_to_all x1, blocking collectives, over_ctx(): return lax.all_to_all(stack, 'ctx', split_axis=0, concat_axis=0, tiled=True)  27.7 us
    ppermute x4, waiting for transfers between devices, swap_ctx(): return lax.ppermute(value, 'ctx', xor_pairs(4, mask))  25.3 us
    pallas_call x2, Pallas kernels, attend_backward(): pl.pallas_call(lambda *refs: attend_back_kernel(256, heads, *refs), out_s...  20.8 us
    pallas_call x3, Pallas kernels, finish(): pl.pallas_call(kernel, out_shape=[jax.ShapeDtypeStruct(s.shape, f32) for...  18 us
  transfers between devices with their start and end apart: 20, of which 5 were waited for; matrix products, arithmetic and copies ran while one was open for 22% of the time, Pallas kernels for 38%

profile of v5, /device:TPU:0, one launch (start us, length us, event | category | flops | bytes accessed | tf_op | source)
XLA Modules:
  0.0 736.7 jit_solution(11898610096135291610)
XLA Ops:
  7.3 17.8 %attention_block.1 = bf16[4,128,1024]{2,1,0:T(8,128)(2,1)} custom-call(f32[3,128,1024]{2,1,0:T(8,128)} %refs_2_.1, f32[1024,128]{1,0:T(8,128)} %refs_3_.1), custom_call_target="tpu_custom_call" | custom-call | flops 393216 | bytes 31457280 | tf_op jit(solution)/shard_map/attention_block/pallas_call | solution.py:980
  29.0 2.5 copy.69
  34.9 17.2 %collective-permute-done = bf16[256,2048]{1,0:T(8,128)(2,1)} collective-permute-done((bf16[256,2048]{1,0:T(8,128)(2,1)S(1)}, bf16[256,2048]{1,0:T(8,128)(2,1)}, u32[]{:S(2)}, u32[]{:S(2)}) %collective-permute-start) | collective-permute-done | bytes 1048608 | tf_op jit(solution)/shard_map/ppermute | solution.py:38
  58.9 6.5 collective-permute-done.2
  69.1 27.7 %all_to_all.15 = bf16[4,128,2048]{1,2,0:T(8,128)(2,1)} all-to-all(bf16[4,128,2048]{1,2,0:T(8,128)(2,1)S(1)} %pad_maximum_fusion.2), channel_id=1, replica_groups=mesh['fsdp'=4,'ctx'=4,'tp'=2] {'ctx'}, dimensions={0} | all-to-all | bytes 4194304 | tf_op jit(solution)/shard_map/all_to_all | solution.py:1055
  96.8 3.9 copy.70
  100.8 3.0 fusion.32
  108.2 3.1 pad_maximum_fusion.1
  115.6 3.8 pack_attention.1
  119.7 3.5 all-to-all-start.1
  123.9 6.6 add_convert_fusion.7.refs_0_.refs_1_.refs_2_
  130.6 5.5 attend_forward.2
  136.1 2.7 fusion.25
  138.8 5.3 add_convert_fusion.6.refs_0_.refs_1_.refs_2_
  144.2 5.9 attend_forward.3
  150.8 4.6 add_convert_fusion.4
  155.4 75.0 %first_rows.1 = (bf16[4,2,128,2048]{3,2,1,0:T(8,128)(2,1)}, f32[2,128,2048]{2,1,0:T(8,128)}, f32[2,128,2048]{2,1,0:T(8,128)}, f32[8,2048]{1,0:T(8,128)}) custom-call(bf16[2,2,2,128,2048]{4,3,2,1,0:T(8,128)(2,1)} %bitcast.124, bf16[2,128,2048]{2,1,0:T(8,128)(2,1)} %bitcast.126, f32[1,2048]{1,0:T(1,128)} %get-tuple-element.288.refs_2_, ...), custom_call_target="tpu_custom_call" | custom-call | flops 31457280 | bytes 136314880 | tf_op jit(solution)/shard_map/first_rows/pallas_call | solution.py:290
  230.5 4.5 all-to-all-start.2
  235.1 11.6 %multiply_convert_fusion.1 = (bf16[1024,1024]{1,0:T(8,128)(2,1)}, f32[1024,1024]{1,0:T(8,128)}) fusion(f32[1024]{0:T(1024)S(1)} %dynamic_slice.29, bf16[1024,2048]{1,0:T(8,128)(2,1)} %bitcast.161, bf16[2048,1024]{1,0:T(8,128)(2,1)} %all-gather.6.cloned.1.call-done), kind=kOutput, calls=%fused_computation.29 | convolution fusion | flops 4305453056 | bytes 14684160 | tf_op jit(solution)/shard_map/dot_general | solution.py:46
  246.7 9.4 %multiply_convert_fusion = (bf16[1024,1024]{1,0:T(8,128)(2,1)}, f32[1024,1024]{1,0:T(8,128)}) fusion(f32[1024]{0:T(1024)S(1)} %slice.231, bf16[1024,2048]{1,0:T(8,128)(2,1)S(1)} %bitcast.162, bf16[2048,1024]{1,0:T(8,128)(2,1)} %collective-permute-done.6), kind=kOutput, calls=%fused_computation.28 | convolution fusion | flops 4305453056 | bytes 14684160 | tf_op jit(solution)/shard_map/dot_general | solution.py:46
  256.1 12.4 %all-gather.8.cloned.1.call-done = bf16[2048,1024]{1,0:T(8,128)(2,1)} async-done(((bf16[512,1024]{1,0:T(8,128)(2,1)}), bf16[2048,1024]{1,0:T(8,128)(2,1)}) %all-gather.8.cloned.1.call-update) | async-done | bytes 4194320 | tf_op jit(solution)/shard_map/all_gather | solution.py:1116
  268.5 7.2 fusion.43
  275.9 6.3 add_convert_fusion.3
  282.2 74.6 %second_rows.1 = (bf16[4,2,128,2048]{3,2,1,0:T(8,128)(2,1)}, bf16[2,128,2048]{2,1,0:T(8,128)(2,1)}, f32[2,128,2048]{2,1,0:T(8,128)}, f32[8,2048]{1,0:T(8,128)}) custom-call(bf16[2,2,2,128,2048]{4,3,2,1,0:T(8,128)(2,1)} %bitcast.133, f32[2,128,2048]{2,1,0:T(8,128)} %get-tuple-element.115.refs_1_, bf16[2,128,2048]{2,1,0:T(8,128)(2,1)} %bitcast.136, ...), custom_call_target="tpu_custom_call" | custom-call | flops 31457280 | bytes 136314880 | tf_op jit(solution)/shard_map/second_rows/pallas_call | solution.py:290
  356.8 7.6 %convolution_convert_fusion.1 = bf16[2048,1024]{1,0:T(8,128)(2,1)S(1)} fusion(bf16[1024,2048]{1,0:T(8,128)(2,1)} %bitcast.165, bf16[1024,1024]{1,0:T(8,128)(2,1)} %get-tuple-element.303), kind=kOutput, calls=%fused_computation.31 | convolution fusion | flops 4297064448 | bytes 10485760 | tf_op jit(solution)/shard_map/dot_general | solution.py:46
  364.4 4.9 fusion.44
  369.4 8.0 %fusion.6 = bf16[1024,1024]{1,0:T(8,128)(2,1)} fusion(f32[1024,1024]{1,0:T(8,128)S(1)} %copy-done.47, f32[1024]{0:T(1024)S(1)} %dynamic_slice.29, bf16[1024,2048]{1,0:T(8,128)(2,1)S(1)} %bitcast.168, bf16[2048,1024]{1,0:T(8,128)(2,1)S(1)} %copy-done.43), kind=kOutput, calls=%fused_computation.17 | convolution fusion | flops 4316987392 | bytes 14684160 | tf_op jit(solution)/shard_map/dot_general | solution.py:46
  377.4 5.9 add_convert_fusion.2
  383.3 12.4 %convert_reduce_fusion = (f32[1024]{0:T(1024)S(1)}, bf16[1024,1024]{1,0:T(8,128)(2,1)S(1)}) fusion(f32[1024,1024]{1,0:T(8,128)} %get-tuple-element.304, f32[1024]{0:T(1024)S(1)} %slice.231, bf16[1024,2048]{1,0:T(8,128)(2,1)} %bitcast.166, bf16[2048,1024]{1,0:T(8,128)(2,1)} %copy-done.44), kind=kOutput, calls=%fused_computation.26 | convolution fusion | flops 4319083520 | bytes 14688256 | tf_op jit(solution)/shard_map/dot_general | solution.py:46
  395.8 6.6 convolution_convert_fusion
  402.9 9.2 %fusion.45 = f32[1024,2048]{1,0:T(8,128)} fusion(bf16[1024,1024]{1,0:T(8,128)(2,1)S(1)} %get-tuple-element.268, bf16[2048,1024]{1,0:T(8,128)(2,1)} %collective-permute-done.6), kind=kOutput, calls=%fused_computation.112 | convolution fusion | flops 4294967296 | bytes 14680064 | tf_op jit(solution)/shard_map/dot_general | solution.py:46
  412.1 8.4 %add_convert_fusion.1 = bf16[1024,2048]{1,0:T(8,128)(2,1)} fusion(f32[1024,2048]{1,0:T(8,128)} %fusion.45, bf16[1024,1024]{1,0:T(8,128)(2,1)S(1)} %copy-done.15, bf16[2048,1024]{1,0:T(8,128)(2,1)S(1)} %copy-done.40), kind=kOutput, calls=%fused_computation.2 | convolution fusion | flops 4299161600 | bytes 18874368 | tf_op jit(solution)/shard_map/dot_general | solution.py:46
  420.5 6.4 add_convert_fusion
  427.0 73.0 %third_rows.1 = (bf16[4,2,128,2048]{3,2,1,0:T(8,128)(2,1)}, f32[2,128,2048]{2,1,0:T(8,128)}, f32[8,2048]{1,0:T(8,128)}) custom-call(bf16[2,2,2,128,2048]{4,3,2,1,0:T(8,128)(2,1)} %bitcast.132, f32[2,128,2048]{2,1,0:T(8,128)} %get-tuple-element.115.refs_1_, f32[2,128,2048]{2,1,0:T(8,128)} %get-tuple-element.128.refs_2_, ...), custom_call_target="tpu_custom_call" | custom-call | flops 31457280 | bytes 136314880 | tf_op jit(solution)/shard_map/third_rows/pallas_call | solution.py:290
  500.0 3.9 convolution_convert_fusion.5.refs_3_
  503.9 10.4 %attend_backward.2.refs_8_ = bf16[1024,768]{1,0:T(8,128)(2,1)S(1)} custom-call(bf16[1024,768]{1,0:T(8,128)(2,1)S(1)} %add_convert_fusion.6.refs_0_.refs_1_.refs_2_, bf16[1024,768]{1,0:T(8,128)(2,1)S(1)} %add_convert_fusion.6.refs_0_.refs_1_.refs_2_, bf16[1024,768]{1,0:T(8,128)(2,1)S(1)} %add_convert_fusion.6.refs_0_.refs_1_.refs_2_, ...), custom_call_target="tpu_custom_call" | custom-call | flops 2684354560 | bytes 3670016 | tf_op jit(solution)/shard_map/attend_backward/pallas_call | solution.py:426
  514.3 5.0 convolution_convert_fusion.2
  522.2 2.5 convolution_convert_fusion.4.refs_3_
  524.7 10.4 %attend_backward.3.refs_7_ = bf16[1024,768]{1,0:T(8,128)(2,1)S(1)} custom-call(bf16[1024,768]{1,0:T(8,128)(2,1)S(1)} %copy-done.3, bf16[1024,768]{1,0:T(8,128)(2,1)S(1)} %copy-done.3, bf16[1024,768]{1,0:T(8,128)(2,1)S(1)} %copy-done.3, bf16[1024,256]{1,0:T(8,128)(2,1)S(1)} %convolution_convert_fusion.4.refs_3_, s32[1024,1]{1,0:T(8,128)S(1)} %bitcast.118, ...), custom_call_target="tpu_custom_call" | custom-call | flops 2684354560 | bytes 3670016 | tf_op jit(solution)/shard_map/attend_backward/pallas_call | solution.py:426
  536.5 5.7 add_convert_fusion.5
  542.3 2.6 pad_maximum_fusion
  544.9 3.2 fusion.33
  552.1 97.7 %feed_forward_slabs.1 = (f32[16,96,128]{2,1,0:T(8,128)}, bf16[4,128,1024]{2,1,0:T(8,128)(2,1)}, bf16[4,128,1024]{2,1,0:T(8,128)(2,1)}, bf16[2,256,2048]{2,1,0:T(...) custom-call(bf16[512,1024]{1,0:T(8,128)(2,1)} %get-tuple-element.272.refs_0_.refs_1_, ...), custom_call_target="tpu_custom_call" | custom-call | flops 1610612736 | bytes 157286400 | tf_op jit(solution)/shard_map/feed_forward_slabs/pallas_call | solution.py:842
  649.8 53.0 %last_slabs.1 = (bf16[4,128,1024]{2,1,0:T(8,128)(2,1)}, bf16[4,128,1024]{2,1,0:T(8,128)(2,1)}, bf16[4,128,1024]{2,1,0:T(8,128)(2,1)}, bf16[4,128,1024]{2,1,0:T(8,128)(2,1)}, f32[2,256,2048]{2,1,0:T(8,128)}) custom-call(bf16[512,1024]{1,0:T(8,128)(2,1)} %bitcast.127, bf16[512,1024]{1,0:T(8,128)(2,1)} %get-tuple-element.272.refs_0_.refs_1_, ...), custom_call_target="tpu_custom_call" | custom-call | flops 2415919104 | bytes 104857600 | tf_op jit(solution)/shard_map/last_slabs/pallas_call | solution.py:896
  703.1 5.9 down_finish.1
  708.9 5.8 up_finish.1
  714.8 6.3 attention_finish.1
  724.3 3.3 copy.100
  (217 shorter events, 42.8 us)
Async XLA Ops:
  7.2 20.2 %copy-start = (bf16[2,1,256,2048]{3,2,1,0:T(8,128)(2,1)S(1)}, bf16[2,1,256,2048]{3,2,1,0:T(8,128)(2,1)}, u32[]{:S(2)}) copy-start(bf16[2,1,256,2048]{3,2,1,0:T(8,128)(2,1)} %param.21) | copy-start | bytes 6291460
  7.2 104.1 %all-gather.4.cloned.1.call-start = ((), (), s32[]{:S(2)}) async-start(), calls=%async_computation.6 | async-start | bytes 5242880 | tf_op jit(solution)/shard_map/all_gather | solution.py:1116
  25.1 205.4 %all-gather.6.cloned.1.call-start = ((), (), s32[]{:S(2)}) async-start(), calls=%async_computation.7 | async-start | bytes 5242880 | tf_op jit(solution)/shard_map/all_gather | solution.py:1116
  27.6 24.5 %collective-permute-start = (bf16[256,2048]{1,0:T(8,128)(2,1)S(1)}, bf16[256,2048]{1,0:T(8,128)(2,1)}, u32[]{:S(2)}, u32[]{:S(2)}) collective-permute-start(bf16[256,2048]{1,0:T(8,128)(2,1)S(1)} %fusion.84), channel_id=1, source_target_pairs={{0,2},{2,0},{4,6},{6,4},{1,3},{3,1},{5,7},{7,5},{8,10},{10,8},{12,... | collective-permute-start | bytes 3145736 | tf_op jit(solution)/shard_map/ppermute | solution.py:38
  28.2 25.7 %collective-permute-start.1 = (bf16[256,2048]{1,0:T(8,128)(2,1)S(1)}, bf16[256,2048]{1,0:T(8,128)(2,1)}, u32[]{:S(2)}, u32[]{:S(2)}) collective-permute-start(bf16[256,2048]{1,0:T(8,128)(2,1)S(1)} %fusion.84), channel_id=1, source_target_pairs={{0,4},{2,6},{4,0},{6,2},{1,5},{3,7},{5,1},{7,3},{8,12},{10,14},{12... | collective-permute-start | bytes 3145736 | tf_op jit(solution)/shard_map/ppermute | solution.py:38
  53.2 12.3 %collective-permute-start.2 = (bf16[128,2048]{1,0:T(8,128)(2,1)S(1)}, bf16[128,2048]{1,0:T(8,128)(2,1)S(1)}, u32[]{:S(2)}, u32[]{:S(2)}) collective-permute-start(bf16[128,2048]{1,0:T(8,128)(2,1)S(1)} %slice.221), channel_id=1, source_target_pairs={{0,4},{2,6},{4,0},{6,2},{1,5},{3,7},{5,1},{7,3},{8,12},{10,14},{12... | collective-permute-start | bytes 1572872 | tf_op jit(solution)/shard_map/ppermute | solution.py:38
  54.9 12.1 %collective-permute-start.3 = (bf16[128,2048]{1,0:T(8,128)(2,1)S(1)}, bf16[128,2048]{1,0:T(8,128)(2,1)S(1)}, u32[]{:S(2)}, u32[]{:S(2)}) collective-permute-start(bf16[128,2048]{1,0:T(8,128)(2,1)S(1)} %slice.222), channel_id=1, source_target_pairs={{0,2},{2,0},{4,6},{6,4},{1,3},{3,1},{5,7},{7,5},{8,10},{10,8},{12,... | collective-permute-start | bytes 1572872 | tf_op jit(solution)/shard_map/ppermute | solution.py:38
  106.9 8.0 %copy-start.27 = (f32[2,2048]{1,0:T(2,128)S(1)}, f32[2,2048]{1,0:T(2,128)}, u32[]{:S(2)}) copy-start(f32[2,2048]{1,0:T(2,128)} %param.31) | copy-start | bytes 49156
  106.9 8.0 %copy-start.29 = (f32[2,2048]{1,0:T(2,128)S(1)}, f32[2,2048]{1,0:T(2,128)}, u32[]{:S(2)}) copy-start(f32[2,2048]{1,0:T(2,128)} %param.32) | copy-start | bytes 49156
  111.3 27.5 %collective-permute-start.4 = (bf16[2048,1024]{1,0:T(8,128)(2,1)}, bf16[2048,1024]{1,0:T(8,128)(2,1)}, u32[]{:S(2)}, u32[]{:S(2)}) collective-permute-start(bf16[2048,1024]{1,0:T(8,128)(2,1)} %all-gather.4.cloned.1.call-done.refs_9_), channel_id=1, source_target_pairs={{0,1},{1,0},{2,3},{3,2},{4,5},{5,4},{6,7},{7,6},{8,9},{9,8},{10,11... | collective-permute-start | bytes 12582920 | tf_op jit(solution)/shard_map/ppermute | solution.py:34
  112.0 7.6 %collective-permute-start.5 = (f32[1536]{0:T(1024)S(1)}, f32[1536]{0:T(1024)S(1)}, u32[]{:S(2)}, u32[]{:S(2)}) collective-permute-start(f32[1536]{0:T(1024)S(1)} %pad_maximum_fusion.3), channel_id=1, source_target_pairs={{0,1},{1,0},{2,3},{3,2},{4,5},{5,4},{6,7},{7,6},{8,9},{9,8},{10,11... | collective-permute-start | bytes 18440 | tf_op jit(solution)/shard_map/ppermute | solution.py:34
  119.6 24.6 %copy-start.6 = (s32[1,1024]{0,1:T(8,128)}, s32[1,1024]{0,1:T(8,128)S(1)}, u32[]{:S(2)}) copy-start(s32[1,1024]{0,1:T(8,128)S(1)} %copy.83) | copy-start | bytes 12292
  119.7 35.7 %all-to-all-start.1 = ((bf16[4,128,1024]{2,1,0:T(8,128)(2,1)}), bf16[4,128,1024]{2,1,0:T(8,128)(2,1)S(1)}, u32[]{:S(2)}, u32[]{:S(2)}) async-start(bf16[4,128,1024]{2,1,0:T(8,128)(2,1)} %pack_attention.1), calls=%async_computation.1 | async-start | bytes 2097152 | tf_op jit(solution)/shard_map/all_to_all | solution.py:1055
  123.2 145.3 %all-gather.8.cloned.1.call-start = ((), (), s32[]{:S(2)}) async-start(), calls=%async_computation.8 | async-start | bytes 5242880 | tf_op jit(solution)/shard_map/all_gather | solution.py:1116
  130.6 8.2 %copy-start.2 = (bf16[1024,768]{1,0:T(8,128)(2,1)}, bf16[1024,768]{1,0:T(8,128)(2,1)S(1)}, u32[]{:S(2)}) copy-start(bf16[1024,768]{1,0:T(8,128)(2,1)S(1)} %add_convert_fusion.7.refs_0_.refs_1_.refs_2_) | copy-start | bytes 4718596
  155.4 75.1 %copy-start.13 = (bf16[4,128,1024]{2,1,0:T(8,128)(2,1)}, bf16[4,128,1024]{2,1,0:T(8,128)(2,1)S(1)}, u32[]{:S(2)}) copy-start(bf16[4,128,1024]{2,1,0:T(8,128)(2,1)S(1)} %all-to-all-done.1) | copy-start | bytes 3145732
  230.4 16.2 %collective-permute-start.6 = (bf16[2048,1024]{1,0:T(8,128)(2,1)}, bf16[2048,1024]{1,0:T(8,128)(2,1)}, u32[]{:S(2)}, u32[]{:S(2)}) collective-permute-start(bf16[2048,1024]{1,0:T(8,128)(2,1)} %all-gather.6.cloned.1.call-done), channel_id=1, source_target_pairs={{0,1},{1,0},{2,3},{3,2},{4,5},{5,4},{6,7},{7,6},{8,9},{9,8},{10,11... | collective-permute-start | bytes 12582920 | tf_op jit(solution)/shard_map/ppermute | solution.py:34
  230.5 38.0 %all-to-all-start.2 = ((bf16[4,128,2048]{2,1,0:T(8,128)(2,1)}), bf16[4,128,2048]{2,1,0:T(8,128)(2,1)}, u32[]{:S(2)}, u32[]{:S(2)}) async-start(bf16[4,128,2048]{2,1,0:T(8,128)(2,1)} %pad_maximum_fusion.1), calls=%async_computation.2 | async-start | bytes 4194304 | tf_op jit(solution)/shard_map/all_to_all | solution.py:1055
  235.0 317.0 %reduce-scatter.6.cloned.1.call-start = ((), (), s32[]{:S(2)}) async-start(), calls=%async_computation.10 | async-start | bytes 5242880 | tf_op jit(solution)/shard_map/reduce_scatter | solution.py:1175
  235.1 11.6 %copy-start.41 = (bf16[4,2,128,2048]{3,2,1,0:T(8,128)(2,1)S(1)}, bf16[4,2,128,2048]{3,2,1,0:T(8,128)(2,1)}, u32[]{:S(2)}) copy-start(bf16[4,2,128,2048]{3,2,1,0:T(8,128)(2,1)} %get-tuple-element.111) | copy-start | bytes 12582916
  268.5 7.4 %collective-permute-start.7 = (bf16[2048,1024]{1,0:T(8,128)(2,1)}, bf16[2048,1024]{1,0:T(8,128)(2,1)S(1)}, u32[]{:S(2)}, u32[]{:S(2)}) collective-permute-start(bf16[2048,1024]{1,0:T(8,128)(2,1)} %all-gather.8.cloned.1.call-done), channel_id=1, source_target_pairs={{0,1},{1,0},{2,3},{3,2},{4,5},{5,4},{6,7},{7,6},{8,9},{9,8},{10,11... | collective-permute-start | bytes 12582920 | tf_op jit(solution)/shard_map/ppermute | solution.py:34
  356.8 7.6 %copy-start.45 = (bf16[4,2,128,2048]{3,2,1,0:T(8,128)(2,1)S(1)}, bf16[4,2,128,2048]{3,2,1,0:T(8,128)(2,1)}, u32[]{:S(2)}) copy-start(bf16[4,2,128,2048]{3,2,1,0:T(8,128)(2,1)} %get-tuple-element.117) | copy-start | bytes 12582916
  356.8 7.6 %copy-start.48 = (bf16[1024,1024]{1,0:T(8,128)(2,1)S(1)}, bf16[1024,1024]{1,0:T(8,128)(2,1)}, u32[]{:S(2)}) copy-start(bf16[1024,1024]{1,0:T(8,128)(2,1)} %get-tuple-element.301) | copy-start | bytes 6291460
  369.3 8.1 %collective-permute-start.8 = (bf16[2048,1024]{1,0:T(8,128)(2,1)S(1)}, bf16[2048,1024]{1,0:T(8,128)(2,1)}, u32[]{:S(2)}, u32[]{:S(2)}) collective-permute-start(bf16[2048,1024]{1,0:T(8,128)(2,1)S(1)} %convolution_convert_fusion.1), channel_id=1, source_target_pairs={{0,1},{1,0},{2,3},{3,2},{4,5},{5,4},{6,7},{7,6},{8,9},{9,8},{10,11... | collective-permute-start | bytes 12582920 | tf_op jit(solution)/shard_map/ppermute | solution.py:34
  383.3 168.8 %reduce-scatter.4.cloned.1.call-start = ((), (), s32[]{:S(2)}) async-start(), calls=%async_computation.9 | async-start | bytes 5242880 | tf_op jit(solution)/shard_map/reduce_scatter | solution.py:1175
  383.3 12.5 %copy-start.42 = (bf16[4,2,128,2048]{3,2,1,0:T(8,128)(2,1)S(1)}, bf16[4,2,128,2048]{3,2,1,0:T(8,128)(2,1)}, u32[]{:S(2)}) copy-start(bf16[4,2,128,2048]{3,2,1,0:T(8,128)(2,1)} %get-tuple-element.111) | copy-start | bytes 12582916
  402.4 9.7 %copy-start.15 = (bf16[1024,1024]{1,0:T(8,128)(2,1)S(1)}, bf16[1024,1024]{1,0:T(8,128)(2,1)}, u32[]{:S(2)}) copy-start(bf16[1024,1024]{1,0:T(8,128)(2,1)} %fusion.6) | copy-start | bytes 6291460
  402.4 9.7 %copy-start.40 = (bf16[2048,1024]{1,0:T(8,128)(2,1)S(1)}, bf16[2048,1024]{1,0:T(8,128)(2,1)}, u32[]{:S(2)}) copy-start(bf16[2048,1024]{1,0:T(8,128)(2,1)} %all-gather.6.cloned.1.call-done) | copy-start | bytes 12582916
  402.4 18.1 %collective-permute-start.9 = (bf16[2048,1024]{1,0:T(8,128)(2,1)}, bf16[2048,1024]{1,0:T(8,128)(2,1)S(1)}, u32[]{:S(2)}, u32[]{:S(2)}) collective-permute-start(bf16[2048,1024]{1,0:T(8,128)(2,1)} %convolution_convert_fusion), channel_id=1, source_target_pairs={{0,1},{1,0},{2,3},{3,2},{4,5},{5,4},{6,7},{7,6},{8,9},{9,8},{10,11... | collective-permute-start | bytes 12582920 | tf_op jit(solution)/shard_map/ppermute | solution.py:34
  426.9 222.9 %reduce-scatter.8.cloned.1.call-start = ((), (), s32[]{:S(2)}) async-start(), calls=%async_computation.11 | async-start | bytes 5242880 | tf_op jit(solution)/shard_map/reduce_scatter | solution.py:1175
  503.9 10.4 %copy-start.19 = (bf16[1024,2048]{1,0:T(8,128)(2,1)S(1)}, bf16[1024,2048]{1,0:T(8,128)(2,1)}, u32[]{:S(2)}) copy-start(bf16[1024,2048]{1,0:T(8,128)(2,1)} %copy-done.17) | copy-start | bytes 12582916
  514.3 35.6 %copy-start.4 = (bf16[1024,768]{1,0:T(8,128)(2,1)}, bf16[1024,768]{1,0:T(8,128)(2,1)S(1)}, u32[]{:S(2)}) copy-start(bf16[1024,768]{1,0:T(8,128)(2,1)S(1)} %attend_backward.2.refs_8_) | copy-start | bytes 4718596
  519.3 17.3 %collective-permute-start.10 = (bf16[2048,768]{1,0:T(8,128)(2,1)}, bf16[2048,768]{1,0:T(8,128)(2,1)}, u32[]{:S(2)}, u32[]{:S(2)}) collective-permute-start(bf16[2048,768]{1,0:T(8,128)(2,1)} %convolution_convert_fusion.2), channel_id=1, source_target_pairs={{0,1},{1,0},{2,3},{3,2},{4,5},{5,4},{6,7},{7,6},{8,9},{9,8},{10,11... | collective-permute-start | bytes 9437192 | tf_op jit(solution)/shard_map/ppermute | solution.py:34
  521.6 13.4 %collective-permute-start.11 = (bf16[2048,256]{1,0:T(8,128)(2,1)}, bf16[2048,256]{1,0:T(8,128)(2,1)S(1)}, u32[]{:S(2)}, u32[]{:S(2)}) collective-permute-start(bf16[2048,256]{1,0:T(8,128)(2,1)} %convolution_convert_fusion.3), channel_id=1, source_target_pairs={{0,1},{1,0},{2,3},{3,2},{4,5},{5,4},{6,7},{7,6},{8,9},{9,8},{10,11... | collective-permute-start | bytes 3145736 | tf_op jit(solution)/shard_map/ppermute | solution.py:34
  524.6 10.5 %copy-start.9 = (bf16[1024,256]{1,0:T(8,128)(2,1)S(1)}, bf16[1024,256]{1,0:T(8,128)(2,1)}, u32[]{:S(2)}) copy-start(bf16[1024,256]{1,0:T(8,128)(2,1)} %copy-done.8) | copy-start | bytes 1572868
  535.1 14.5 %copy-start.5 = (bf16[1024,768]{1,0:T(8,128)(2,1)}, bf16[1024,768]{1,0:T(8,128)(2,1)S(1)}, u32[]{:S(2)}) copy-start(bf16[1024,768]{1,0:T(8,128)(2,1)S(1)} %attend_backward.3.refs_7_) | copy-start | bytes 4718596
  649.8 53.1 %copy-start.20 = (f32[192,128]{1,0:T(8,128)S(1)}, f32[192,128]{1,0:T(8,128)}, u32[]{:S(2)}) copy-start(f32[192,128]{1,0:T(8,128)} %get-tuple-element.147) | copy-start | bytes 294916
  702.9 18.2 %copy-start.23 = (f32[1,4096]{1,0:T(1,128)}, f32[1,4096]{1,0:T(1,128)S(1)}, u32[]{:S(2)}) copy-start(f32[1,4096]{1,0:T(1,128)S(1)} %constant_dynamic-slice_fusion.1) | copy-start | bytes 49156
  703.0 18.8 %copy-start.24 = (f32[2,2048]{1,0:T(2,128)}, f32[2,2048]{1,0:T(2,128)S(1)}, u32[]{:S(2)}) copy-start(f32[2,2048]{1,0:T(2,128)S(1)} %slice.214) | copy-start | bytes 49156
  703.0 19.4 %copy-start.25 = (f32[2,2048]{1,0:T(2,128)}, f32[2,2048]{1,0:T(2,128)S(1)}, u32[]{:S(2)}) copy-start(f32[2,2048]{1,0:T(2,128)S(1)} %slice.216) | copy-start | bytes 49156
  703.0 20.0 %copy-start.26 = (f32[2,2048]{1,0:T(2,128)}, f32[2,2048]{1,0:T(2,128)S(1)}, u32[]{:S(2)}) copy-start(f32[2,2048]{1,0:T(2,128)S(1)} %slice.218) | copy-start | bytes 49156
  714.8 7.7 %copy-start.28 = (f32[2,2048]{1,0:T(2,128)S(1)}, f32[2,2048]{1,0:T(2,128)}, u32[]{:S(2)}) copy-start(f32[2,2048]{1,0:T(2,128)} %param.31) | copy-start | bytes 49156
  714.8 7.6 %copy-start.36 = (f32[2,2048]{1,0:T(2,128)S(1)}, f32[2,2048]{1,0:T(2,128)}, u32[]{:S(2)}) copy-start(f32[2,2048]{1,0:T(2,128)} %param.40) | copy-start | bytes 49156
  714.8 8.3 %copy-start.30 = (f32[2,2048]{1,0:T(2,128)S(1)}, f32[2,2048]{1,0:T(2,128)}, u32[]{:S(2)}) copy-start(f32[2,2048]{1,0:T(2,128)} %param.32) | copy-start | bytes 49156
  714.8 8.3 %copy-start.37 = (f32[2,2048]{1,0:T(2,128)S(1)}, f32[2,2048]{1,0:T(2,128)}, u32[]{:S(2)}) copy-start(f32[2,2048]{1,0:T(2,128)} %param.41) | copy-start | bytes 49156
  714.8 8.9 %copy-start.33 = (f32[2,1024]{1,0:T(2,128)S(1)}, f32[2,1024]{1,0:T(2,128)}, u32[]{:S(2)}) copy-start(f32[2,1024]{1,0:T(2,128)} %param.28) | copy-start | bytes 24580
  714.8 8.9 %copy-start.38 = (f32[2,1024]{1,0:T(2,128)S(1)}, f32[2,1024]{1,0:T(2,128)}, u32[]{:S(2)}) copy-start(f32[2,1024]{1,0:T(2,128)} %param.37) | copy-start | bytes 24580
  714.8 12.8 %copy-start.14 = (f32[2,256,2048]{2,1,0:T(8,128)S(1)}, f32[2,256,2048]{2,1,0:T(8,128)}, u32[]{:S(2)}) copy-start(f32[2,256,2048]{2,1,0:T(8,128)} %get-tuple-element.143) | copy-start | bytes 12582916
  (22 other events, 106.0 us)
Sparse Core Ops, SparseCore 0:
  25.2 80.3 all-gather.3
  107.7 79.2 all-gather.5
  189.2 79.2 all-gather.7
  383.4 74.4 reduce-scatter.5
  460.2 77.2 reduce-scatter.3
  545.0 102.3 reduce-scatter.7

commit v6 on v5

--- a/solution.py
+++ b/solution.py
@@ -1170,7 +1170,8 @@
     )
 
     def pair_sum(terms):
-        return (terms[0] + swap_core(terms[1].astype(bf16)).astype(f32)).astype(bf16)
+        own, other = (term.astype(bf16) for term in terms)
+        return (own.astype(f32) + swap_core(other).astype(f32)).astype(bf16)
 
     scatter_z = lambda v: lax.psum_scatter(v, "fsdp", scatter_dimension=0, tiled=True)
     term_down = [None, mm(branch_all, active[1], (0, 0)).astype(bf16)]

time: 742 us -> 742 us (level)
  no operation moved by 1% of the time
where the time goes in v6:
time: 742 us; the launch traced here: 737 us
  Pallas kernels  445 us (60%)
  matrix products  139 us (19%)
  waiting for transfers between devices  38.6 us (5%)
  local copies, waits for them, and re-layouts  36.9 us (5%)
  blocking collectives  27.7 us (4%)
  other arithmetic  21.1 us (3%)
  between operations  15.5 us (2%)
  starting transfers between devices  13.4 us (2%)
    pallas_call x3, Pallas kernels, exchange(): pl.pallas_call(staged(kernel, len(operands), n_in, 2 + len(out_types)), o...  222 us
    dot_general x22, matrix products, mm(): lax.dot_general(left, right, ((dims[:1], dims[1:]), ((), ())), preferred_...  139 us
    pallas_call x1, Pallas kernels, feed_forward_slabs(): pl.pallas_call(staged(feed_forward_kernel, 11, 11, 6), out_shape=[jax.Sha...  97.7 us
    pallas_call x1, Pallas kernels, last_slabs(): pl.pallas_call(staged(last_kernel, 8, 8, 5), out_shape=[*[block] * 4, jax...  53 us
    all_to_all x1, blocking collectives, over_ctx(): return lax.all_to_all(stack, 'ctx', split_axis=0, concat_axis=0, tiled=True)  27.7 us
    ppermute x4, waiting for transfers between devices, swap_ctx(): return lax.ppermute(value, 'ctx', xor_pairs(4, mask))  25.3 us
    pallas_call x2, Pallas kernels, attend_backward(): pl.pallas_call(lambda *refs: attend_back_kernel(256, heads, *refs), out_s...  21 us
    pallas_call x3, Pallas kernels, finish(): pl.pallas_call(kernel, out_shape=[jax.ShapeDtypeStruct(s.shape, f32) for...  18 us
  transfers between devices with their start and end apart: 20, of which 5 were waited for; matrix products, arithmetic and copies ran while one was open for 22% of the time, Pallas kernels for 38%

profile of v6, /device:TPU:0, one launch (start us, length us, event | category | flops | bytes accessed | tf_op | source)
XLA Modules:
  0.0 737.3 jit_solution(7604520872135740736)
XLA Ops:
  7.3 17.8 %attention_block.1 = bf16[4,128,1024]{2,1,0:T(8,128)(2,1)} custom-call(f32[3,128,1024]{2,1,0:T(8,128)} %refs_2_.1, f32[1024,128]{1,0:T(8,128)} %refs_3_.1), custom_call_target="tpu_custom_call" | custom-call | flops 393216 | bytes 31457280 | tf_op jit(solution)/shard_map/attention_block/pallas_call | solution.py:980
  29.0 2.5 copy.69
  34.9 17.2 %collective-permute-done = bf16[256,2048]{1,0:T(8,128)(2,1)} collective-permute-done((bf16[256,2048]{1,0:T(8,128)(2,1)S(1)}, bf16[256,2048]{1,0:T(8,128)(2,1)}, u32[]{:S(2)}, u32[]{:S(2)}) %collective-permute-start) | collective-permute-done | bytes 1048608 | tf_op jit(solution)/shard_map/ppermute | solution.py:38
  58.9 6.5 collective-permute-done.2
  69.1 27.7 %all_to_all.15 = bf16[4,128,2048]{1,2,0:T(8,128)(2,1)} all-to-all(bf16[4,128,2048]{1,2,0:T(8,128)(2,1)S(1)} %pad_maximum_fusion.2), channel_id=1, replica_groups=mesh['fsdp'=4,'ctx'=4,'tp'=2] {'ctx'}, dimensions={0} | all-to-all | bytes 4194304 | tf_op jit(solution)/shard_map/all_to_all | solution.py:1055
  96.8 3.9 copy.70
  100.8 3.0 fusion.33
  108.2 3.1 pad_maximum_fusion.1
  115.6 3.8 pack_attention.1
  119.7 3.5 all-to-all-start.1
  123.9 6.6 add_convert_fusion.7.refs_0_.refs_1_.refs_2_
  130.6 5.5 attend_forward.2
  136.1 2.7 fusion.26
  138.8 5.3 add_convert_fusion.6.refs_0_.refs_1_.refs_2_
  144.2 5.9 attend_forward.3
  150.8 4.6 add_convert_fusion.4
  155.4 75.0 %first_rows.1 = (bf16[4,2,128,2048]{3,2,1,0:T(8,128)(2,1)}, f32[2,128,2048]{2,1,0:T(8,128)}, f32[2,128,2048]{2,1,0:T(8,128)}, f32[8,2048]{1,0:T(8,128)}) custom-call(bf16[2,2,2,128,2048]{4,3,2,1,0:T(8,128)(2,1)} %bitcast.124, bf16[2,128,2048]{2,1,0:T(8,128)(2,1)} %bitcast.126, f32[1,2048]{1,0:T(1,128)} %get-tuple-element.288.refs_2_, ...), custom_call_target="tpu_custom_call" | custom-call | flops 31457280 | bytes 136314880 | tf_op jit(solution)/shard_map/first_rows/pallas_call | solution.py:290
  230.5 4.5 all-to-all-start.2
  235.1 11.6 %multiply_convert_fusion.1 = (bf16[1024,1024]{1,0:T(8,128)(2,1)}, f32[1024,1024]{1,0:T(8,128)}) fusion(f32[1024]{0:T(1024)S(1)} %dynamic_slice.29, bf16[1024,2048]{1,0:T(8,128)(2,1)} %bitcast.161, bf16[2048,1024]{1,0:T(8,128)(2,1)} %all-gather.6.cloned.1.call-done), kind=kOutput, calls=%fused_computation.29 | convolution fusion | flops 4305453056 | bytes 14684160 | tf_op jit(solution)/shard_map/dot_general | solution.py:46
  246.7 9.4 %multiply_convert_fusion = (bf16[1024,1024]{1,0:T(8,128)(2,1)}, f32[1024,1024]{1,0:T(8,128)}) fusion(f32[1024]{0:T(1024)S(1)} %slice.231, bf16[1024,2048]{1,0:T(8,128)(2,1)S(1)} %bitcast.162, bf16[2048,1024]{1,0:T(8,128)(2,1)} %collective-permute-done.6), kind=kOutput, calls=%fused_computation.28 | convolution fusion | flops 4305453056 | bytes 14684160 | tf_op jit(solution)/shard_map/dot_general | solution.py:46
  256.1 12.5 %all-gather.8.cloned.1.call-done = bf16[2048,1024]{1,0:T(8,128)(2,1)} async-done(((bf16[512,1024]{1,0:T(8,128)(2,1)}), bf16[2048,1024]{1,0:T(8,128)(2,1)}) %all-gather.8.cloned.1.call-update) | async-done | bytes 4194320 | tf_op jit(solution)/shard_map/all_gather | solution.py:1116
  268.5 7.2 fusion.44
  275.9 6.4 add_convert_fusion.3
  282.3 74.5 %second_rows.1 = (bf16[4,2,128,2048]{3,2,1,0:T(8,128)(2,1)}, bf16[2,128,2048]{2,1,0:T(8,128)(2,1)}, f32[2,128,2048]{2,1,0:T(8,128)}, f32[8,2048]{1,0:T(8,128)}) custom-call(bf16[2,2,2,128,2048]{4,3,2,1,0:T(8,128)(2,1)} %bitcast.133, f32[2,128,2048]{2,1,0:T(8,128)} %get-tuple-element.115.refs_1_, bf16[2,128,2048]{2,1,0:T(8,128)(2,1)} %bitcast.136, ...), custom_call_target="tpu_custom_call" | custom-call | flops 31457280 | bytes 136314880 | tf_op jit(solution)/shard_map/second_rows/pallas_call | solution.py:290
  356.9 7.6 %convolution_convert_fusion.1 = bf16[2048,1024]{1,0:T(8,128)(2,1)S(1)} fusion(bf16[1024,2048]{1,0:T(8,128)(2,1)} %bitcast.165, bf16[1024,1024]{1,0:T(8,128)(2,1)} %get-tuple-element.303), kind=kOutput, calls=%fused_computation.31 | convolution fusion | flops 4297064448 | bytes 10485760 | tf_op jit(solution)/shard_map/dot_general | solution.py:46
  364.5 4.9 fusion.45
  369.5 8.2 %fusion.6 = bf16[1024,1024]{1,0:T(8,128)(2,1)} fusion(f32[1024,1024]{1,0:T(8,128)S(1)} %copy-done.48, f32[1024]{0:T(1024)S(1)} %dynamic_slice.29, bf16[1024,2048]{1,0:T(8,128)(2,1)S(1)} %bitcast.168, bf16[2048,1024]{1,0:T(8,128)(2,1)S(1)} %copy-done.43), kind=kOutput, calls=%fused_computation.17 | convolution fusion | flops 4316987392 | bytes 14684160 | tf_op jit(solution)/shard_map/dot_general | solution.py:46
  377.7 4.3 add_convert_fusion.2
  382.0 12.4 %convert_reduce_fusion = (f32[1024]{0:T(1024)S(1)}, bf16[1024,1024]{1,0:T(8,128)(2,1)S(1)}) fusion(f32[1024,1024]{1,0:T(8,128)} %get-tuple-element.304, f32[1024]{0:T(1024)S(1)} %slice.231, bf16[1024,2048]{1,0:T(8,128)(2,1)} %bitcast.166, bf16[2048,1024]{1,0:T(8,128)(2,1)} %copy-done.44), kind=kOutput, calls=%fused_computation.26 | convolution fusion | flops 4319083520 | bytes 14688256 | tf_op jit(solution)/shard_map/dot_general | solution.py:46
  394.5 6.6 convolution_convert_fusion
  401.6 9.2 %fusion.46 = f32[1024,2048]{1,0:T(8,128)} fusion(bf16[1024,1024]{1,0:T(8,128)(2,1)S(1)} %get-tuple-element.268, bf16[2048,1024]{1,0:T(8,128)(2,1)} %collective-permute-done.6), kind=kOutput, calls=%fused_computation.115 | convolution fusion | flops 4294967296 | bytes 14680064 | tf_op jit(solution)/shard_map/dot_general | solution.py:46
  410.8 8.4 %add_convert_fusion.1 = bf16[1024,2048]{1,0:T(8,128)(2,1)} fusion(f32[1024,2048]{1,0:T(8,128)} %fusion.46, bf16[1024,1024]{1,0:T(8,128)(2,1)S(1)} %copy-done.15, bf16[2048,1024]{1,0:T(8,128)(2,1)S(1)} %copy-done.40), kind=kOutput, calls=%fused_computation.2 | convolution fusion | flops 4299161600 | bytes 18874368 | tf_op jit(solution)/shard_map/dot_general | solution.py:46
  419.2 6.4 add_convert_fusion
  425.7 73.0 %third_rows.1 = (bf16[4,2,128,2048]{3,2,1,0:T(8,128)(2,1)}, f32[2,128,2048]{2,1,0:T(8,128)}, f32[8,2048]{1,0:T(8,128)}) custom-call(bf16[2,2,2,128,2048]{4,3,2,1,0:T(8,128)(2,1)} %bitcast.132, f32[2,128,2048]{2,1,0:T(8,128)} %get-tuple-element.115.refs_1_, f32[2,128,2048]{2,1,0:T(8,128)} %get-tuple-element.128.refs_2_, ...), custom_call_target="tpu_custom_call" | custom-call | flops 31457280 | bytes 136314880 | tf_op jit(solution)/shard_map/third_rows/pallas_call | solution.py:290
  498.7 3.9 convolution_convert_fusion.7.refs_3_
  502.6 10.4 %attend_backward.2.refs_8_ = bf16[1024,768]{1,0:T(8,128)(2,1)S(1)} custom-call(bf16[1024,768]{1,0:T(8,128)(2,1)S(1)} %add_convert_fusion.6.refs_0_.refs_1_.refs_2_, bf16[1024,768]{1,0:T(8,128)(2,1)S(1)} %add_convert_fusion.6.refs_0_.refs_1_.refs_2_, bf16[1024,768]{1,0:T(8,128)(2,1)S(1)} %add_convert_fusion.6.refs_0_.refs_1_.refs_2_, ...), custom_call_target="tpu_custom_call" | custom-call | flops 2684354560 | bytes 3670016 | tf_op jit(solution)/shard_map/attend_backward/pallas_call | solution.py:426
  513.0 5.1 convolution_convert_fusion.3
  521.0 2.5 convolution_convert_fusion.6.refs_3_
  523.5 10.6 %attend_backward.3.refs_7_ = bf16[1024,768]{1,0:T(8,128)(2,1)S(1)} custom-call(bf16[1024,768]{1,0:T(8,128)(2,1)S(1)} %copy-done.3, bf16[1024,768]{1,0:T(8,128)(2,1)S(1)} %copy-done.3, bf16[1024,768]{1,0:T(8,128)(2,1)S(1)} %copy-done.3, bf16[1024,256]{1,0:T(8,128)(2,1)S(1)} %convolution_convert_fusion.6.refs_3_, s32[1024,1]{1,0:T(8,128)S(1)} %bitcast.118, ...), custom_call_target="tpu_custom_call" | custom-call | flops 2684354560 | bytes 3670016 | tf_op jit(solution)/shard_map/attend_backward/pallas_call | solution.py:426
  534.1 6.4 convolution_convert_fusion.2
  542.9 2.6 pad_maximum_fusion
  545.5 3.2 fusion.34
  552.7 97.7 %feed_forward_slabs.1 = (f32[16,96,128]{2,1,0:T(8,128)}, bf16[4,128,1024]{2,1,0:T(8,128)(2,1)}, bf16[4,128,1024]{2,1,0:T(8,128)(2,1)}, bf16[2,256,2048]{2,1,0:T(...) custom-call(bf16[512,1024]{1,0:T(8,128)(2,1)} %get-tuple-element.272.refs_0_.refs_1_, ...), custom_call_target="tpu_custom_call" | custom-call | flops 1610612736 | bytes 157286400 | tf_op jit(solution)/shard_map/feed_forward_slabs/pallas_call | solution.py:842
  650.4 53.0 %last_slabs.1 = (bf16[4,128,1024]{2,1,0:T(8,128)(2,1)}, bf16[4,128,1024]{2,1,0:T(8,128)(2,1)}, bf16[4,128,1024]{2,1,0:T(8,128)(2,1)}, bf16[4,128,1024]{2,1,0:T(8,128)(2,1)}, f32[2,256,2048]{2,1,0:T(8,128)}) custom-call(bf16[512,1024]{1,0:T(8,128)(2,1)} %bitcast.127, bf16[512,1024]{1,0:T(8,128)(2,1)} %get-tuple-element.272.refs_0_.refs_1_, ...), custom_call_target="tpu_custom_call" | custom-call | flops 2415919104 | bytes 104857600 | tf_op jit(solution)/shard_map/last_slabs/pallas_call | solution.py:896
  703.7 5.9 down_finish.1
  709.6 5.8 up_finish.1
  715.5 6.3 attention_finish.1
  724.9 3.3 copy.100
  (220 shorter events, 43.7 us)
Async XLA Ops:
  7.2 20.2 %copy-start = (bf16[2,1,256,2048]{3,2,1,0:T(8,128)(2,1)S(1)}, bf16[2,1,256,2048]{3,2,1,0:T(8,128)(2,1)}, u32[]{:S(2)}) copy-start(bf16[2,1,256,2048]{3,2,1,0:T(8,128)(2,1)} %param.21) | copy-start | bytes 6291460
  7.2 104.1 %all-gather.4.cloned.1.call-start = ((), (), s32[]{:S(2)}) async-start(), calls=%async_computation.6 | async-start | bytes 5242880 | tf_op jit(solution)/shard_map/all_gather | solution.py:1116
  25.1 205.3 %all-gather.6.cloned.1.call-start = ((), (), s32[]{:S(2)}) async-start(), calls=%async_computation.7 | async-start | bytes 5242880 | tf_op jit(solution)/shard_map/all_gather | solution.py:1116
  27.6 24.5 %collective-permute-start = (bf16[256,2048]{1,0:T(8,128)(2,1)S(1)}, bf16[256,2048]{1,0:T(8,128)(2,1)}, u32[]{:S(2)}, u32[]{:S(2)}) collective-permute-start(bf16[256,2048]{1,0:T(8,128)(2,1)S(1)} %fusion.85), channel_id=1, source_target_pairs={{0,2},{2,0},{4,6},{6,4},{1,3},{3,1},{5,7},{7,5},{8,10},{10,8},{12,... | collective-permute-start | bytes 3145736 | tf_op jit(solution)/shard_map/ppermute | solution.py:38
  28.2 25.7 %collective-permute-start.1 = (bf16[256,2048]{1,0:T(8,128)(2,1)S(1)}, bf16[256,2048]{1,0:T(8,128)(2,1)}, u32[]{:S(2)}, u32[]{:S(2)}) collective-permute-start(bf16[256,2048]{1,0:T(8,128)(2,1)S(1)} %fusion.85), channel_id=1, source_target_pairs={{0,4},{2,6},{4,0},{6,2},{1,5},{3,7},{5,1},{7,3},{8,12},{10,14},{12... | collective-permute-start | bytes 3145736 | tf_op jit(solution)/shard_map/ppermute | solution.py:38
  53.2 12.3 %collective-permute-start.2 = (bf16[128,2048]{1,0:T(8,128)(2,1)S(1)}, bf16[128,2048]{1,0:T(8,128)(2,1)S(1)}, u32[]{:S(2)}, u32[]{:S(2)}) collective-permute-start(bf16[128,2048]{1,0:T(8,128)(2,1)S(1)} %slice.221), channel_id=1, source_target_pairs={{0,4},{2,6},{4,0},{6,2},{1,5},{3,7},{5,1},{7,3},{8,12},{10,14},{12... | collective-permute-start | bytes 1572872 | tf_op jit(solution)/shard_map/ppermute | solution.py:38
  54.9 12.1 %collective-permute-start.3 = (bf16[128,2048]{1,0:T(8,128)(2,1)S(1)}, bf16[128,2048]{1,0:T(8,128)(2,1)S(1)}, u32[]{:S(2)}, u32[]{:S(2)}) collective-permute-start(bf16[128,2048]{1,0:T(8,128)(2,1)S(1)} %slice.222), channel_id=1, source_target_pairs={{0,2},{2,0},{4,6},{6,4},{1,3},{3,1},{5,7},{7,5},{8,10},{10,8},{12,... | collective-permute-start | bytes 1572872 | tf_op jit(solution)/shard_map/ppermute | solution.py:38
  106.9 7.4 %copy-start.21 = (f32[2,2048]{1,0:T(2,128)S(1)}, f32[2,2048]{1,0:T(2,128)}, u32[]{:S(2)}) copy-start(f32[2,2048]{1,0:T(2,128)} %param.30) | copy-start | bytes 49156
  106.9 8.0 %copy-start.27 = (f32[2,2048]{1,0:T(2,128)S(1)}, f32[2,2048]{1,0:T(2,128)}, u32[]{:S(2)}) copy-start(f32[2,2048]{1,0:T(2,128)} %param.31) | copy-start | bytes 49156
  106.9 8.0 %copy-start.29 = (f32[2,2048]{1,0:T(2,128)S(1)}, f32[2,2048]{1,0:T(2,128)}, u32[]{:S(2)}) copy-start(f32[2,2048]{1,0:T(2,128)} %param.32) | copy-start | bytes 49156
  111.3 27.5 %collective-permute-start.4 = (bf16[2048,1024]{1,0:T(8,128)(2,1)}, bf16[2048,1024]{1,0:T(8,128)(2,1)}, u32[]{:S(2)}, u32[]{:S(2)}) collective-permute-start(bf16[2048,1024]{1,0:T(8,128)(2,1)} %all-gather.4.cloned.1.call-done.refs_9_), channel_id=1, source_target_pairs={{0,1},{1,0},{2,3},{3,2},{4,5},{5,4},{6,7},{7,6},{8,9},{9,8},{10,11... | collective-permute-start | bytes 12582920 | tf_op jit(solution)/shard_map/ppermute | solution.py:34
  112.0 7.6 %collective-permute-start.5 = (f32[1536]{0:T(1024)S(1)}, f32[1536]{0:T(1024)S(1)}, u32[]{:S(2)}, u32[]{:S(2)}) collective-permute-start(f32[1536]{0:T(1024)S(1)} %pad_maximum_fusion.3), channel_id=1, source_target_pairs={{0,1},{1,0},{2,3},{3,2},{4,5},{5,4},{6,7},{7,6},{8,9},{9,8},{10,11... | collective-permute-start | bytes 18440 | tf_op jit(solution)/shard_map/ppermute | solution.py:34
  119.6 24.6 %copy-start.6 = (s32[1,1024]{0,1:T(8,128)}, s32[1,1024]{0,1:T(8,128)S(1)}, u32[]{:S(2)}) copy-start(s32[1,1024]{0,1:T(8,128)S(1)} %copy.83) | copy-start | bytes 12292
  119.7 35.7 %all-to-all-start.1 = ((bf16[4,128,1024]{2,1,0:T(8,128)(2,1)}), bf16[4,128,1024]{2,1,0:T(8,128)(2,1)S(1)}, u32[]{:S(2)}, u32[]{:S(2)}) async-start(bf16[4,128,1024]{2,1,0:T(8,128)(2,1)} %pack_attention.1), calls=%async_computation.1 | async-start | bytes 2097152 | tf_op jit(solution)/shard_map/all_to_all | solution.py:1055
  123.2 145.3 %all-gather.8.cloned.1.call-start = ((), (), s32[]{:S(2)}) async-start(), calls=%async_computation.8 | async-start | bytes 5242880 | tf_op jit(solution)/shard_map/all_gather | solution.py:1116
  130.6 8.2 %copy-start.2 = (bf16[1024,768]{1,0:T(8,128)(2,1)}, bf16[1024,768]{1,0:T(8,128)(2,1)S(1)}, u32[]{:S(2)}) copy-start(bf16[1024,768]{1,0:T(8,128)(2,1)S(1)} %add_convert_fusion.7.refs_0_.refs_1_.refs_2_) | copy-start | bytes 4718596
  155.4 75.1 %copy-start.13 = (bf16[4,128,1024]{2,1,0:T(8,128)(2,1)}, bf16[4,128,1024]{2,1,0:T(8,128)(2,1)S(1)}, u32[]{:S(2)}) copy-start(bf16[4,128,1024]{2,1,0:T(8,128)(2,1)S(1)} %all-to-all-done.1) | copy-start | bytes 3145732
  230.4 16.2 %collective-permute-start.6 = (bf16[2048,1024]{1,0:T(8,128)(2,1)}, bf16[2048,1024]{1,0:T(8,128)(2,1)}, u32[]{:S(2)}, u32[]{:S(2)}) collective-permute-start(bf16[2048,1024]{1,0:T(8,128)(2,1)} %all-gather.6.cloned.1.call-done), channel_id=1, source_target_pairs={{0,1},{1,0},{2,3},{3,2},{4,5},{5,4},{6,7},{7,6},{8,9},{9,8},{10,11... | collective-permute-start | bytes 12582920 | tf_op jit(solution)/shard_map/ppermute | solution.py:34
  230.5 38.0 %all-to-all-start.2 = ((bf16[4,128,2048]{2,1,0:T(8,128)(2,1)}), bf16[4,128,2048]{2,1,0:T(8,128)(2,1)}, u32[]{:S(2)}, u32[]{:S(2)}) async-start(bf16[4,128,2048]{2,1,0:T(8,128)(2,1)} %pad_maximum_fusion.1), calls=%async_computation.2 | async-start | bytes 4194304 | tf_op jit(solution)/shard_map/all_to_all | solution.py:1055
  235.0 317.7 %reduce-scatter.6.cloned.1.call-start = ((), (), s32[]{:S(2)}) async-start(), calls=%async_computation.10 | async-start | bytes 5242880 | tf_op jit(solution)/shard_map/reduce_scatter | solution.py:1176
  235.1 11.6 %copy-start.41 = (bf16[4,2,128,2048]{3,2,1,0:T(8,128)(2,1)S(1)}, bf16[4,2,128,2048]{3,2,1,0:T(8,128)(2,1)}, u32[]{:S(2)}) copy-start(bf16[4,2,128,2048]{3,2,1,0:T(8,128)(2,1)} %get-tuple-element.111) | copy-start | bytes 12582916
  268.5 7.4 collective-permute-start.7
  356.8 7.6 %copy-start.45 = (bf16[4,2,128,2048]{3,2,1,0:T(8,128)(2,1)S(1)}, bf16[4,2,128,2048]{3,2,1,0:T(8,128)(2,1)}, u32[]{:S(2)}) copy-start(bf16[4,2,128,2048]{3,2,1,0:T(8,128)(2,1)} %get-tuple-element.117) | copy-start | bytes 12582916
  356.8 7.6 %copy-start.49 = (bf16[1024,1024]{1,0:T(8,128)(2,1)S(1)}, bf16[1024,1024]{1,0:T(8,128)(2,1)}, u32[]{:S(2)}) copy-start(bf16[1024,1024]{1,0:T(8,128)(2,1)} %get-tuple-element.301) | copy-start | bytes 6291460
  369.4 8.3 %collective-permute-start.8 = (bf16[2048,1024]{1,0:T(8,128)(2,1)S(1)}, bf16[2048,1024]{1,0:T(8,128)(2,1)S(1)}, u32[]{:S(2)}, u32[]{:S(2)}) collective-permute-start(bf16[2048,1024]{1,0:T(8,128)(2,1)S(1)} %convolution_convert_fusion.1), channel_id=1, source_target_pairs={{0,1},{1,0},{2,3},{3,2},{4,5},{5,4},{6,7},{7,6},{8,9},{9,8},{10,11... | collective-permute-start | bytes 12582920 | tf_op jit(solution)/shard_map/ppermute | solution.py:34
  382.0 170.7 %reduce-scatter.4.cloned.1.call-start = ((), (), s32[]{:S(2)}) async-start(), calls=%async_computation.9 | async-start | bytes 5242880 | tf_op jit(solution)/shard_map/reduce_scatter | solution.py:1176
  382.0 12.5 %copy-start.42 = (bf16[4,2,128,2048]{3,2,1,0:T(8,128)(2,1)S(1)}, bf16[4,2,128,2048]{3,2,1,0:T(8,128)(2,1)}, u32[]{:S(2)}) copy-start(bf16[4,2,128,2048]{3,2,1,0:T(8,128)(2,1)} %get-tuple-element.111) | copy-start | bytes 12582916
  401.1 9.7 %copy-start.15 = (bf16[1024,1024]{1,0:T(8,128)(2,1)S(1)}, bf16[1024,1024]{1,0:T(8,128)(2,1)}, u32[]{:S(2)}) copy-start(bf16[1024,1024]{1,0:T(8,128)(2,1)} %fusion.6) | copy-start | bytes 6291460
  401.1 9.7 %copy-start.40 = (bf16[2048,1024]{1,0:T(8,128)(2,1)S(1)}, bf16[2048,1024]{1,0:T(8,128)(2,1)}, u32[]{:S(2)}) copy-start(bf16[2048,1024]{1,0:T(8,128)(2,1)} %all-gather.6.cloned.1.call-done) | copy-start | bytes 12582916
  401.1 18.1 %collective-permute-start.9 = (bf16[2048,1024]{1,0:T(8,128)(2,1)}, bf16[2048,1024]{1,0:T(8,128)(2,1)S(1)}, u32[]{:S(2)}, u32[]{:S(2)}) collective-permute-start(bf16[2048,1024]{1,0:T(8,128)(2,1)} %convolution_convert_fusion), channel_id=1, source_target_pairs={{0,1},{1,0},{2,3},{3,2},{4,5},{5,4},{6,7},{7,6},{8,9},{9,8},{10,11... | collective-permute-start | bytes 12582920 | tf_op jit(solution)/shard_map/ppermute | solution.py:34
  425.6 224.7 %reduce-scatter.8.cloned.1.call-start = ((), (), s32[]{:S(2)}) async-start(), calls=%async_computation.11 | async-start | bytes 5242880 | tf_op jit(solution)/shard_map/reduce_scatter | solution.py:1176
  502.6 10.4 %copy-start.19 = (bf16[1024,2048]{1,0:T(8,128)(2,1)S(1)}, bf16[1024,2048]{1,0:T(8,128)(2,1)}, u32[]{:S(2)}) copy-start(bf16[1024,2048]{1,0:T(8,128)(2,1)} %copy-done.17) | copy-start | bytes 12582916
  513.0 37.5 %copy-start.4 = (bf16[1024,768]{1,0:T(8,128)(2,1)}, bf16[1024,768]{1,0:T(8,128)(2,1)S(1)}, u32[]{:S(2)}) copy-start(bf16[1024,768]{1,0:T(8,128)(2,1)S(1)} %attend_backward.2.refs_8_) | copy-start | bytes 4718596
  518.1 23.9 %collective-permute-start.10 = (bf16[2048,768]{1,0:T(8,128)(2,1)}, bf16[2048,768]{1,0:T(8,128)(2,1)S(1)}, u32[]{:S(2)}, u32[]{:S(2)}) collective-permute-start(bf16[2048,768]{1,0:T(8,128)(2,1)} %convolution_convert_fusion.3), channel_id=1, source_target_pairs={{0,1},{1,0},{2,3},{3,2},{4,5},{5,4},{6,7},{7,6},{8,9},{9,8},{10,11... | collective-permute-start | bytes 9437192 | tf_op jit(solution)/shard_map/ppermute | solution.py:34
  520.5 20.1 %collective-permute-start.11 = (bf16[2048,256]{1,0:T(8,128)(2,1)}, bf16[2048,256]{1,0:T(8,128)(2,1)S(1)}, u32[]{:S(2)}, u32[]{:S(2)}) collective-permute-start(bf16[2048,256]{1,0:T(8,128)(2,1)} %convolution_convert_fusion.5), channel_id=1, source_target_pairs={{0,1},{1,0},{2,3},{3,2},{4,5},{5,4},{6,7},{7,6},{8,9},{9,8},{10,11... | collective-permute-start | bytes 3145736 | tf_op jit(solution)/shard_map/ppermute | solution.py:34
  534.1 16.1 %copy-start.5 = (bf16[1024,768]{1,0:T(8,128)(2,1)}, bf16[1024,768]{1,0:T(8,128)(2,1)S(1)}, u32[]{:S(2)}) copy-start(bf16[1024,768]{1,0:T(8,128)(2,1)S(1)} %attend_backward.3.refs_7_) | copy-start | bytes 4718596
  650.4 53.1 %copy-start.20 = (f32[192,128]{1,0:T(8,128)S(1)}, f32[192,128]{1,0:T(8,128)}, u32[]{:S(2)}) copy-start(f32[192,128]{1,0:T(8,128)} %get-tuple-element.147) | copy-start | bytes 294916
  703.5 18.2 %copy-start.23 = (f32[1,4096]{1,0:T(1,128)}, f32[1,4096]{1,0:T(1,128)S(1)}, u32[]{:S(2)}) copy-start(f32[1,4096]{1,0:T(1,128)S(1)} %constant_dynamic-slice_fusion.1) | copy-start | bytes 49156
  703.6 18.8 %copy-start.24 = (f32[2,2048]{1,0:T(2,128)}, f32[2,2048]{1,0:T(2,128)S(1)}, u32[]{:S(2)}) copy-start(f32[2,2048]{1,0:T(2,128)S(1)} %slice.214) | copy-start | bytes 49156
  703.6 19.4 %copy-start.25 = (f32[2,2048]{1,0:T(2,128)}, f32[2,2048]{1,0:T(2,128)S(1)}, u32[]{:S(2)}) copy-start(f32[2,2048]{1,0:T(2,128)S(1)} %slice.216) | copy-start | bytes 49156
  703.6 20.0 %copy-start.26 = (f32[2,2048]{1,0:T(2,128)}, f32[2,2048]{1,0:T(2,128)S(1)}, u32[]{:S(2)}) copy-start(f32[2,2048]{1,0:T(2,128)S(1)} %slice.218) | copy-start | bytes 49156
  715.4 7.7 %copy-start.28 = (f32[2,2048]{1,0:T(2,128)S(1)}, f32[2,2048]{1,0:T(2,128)}, u32[]{:S(2)}) copy-start(f32[2,2048]{1,0:T(2,128)} %param.31) | copy-start | bytes 49156
  715.4 7.6 %copy-start.36 = (f32[2,2048]{1,0:T(2,128)S(1)}, f32[2,2048]{1,0:T(2,128)}, u32[]{:S(2)}) copy-start(f32[2,2048]{1,0:T(2,128)} %param.40) | copy-start | bytes 49156
  715.4 8.3 %copy-start.30 = (f32[2,2048]{1,0:T(2,128)S(1)}, f32[2,2048]{1,0:T(2,128)}, u32[]{:S(2)}) copy-start(f32[2,2048]{1,0:T(2,128)} %param.32) | copy-start | bytes 49156
  715.4 8.3 %copy-start.37 = (f32[2,2048]{1,0:T(2,128)S(1)}, f32[2,2048]{1,0:T(2,128)}, u32[]{:S(2)}) copy-start(f32[2,2048]{1,0:T(2,128)} %param.41) | copy-start | bytes 49156
  715.4 8.9 %copy-start.33 = (f32[2,1024]{1,0:T(2,128)S(1)}, f32[2,1024]{1,0:T(2,128)}, u32[]{:S(2)}) copy-start(f32[2,1024]{1,0:T(2,128)} %param.28) | copy-start | bytes 24580
  715.4 8.9 %copy-start.38 = (f32[2,1024]{1,0:T(2,128)S(1)}, f32[2,1024]{1,0:T(2,128)}, u32[]{:S(2)}) copy-start(f32[2,1024]{1,0:T(2,128)} %param.37) | copy-start | bytes 24580
  715.4 12.8 %copy-start.14 = (f32[2,256,2048]{2,1,0:T(8,128)S(1)}, f32[2,256,2048]{2,1,0:T(8,128)}, u32[]{:S(2)}) copy-start(f32[2,256,2048]{2,1,0:T(8,128)} %get-tuple-element.143) | copy-start | bytes 12582916
  (23 other events, 111.8 us)
Sparse Core Ops, SparseCore 0:
  25.2 80.3 all-gather.3
  107.7 79.2 all-gather.5
  189.2 79.2 all-gather.7
  382.1 74.4 reduce-scatter.5
  458.9 77.2 reduce-scatter.3
  545.6 102.3 reduce-scatter.7
